TPU v7x, 32 devices: a whole 2x2x4 slice. The times are simulated.
32 devices in a mesh: groups: 2 (over y), row: 4 (over x, core), col: 4 (over z).
Axes of the slice: x: 2, y: 2, z: 4, core: 2. Of those that a mesh axis runs over, the one named last changes fastest.
Arguments:
- features: bfloat16 [8, 4, 256, 256], P(('groups', 'col'), 'row'), parts along dimension 0, may hold values from -6 to 6
- weight: bfloat16 [256, 256], replicated, may hold values from -0.375 to 0.375
- bias: float32 [256], replicated, may hold values from -3 to 3
- tile_rows: int32 [8, 4, 128], P(('groups', 'row'), 'col'), parts along dimension 0, may hold values from 0 to 7
- tile_cols: int32 [8, 4, 128], P(('groups', 'row'), 'col'), parts along dimension 0, may hold values from 0 to 7
- tile_vals: bfloat16 [8, 4, 128, 128, 128], P(('groups', 'row'), 'col'), parts along dimension 0, may hold values from -0.0625 to 0.0625
- tile_count: int32 [8, 4], P(('groups', 'row'), 'col'), parts along dimension 0, may hold values from 32 to 128, as said below
- cotangent: bfloat16 [8, 4, 256, 256], P(('groups', 'row'), 'col'), parts along dimension 0, may hold values from -6 to 6
Outputs:
- hidden: bfloat16 [8, 4, 256, 256], P(('groups', 'row'), 'col'), parts along dimension 0
- grad_features: bfloat16 [8, 4, 256, 256], P(('groups', 'col'), 'row'), parts along dimension 0
- grad_weight: float32 [512, 256], P('groups'), parts along dimension 0
- grad_bias: float32 [512], P('groups'), parts along dimension 0
There are 2 independent parts, one for each index of `groups`. A program takes and returns all parts, laid end to end along the dimension named above; an argument that names none is the same for every part. Nothing has to cross between parts.
Inputs may be any that keep to these rules, and one draw needn't show every extreme that they name: `tile_count`: some grid block has all 128 slots live.
All inputs are finite; a program needn't handle non-finite values.
Results may differ from a plain program's by a relative error of at most 0.024.
Values may be sent and summed in bfloat16 or wider, within the bound.
No kernel may reach another device: no remote copies, remote signals or barrier semaphores. Data moves between devices by JAX's collectives and lax.ppermute only.
A program may use at most 64 MiB of HBM per device.

v0:
```python
import jax
import jax.numpy as jnp
from jax import lax
from jax.sharding import PartitionSpec as P


def tile_terms(values, picked, forward):
    if forward:
        return jnp.einsum("tij,tjf->tif", values, picked, preferred_element_type=jnp.float32)
    return jnp.einsum("tji,tjf->tif", values, picked, preferred_element_type=jnp.float32)


def slot_rounds(values, source_idx, target_idx, live_count, source, forward, rounds):
    width = min(16, values.shape[0])
    targets = source.shape[0]

    def advance(index, carry):
        start = index * width
        block_values = lax.dynamic_slice_in_dim(values, start, width, 0)
        block_source = lax.dynamic_slice_in_dim(source_idx, start, width, 0)
        block_target = lax.dynamic_slice_in_dim(target_idx, start, width, 0)
        picked = jnp.take(source, block_source, axis=0)
        terms = tile_terms(block_values, picked, forward)
        alive_mask = (start + jnp.arange(width) < live_count).astype(jnp.float32)
        placing = (jnp.arange(targets)[:, None] == block_target[None, :]).astype(jnp.float32)
        placing = placing * alive_mask[None, :]
        added = jnp.einsum("rt,tif->rif", placing, terms, precision=lax.Precision.HIGHEST)
        return carry + added

    initial = jnp.zeros(source.shape, jnp.float32)
    return lax.fori_loop(0, rounds, advance, initial)


def every_slot(values, source_idx, target_idx, live_count, source, forward):
    width = min(16, values.shape[0])
    return slot_rounds(
        values, source_idx, target_idx, live_count, source, forward, values.shape[0] // width
    )


def per_device(features, weight, bias, tile_rows, tile_cols, tile_vals, tile_count, cotangent):
    own_rows = features[0, 0]
    rows_dev, feat = own_rows.shape
    tile = tile_vals.shape[-1]
    values = tile_vals[0, 0]
    row_idx = tile_rows[0, 0]
    col_idx = tile_cols[0, 0]
    live_count = tile_count[0, 0]
    gathered = lax.all_gather(own_rows, "row", axis=0, tiled=True)
    block_nodes = gathered.shape[0]
    source = gathered.reshape(block_nodes // tile, tile, feat)
    forward_terms = every_slot(values, col_idx, row_idx, live_count, source, True)
    summed = lax.psum_scatter(
        forward_terms.reshape(block_nodes, feat).astype(jnp.bfloat16),
        "col",
        scatter_dimension=0,
        tiled=True,
    )
    pre = jnp.dot(summed, weight, preferred_element_type=jnp.float32) + bias
    hidden = jax.nn.silu(pre).astype(jnp.bfloat16)
    sigma = jax.nn.sigmoid(pre)
    slope = sigma * (1.0 + pre * (1.0 - sigma))
    grad_pre = (cotangent[0, 0].astype(jnp.float32) * slope).astype(jnp.bfloat16)
    weight_term = lax.dot_general(
        summed, grad_pre, (((0,), (0,)), ((), ())), preferred_element_type=jnp.float32
    )
    bias_term = jnp.sum(grad_pre.astype(jnp.float32), axis=0)
    weight_sum, bias_sum = lax.psum((weight_term, bias_term), ("row", "col"))
    node_total = rows_dev * lax.axis_size("row") * lax.axis_size("col")
    factor = float(node_total) ** (-0.5)
    grad_local = jnp.dot(grad_pre, weight.T, preferred_element_type=jnp.float32).astype(
        jnp.bfloat16
    )
    grad_rows = lax.all_gather(grad_local, "col", axis=0, tiled=True)
    grad_source = grad_rows.reshape(block_nodes // tile, tile, feat)
    backward_terms = every_slot(values, row_idx, col_idx, live_count, grad_source, False)
    back_summed = lax.psum_scatter(
        backward_terms.reshape(block_nodes, feat).astype(jnp.bfloat16),
        "row",
        scatter_dimension=0,
        tiled=True,
    )
    hidden_out = hidden.reshape(1, 1, rows_dev, feat)
    grad_features = back_summed.reshape(1, 1, rows_dev, feat)
    return (hidden_out, grad_features, weight_sum * factor, bias_sum * factor)


def solution(mesh):
    placed = (
        P(("groups", "col"), "row", None, None),
        P(),
        P(),
        P(("groups", "row"), "col", None),
        P(("groups", "row"), "col", None),
        P(("groups", "row"), "col", None, None, None),
        P(("groups", "row"), "col"),
        P(("groups", "row"), "col", None, None),
    )
    return jax.shard_map(
        per_device,
        mesh=mesh,
        in_specs=placed,
        out_specs=(
            P(("groups", "row"), "col", None, None),
            P(("groups", "col"), "row", None, None),
            P("groups", None),
            P("groups"),
        ),
        check_vma=False,
    )
```

profile of v0, /device:TPU:0, one launch (start us, length us, event | category | flops | bytes accessed | tf_op | source)
XLA Modules:
  0.0 241.6 jit_solution(13515170279464524184)
XLA Ops:
  7.2 10.2 %all-gather = bf16[1,1,1024,256]{3,2,1,0:T(8,128)(2,1)} all-gather(bf16[1,1,256,256]{3,2,1,0:T(8,128)(2,1)} %param.14), channel_id=2, replica_groups=mesh['groups'=2,'row'=4,'col'=4] {'row'}, dimensions={2}, use_global_device_ids=true | all-gather | bytes 655360 | tf_op jit(solution)/shard_map/all_gather | solution.py:49
  17.4 72.1 %while.28 = (s32[]{:T(128)}, f32[8,128,256]{2,0,1:T(8,128)}, s32[128]{0:T(128)}, s32[]{:T(128)}, bf16[128,128,128]{2,1,0:T(8,128)(2,1)}, /*index=5*/s32[128]{0:T...) while((s32[]{:T(128)}, f32[8,128,256]{2,0,1:T(8,128)}, ...), condition=%wide.region_1.3_spmd.clone, body=%wide.region_0.2_spmd.clone.sunk | while | flops 185599376 | bytes 9968437 | solution.py:31
  22.1 3.2 %fusion.63 = f32[8,128,256]{2,0,1:T(8,128)} fusion(f32[16,128,256]{2,1,0:T(8,128)S(1)} %fusion.62, f32[8,128,256]{2,0,1:T(8,128)} %get-tuple-element.450, pred[]{:T(512)S(6)} %compare.6, f32[16]{0:T(128)S(1)} %get-tuple-element.427, s32[16]{0:T(128)S(1)} %dynamic_slice.61), kind=kOutput, calls=%fused_computation.4.clone.1 | convolution fusion | flops 50856192 | bytes 4194433 | tf_op jit(solution)/shard_map/while/body/eval_jaxpr/rt,tif->rif/dot_general | solution.py:27
  30.1 4.5 %fusion.63 = f32[8,128,256]{2,0,1:T(8,128)} fusion(f32[16,128,256]{2,1,0:T(8,128)S(1)} %fusion.62, f32[8,128,256]{2,0,1:T(8,128)} %get-tuple-element.450, pred[]{:T(512)S(6)} %compare.6, f32[16]{0:T(128)S(1)} %get-tuple-element.427, s32[16]{0:T(128)S(1)} %dynamic_slice.61), kind=kOutput, calls=%fused_computation.4.clone.1 | convolution fusion | flops 50856192 | bytes 4194433 | tf_op jit(solution)/shard_map/while/body/eval_jaxpr/rt,tif->rif/dot_general | solution.py:27
  39.2 4.5 %fusion.63 = f32[8,128,256]{2,0,1:T(8,128)} fusion(f32[16,128,256]{2,1,0:T(8,128)S(1)} %fusion.62, f32[8,128,256]{2,0,1:T(8,128)} %get-tuple-element.450, pred[]{:T(512)S(6)} %compare.6, f32[16]{0:T(128)S(1)} %get-tuple-element.427, s32[16]{0:T(128)S(1)} %dynamic_slice.61), kind=kOutput, calls=%fused_computation.4.clone.1 | convolution fusion | flops 50856192 | bytes 4194433 | tf_op jit(solution)/shard_map/while/body/eval_jaxpr/rt,tif->rif/dot_general | solution.py:27
  48.4 4.5 %fusion.63 = f32[8,128,256]{2,0,1:T(8,128)} fusion(f32[16,128,256]{2,1,0:T(8,128)S(1)} %fusion.62, f32[8,128,256]{2,0,1:T(8,128)} %get-tuple-element.450, pred[]{:T(512)S(6)} %compare.6, f32[16]{0:T(128)S(1)} %get-tuple-element.427, s32[16]{0:T(128)S(1)} %dynamic_slice.61), kind=kOutput, calls=%fused_computation.4.clone.1 | convolution fusion | flops 50856192 | bytes 4194433 | tf_op jit(solution)/shard_map/while/body/eval_jaxpr/rt,tif->rif/dot_general | solution.py:27
  57.6 4.5 %fusion.63 = f32[8,128,256]{2,0,1:T(8,128)} fusion(f32[16,128,256]{2,1,0:T(8,128)S(1)} %fusion.62, f32[8,128,256]{2,0,1:T(8,128)} %get-tuple-element.450, pred[]{:T(512)S(6)} %compare.6, f32[16]{0:T(128)S(1)} %get-tuple-element.427, s32[16]{0:T(128)S(1)} %dynamic_slice.61), kind=kOutput, calls=%fused_computation.4.clone.1 | convolution fusion | flops 50856192 | bytes 4194433 | tf_op jit(solution)/shard_map/while/body/eval_jaxpr/rt,tif->rif/dot_general | solution.py:27
  66.7 4.5 %fusion.63 = f32[8,128,256]{2,0,1:T(8,128)} fusion(f32[16,128,256]{2,1,0:T(8,128)S(1)} %fusion.62, f32[8,128,256]{2,0,1:T(8,128)} %get-tuple-element.450, pred[]{:T(512)S(6)} %compare.6, f32[16]{0:T(128)S(1)} %get-tuple-element.427, s32[16]{0:T(128)S(1)} %dynamic_slice.61), kind=kOutput, calls=%fused_computation.4.clone.1 | convolution fusion | flops 50856192 | bytes 4194433 | tf_op jit(solution)/shard_map/while/body/eval_jaxpr/rt,tif->rif/dot_general | solution.py:27
  75.9 4.5 %fusion.63 = f32[8,128,256]{2,0,1:T(8,128)} fusion(f32[16,128,256]{2,1,0:T(8,128)S(1)} %fusion.62, f32[8,128,256]{2,0,1:T(8,128)} %get-tuple-element.450, pred[]{:T(512)S(6)} %compare.6, f32[16]{0:T(128)S(1)} %get-tuple-element.427, s32[16]{0:T(128)S(1)} %dynamic_slice.61), kind=kOutput, calls=%fused_computation.4.clone.1 | convolution fusion | flops 50856192 | bytes 4194433 | tf_op jit(solution)/shard_map/while/body/eval_jaxpr/rt,tif->rif/dot_general | solution.py:27
  85.0 4.5 %fusion.63 = f32[8,128,256]{2,0,1:T(8,128)} fusion(f32[16,128,256]{2,1,0:T(8,128)S(1)} %fusion.62, f32[8,128,256]{2,0,1:T(8,128)} %get-tuple-element.450, pred[]{:T(512)S(6)} %compare.6, f32[16]{0:T(128)S(1)} %get-tuple-element.427, s32[16]{0:T(128)S(1)} %dynamic_slice.61), kind=kOutput, calls=%fused_computation.4.clone.1 | convolution fusion | flops 50856192 | bytes 4194433 | tf_op jit(solution)/shard_map/while/body/eval_jaxpr/rt,tif->rif/dot_general | solution.py:27
  89.5 2.4 copy.26
  91.9 22.1 %reduce-scatter.3.cloned.1.call-done = bf16[256,256]{1,0:T(8,128)(2,1)} async-done(((bf16[1024,256]{1,0:T(8,128)(2,1)}), bf16[256,256]{1,0:T(8,128)(2,1)}) %reduce-scatter.3.cloned.1.call-update) | async-done | bytes 131088 | tf_op jit(solution)/shard_map/reduce_scatter | solution.py:53
  114.1 1.9 convert_reduce_fusion
  117.2 16.9 %all_gather.7 = bf16[1024,256]{1,0:T(8,128)(2,1)} all-gather(bf16[256,256]{1,0:T(8,128)(2,1)S(1)} %convolution_convert_fusion), channel_id=1, replica_groups=mesh['groups'=2,'row'=4,'col'=4] {'col'}, dimensions={0}, use_global_device_ids=true | all-gather | bytes 655360 | tf_op jit(solution)/shard_map/all_gather | solution.py:74
  134.2 66.7 %while.29 = (s32[]{:T(128)}, f32[8,128,256]{2,0,1:T(8,128)}, s32[128]{0:T(128)S(1)}, s32[]{:T(128)}, bf16[128,128,128]{2,1,0:T(8,128)(2,1)}, /*index=5*/s32[128]...) while((s32[]{:T(128)}, f32[8,128,256]{2,0,1:T(8,128)}, ...), condition=%wide.region_4.6_spmd.clone, body=%wide.region_3.5_spmd.clone.sunk | while | flops 185599376 | bytes 9966361 | solution.py:31
  138.2 3.2 %fusion.69 = f32[8,128,256]{2,0,1:T(8,128)} fusion(f32[16,128,256]{2,1,0:T(8,128)S(1)} %fusion.68, f32[8,128,256]{2,0,1:T(8,128)} %get-tuple-element.483, pred[]{:T(512)S(6)} %compare.7, f32[16]{0:T(128)S(1)} %get-tuple-element.437, s32[16]{0:T(128)S(1)} %dynamic_slice.63), kind=kOutput, calls=%fused_computation.25.clone.1 | convolution fusion | flops 50856192 | bytes 4194433 | tf_op jit(solution)/shard_map/while/body/eval_jaxpr/rt,tif->rif/dot_general | solution.py:27
  145.5 4.5 %fusion.69 = f32[8,128,256]{2,0,1:T(8,128)} fusion(f32[16,128,256]{2,1,0:T(8,128)S(1)} %fusion.68, f32[8,128,256]{2,0,1:T(8,128)} %get-tuple-element.483, pred[]{:T(512)S(6)} %compare.7, f32[16]{0:T(128)S(1)} %get-tuple-element.437, s32[16]{0:T(128)S(1)} %dynamic_slice.63), kind=kOutput, calls=%fused_computation.25.clone.1 | convolution fusion | flops 50856192 | bytes 4194433 | tf_op jit(solution)/shard_map/while/body/eval_jaxpr/rt,tif->rif/dot_general | solution.py:27
  153.9 4.5 %fusion.69 = f32[8,128,256]{2,0,1:T(8,128)} fusion(f32[16,128,256]{2,1,0:T(8,128)S(1)} %fusion.68, f32[8,128,256]{2,0,1:T(8,128)} %get-tuple-element.483, pred[]{:T(512)S(6)} %compare.7, f32[16]{0:T(128)S(1)} %get-tuple-element.437, s32[16]{0:T(128)S(1)} %dynamic_slice.63), kind=kOutput, calls=%fused_computation.25.clone.1 | convolution fusion | flops 50856192 | bytes 4194433 | tf_op jit(solution)/shard_map/while/body/eval_jaxpr/rt,tif->rif/dot_general | solution.py:27
  162.4 4.5 %fusion.69 = f32[8,128,256]{2,0,1:T(8,128)} fusion(f32[16,128,256]{2,1,0:T(8,128)S(1)} %fusion.68, f32[8,128,256]{2,0,1:T(8,128)} %get-tuple-element.483, pred[]{:T(512)S(6)} %compare.7, f32[16]{0:T(128)S(1)} %get-tuple-element.437, s32[16]{0:T(128)S(1)} %dynamic_slice.63), kind=kOutput, calls=%fused_computation.25.clone.1 | convolution fusion | flops 50856192 | bytes 4194433 | tf_op jit(solution)/shard_map/while/body/eval_jaxpr/rt,tif->rif/dot_general | solution.py:27
  170.9 4.5 %fusion.69 = f32[8,128,256]{2,0,1:T(8,128)} fusion(f32[16,128,256]{2,1,0:T(8,128)S(1)} %fusion.68, f32[8,128,256]{2,0,1:T(8,128)} %get-tuple-element.483, pred[]{:T(512)S(6)} %compare.7, f32[16]{0:T(128)S(1)} %get-tuple-element.437, s32[16]{0:T(128)S(1)} %dynamic_slice.63), kind=kOutput, calls=%fused_computation.25.clone.1 | convolution fusion | flops 50856192 | bytes 4194433 | tf_op jit(solution)/shard_map/while/body/eval_jaxpr/rt,tif->rif/dot_general | solution.py:27
  179.4 4.5 %fusion.69 = f32[8,128,256]{2,0,1:T(8,128)} fusion(f32[16,128,256]{2,1,0:T(8,128)S(1)} %fusion.68, f32[8,128,256]{2,0,1:T(8,128)} %get-tuple-element.483, pred[]{:T(512)S(6)} %compare.7, f32[16]{0:T(128)S(1)} %get-tuple-element.437, s32[16]{0:T(128)S(1)} %dynamic_slice.63), kind=kOutput, calls=%fused_computation.25.clone.1 | convolution fusion | flops 50856192 | bytes 4194433 | tf_op jit(solution)/shard_map/while/body/eval_jaxpr/rt,tif->rif/dot_general | solution.py:27
  187.9 4.5 %fusion.69 = f32[8,128,256]{2,0,1:T(8,128)} fusion(f32[16,128,256]{2,1,0:T(8,128)S(1)} %fusion.68, f32[8,128,256]{2,0,1:T(8,128)} %get-tuple-element.483, pred[]{:T(512)S(6)} %compare.7, f32[16]{0:T(128)S(1)} %get-tuple-element.437, s32[16]{0:T(128)S(1)} %dynamic_slice.63), kind=kOutput, calls=%fused_computation.25.clone.1 | convolution fusion | flops 50856192 | bytes 4194433 | tf_op jit(solution)/shard_map/while/body/eval_jaxpr/rt,tif->rif/dot_general | solution.py:27
  196.4 4.5 %fusion.69 = f32[8,128,256]{2,0,1:T(8,128)} fusion(f32[16,128,256]{2,1,0:T(8,128)S(1)} %fusion.68, f32[8,128,256]{2,0,1:T(8,128)} %get-tuple-element.483, pred[]{:T(512)S(6)} %compare.7, f32[16]{0:T(128)S(1)} %get-tuple-element.437, s32[16]{0:T(128)S(1)} %dynamic_slice.63), kind=kOutput, calls=%fused_computation.25.clone.1 | convolution fusion | flops 50856192 | bytes 4194433 | tf_op jit(solution)/shard_map/while/body/eval_jaxpr/rt,tif->rif/dot_general | solution.py:27
  203.0 29.9 %psum.15 = f32[256]{0:T(256)S(1)} all-reduce(f32[256]{0:T(256)S(1)} %get-tuple-element.335), channel_id=1, replica_groups=mesh['groups'=2,'row'=4,'col'=4] {'row','col'}, use_global_device_ids=true, to_apply=%region_8.10 | all-reduce | flops 256 | bytes 2048 | tf_op jit(solution)/shard_map/psum | solution.py:68
  (124 shorter events, 75.3 us)
Async XLA Ops:
  7.2 106.9 %copy-start = (bf16[256,256]{1,0:T(8,128)(2,1)S(1)}, bf16[256,256]{1,0:T(8,128)(2,1)}, u32[]{:S(2)}) copy-start(bf16[256,256]{1,0:T(8,128)(2,1)} %param.15) | copy-start | bytes 393220
  7.2 106.9 %reduce-scatter.3.cloned.1.call-start = ((), (), s32[]{:S(2)}) async-start(), calls=%async_computation.2 | async-start | bytes 655360 | tf_op jit(solution)/shard_map/reduce_scatter | solution.py:53
  20.5 1.6 copy-start.2
  28.4 1.6 copy-start.2
  37.6 1.6 copy-start.2
  46.7 1.6 copy-start.2
  55.9 1.6 copy-start.2
  65.1 1.6 copy-start.2
  74.2 1.6 copy-start.2
  83.4 1.6 copy-start.2
  89.5 24.6 %copy-start.5 = (bf16[1,1,256,256]{3,2,1,0:T(8,128)(2,1)S(1)}, bf16[1,1,256,256]{3,2,1,0:T(8,128)(2,1)}, u32[]{:S(2)}) copy-start(bf16[1,1,256,256]{3,2,1,0:T(8,128)(2,1)} %param.21) | copy-start | bytes 393220
  89.5 24.6 %copy-start.6 = (f32[256]{0:T(256)S(1)}, f32[256]{0:T(256)}, u32[]{:S(2)}) copy-start(f32[256]{0:T(256)} %param.16) | copy-start | bytes 3076
  91.9 42.3 %copy-start.3 = (s32[128]{0:T(128)S(1)}, s32[128]{0:T(128)}, u32[]{:S(2)}) copy-start(s32[128]{0:T(128)} %get-tuple-element.516) | copy-start | bytes 1540
  91.9 42.3 %copy-start.4 = (s32[128]{0:T(128)S(1)}, s32[128]{0:T(128)}, u32[]{:S(2)}) copy-start(s32[128]{0:T(128)} %get-tuple-element.517) | copy-start | bytes 1540
  91.9 141.6 %all-reduce.2.cloned.1.call-start = ((), (), s32[]{:S(2)}) async-start(), calls=%async_computation.4 | async-start | bytes 524288 | tf_op jit(solution)/shard_map/psum | solution.py:68
  114.1 2.2 copy-start.1
  117.2 117.9 %reduce-scatter.5.cloned.1.call-start = ((), (), s32[]{:S(2)}) async-start(), calls=%async_computation.3 | async-start | bytes 655360 | tf_op jit(solution)/shard_map/reduce_scatter | solution.py:77
Sparse Core Ops, SparseCore 0:
  92.0 22.0 reduce-scatter.2
  118.0 87.3 all-reduce.1
  208.5 22.1 reduce-scatter.4
where the time goes:
time: 244 us; the launch traced here: 242 us
  matrix products  96.6 us (40%)
  blocking collectives  57 us (23%)
  local copies, waits for them, and re-layouts  31.1 us (13%)
  waiting for transfers between devices  22.2 us (9%)
  other arithmetic  20.4 us (8%)
  between operations  13.8 us (6%)
    dot_general x16, matrix products, advance(): jnp.einsum('rt,tif->rif', placing, terms, precision=lax.Precision.HIGHEST)  68.8 us
    psum x1, blocking collectives, per_device(): weight_sum, bias_sum = lax.psum((weight_term, bias_term), ('row', 'col'))  29.9 us
    gather x16, local copies, waits for them, and re-layouts, advance(): picked = jnp.take(source, block_source, axis=0)  26.5 us
    reduce_scatter x1, waiting for transfers between devices, per_device(): lax.psum_scatter(forward_terms.reshape(block_nodes, feat).astype(jnp.bflo...  22.1 us
    all_gather x1, blocking collectives, per_device(): grad_rows = lax.all_gather(grad_local, 'col', axis=0, tiled=True)  16.9 us
    and x16, other arithmetic, advance(): picked = jnp.take(source, block_source, axis=0)  16.8 us
    dot_general x8, matrix products, tile_terms(): jnp.einsum('tij,tjf->tif', values, picked, preferred_element_type=jnp.flo...  12.4 us
    dot_general x8, matrix products, tile_terms(): jnp.einsum('tji,tjf->tif', values, picked, preferred_element_type=jnp.flo...  12.4 us
  transfers between devices with their start and end apart: 3, of which 1 were waited for; matrix products, arithmetic and copies ran while one was open for 29% of the time, Pallas kernels for 0%

commit v1 on v0

--- a/solution.py
+++ b/solution.py
@@ -1,7 +1,16 @@
+import functools
+
 import jax
 import jax.numpy as jnp
 from jax import lax
+from jax.experimental import pallas as pl
+from jax.experimental.pallas import tpu as pltpu
 from jax.sharding import PartitionSpec as P
+
+BF = jnp.bfloat16
+F32 = jnp.float32
+VMEM = pl.BlockSpec(memory_space=pltpu.VMEM)
+SMEM = pl.BlockSpec(memory_space=pltpu.SMEM)
 
 
 def tile_terms(values, picked, forward):
@@ -10,7 +19,7 @@
     return jnp.einsum("tji,tjf->tif", values, picked, preferred_element_type=jnp.float32)
 
 
-def slot_rounds(values, source_idx, target_idx, live_count, source, forward, rounds):
+def every_slot(values, source_idx, target_idx, live_count, source, forward):
     width = min(16, values.shape[0])
     targets = source.shape[0]
 
@@ -28,17 +37,10 @@
         return carry + added
 
     initial = jnp.zeros(source.shape, jnp.float32)
-    return lax.fori_loop(0, rounds, advance, initial)
-
-
-def every_slot(values, source_idx, target_idx, live_count, source, forward):
-    width = min(16, values.shape[0])
-    return slot_rounds(
-        values, source_idx, target_idx, live_count, source, forward, values.shape[0] // width
-    )
-
-
-def per_device(features, weight, bias, tile_rows, tile_cols, tile_vals, tile_count, cotangent):
+    return lax.fori_loop(0, values.shape[0] // width, advance, initial)
+
+
+def sparse_device(features, weight, bias, tile_rows, tile_cols, tile_vals, tile_count, cotangent):
     own_rows = features[0, 0]
     rows_dev, feat = own_rows.shape
     tile = tile_vals.shape[-1]
@@ -51,38 +53,229 @@
     source = gathered.reshape(block_nodes // tile, tile, feat)
     forward_terms = every_slot(values, col_idx, row_idx, live_count, source, True)
     summed = lax.psum_scatter(
-        forward_terms.reshape(block_nodes, feat).astype(jnp.bfloat16),
-        "col",
-        scatter_dimension=0,
-        tiled=True,
-    )
-    pre = jnp.dot(summed, weight, preferred_element_type=jnp.float32) + bias
-    hidden = jax.nn.silu(pre).astype(jnp.bfloat16)
+        forward_terms.reshape(block_nodes, feat).astype(BF), "col", scatter_dimension=0, tiled=True
+    )
+    pre = jnp.dot(summed, weight, preferred_element_type=F32) + bias
+    hidden = jax.nn.silu(pre).astype(BF)
     sigma = jax.nn.sigmoid(pre)
     slope = sigma * (1.0 + pre * (1.0 - sigma))
-    grad_pre = (cotangent[0, 0].astype(jnp.float32) * slope).astype(jnp.bfloat16)
+    grad_pre = (cotangent[0, 0].astype(F32) * slope).astype(BF)
     weight_term = lax.dot_general(
-        summed, grad_pre, (((0,), (0,)), ((), ())), preferred_element_type=jnp.float32
-    )
-    bias_term = jnp.sum(grad_pre.astype(jnp.float32), axis=0)
+        summed, grad_pre, (((0,), (0,)), ((), ())), preferred_element_type=F32
+    )
+    bias_term = jnp.sum(grad_pre.astype(F32), axis=0)
     weight_sum, bias_sum = lax.psum((weight_term, bias_term), ("row", "col"))
     node_total = rows_dev * lax.axis_size("row") * lax.axis_size("col")
     factor = float(node_total) ** (-0.5)
-    grad_local = jnp.dot(grad_pre, weight.T, preferred_element_type=jnp.float32).astype(
-        jnp.bfloat16
-    )
+    grad_local = jnp.dot(grad_pre, weight.T, preferred_element_type=F32).astype(BF)
     grad_rows = lax.all_gather(grad_local, "col", axis=0, tiled=True)
     grad_source = grad_rows.reshape(block_nodes // tile, tile, feat)
     backward_terms = every_slot(values, row_idx, col_idx, live_count, grad_source, False)
     back_summed = lax.psum_scatter(
-        backward_terms.reshape(block_nodes, feat).astype(jnp.bfloat16),
-        "row",
-        scatter_dimension=0,
-        tiled=True,
+        backward_terms.reshape(block_nodes, feat).astype(BF), "row", scatter_dimension=0, tiled=True
     )
     hidden_out = hidden.reshape(1, 1, rows_dev, feat)
     grad_features = back_summed.reshape(1, 1, rows_dev, feat)
     return (hidden_out, grad_features, weight_sum * factor, bias_sum * factor)
+
+
+def swap(x, axis, bit):
+    size = lax.axis_size(axis)
+    return lax.ppermute(x, axis, [(i, i ^ bit) for i in range(size)])
+
+
+def build_kernel(rows_ref, cols_ref, count_ref, vals_ref, dense_ref, total):
+    step = pl.program_id(0)
+    width, tile, _ = vals_ref.shape
+    wide, nodes, _ = total.shape
+    per = dense_ref.shape[2] // tile
+
+    @pl.when(step == 0)
+    def _():
+        total[...] = jnp.zeros_like(total)
+
+    def place(slot, carry):
+        row = rows_ref[step * width + slot]
+        col = cols_ref[step * width + slot]
+        where = pl.ds(pl.multiple_of(row * tile, tile), tile)
+        total[col, where, :] += vals_ref[slot].astype(F32)
+        return carry
+
+    lax.fori_loop(0, jnp.clip(count_ref[0] - step * width, 0, width), place, 0)
+
+    @pl.when(step == pl.num_programs(0) - 1)
+    def _():
+        for col in range(wide):
+            dense_ref[col // per, :, (col % per) * tile : (col % per + 1) * tile] = total[col].astype(BF)
+
+
+def build_dense(values, row_idx, col_idx, count, parts, rows_dev):
+    slots, tile, _ = values.shape
+    nodes = parts * rows_dev
+    width = 16
+
+    def live_block(step, rows, cols, live):
+        return (jnp.minimum(step, jnp.maximum(live[0] - 1, 0) // width), 0, 0)
+
+    return pl.pallas_call(
+        build_kernel,
+        grid_spec=pltpu.PrefetchScalarGridSpec(
+            num_scalar_prefetch=3,
+            grid=(slots // width,),
+            in_specs=[pl.BlockSpec((width, tile, tile), live_block)],
+            out_specs=pl.BlockSpec((parts, nodes, rows_dev), lambda *_: (0, 0, 0)),
+            scratch_shapes=[pltpu.VMEM((nodes // tile, nodes, tile), F32)],
+        ),
+        out_shape=jax.ShapeDtypeStruct((parts, nodes, rows_dev), BF),
+        compiler_params=pltpu.CompilerParams(vmem_limit_bytes=32 << 20),
+        cost_estimate=pl.CostEstimate(flops=8 * nodes * nodes, bytes_accessed=6 * nodes * nodes, transcendentals=0),
+        name="build_dense",
+    )(row_idx, col_idx, count, values)
+
+
+def forward_kernel(place_ref, dense_ref, *refs):
+    parts = dense_ref.shape[0]
+    sources, outs = refs[:parts], refs[parts:]
+    rows = sources[0].shape[0]
+    row, col = place_ref[0], place_ref[1]
+    for k in range(parts):
+        where = pl.ds(pl.multiple_of((col ^ k) * rows, rows), rows)
+        total = None
+        for j in range(parts):
+            term = jnp.dot(dense_ref[row ^ j, where, :], sources[j][...], preferred_element_type=F32)
+            total = term if total is None else total + term
+        outs[k][...] = total.astype(BF)
+
+
+def backward_kernel(place_ref, dense_ref, *refs):
+    parts = dense_ref.shape[0]
+    sources, outs = refs[:parts], refs[parts:]
+    rows = sources[0].shape[0]
+    row, col = place_ref[0], place_ref[1]
+    for k in range(parts):
+        total = None
+        for j in range(parts):
+            where = pl.ds(pl.multiple_of((col ^ j) * rows, rows), rows)
+            term = lax.dot_general(
+                dense_ref[row ^ k, where, :], sources[j][...], (((0,), (0,)), ((), ())),
+                preferred_element_type=F32,
+            )
+            total = term if total is None else total + term
+        outs[k][...] = total.astype(BF)
+
+
+def product(kernel, name, place, dense, sources):
+    parts = len(sources)
+    rows, feat = sources[0].shape
+    return pl.pallas_call(
+        kernel,
+        in_specs=[SMEM] + [VMEM] * (1 + parts),
+        out_specs=[VMEM] * parts,
+        out_shape=[jax.ShapeDtypeStruct((rows, feat), BF)] * parts,
+        compiler_params=pltpu.CompilerParams(vmem_limit_bytes=32 << 20),
+        cost_estimate=pl.CostEstimate(
+            flops=2 * parts * parts * rows * rows * feat,
+            bytes_accessed=2 * parts * rows * (parts * rows + 2 * feat),
+            transcendentals=0,
+        ),
+        name=name,
+    )(place, dense, *sources)
+
+
+def layer_kernel(weight_ref, bias_ref, cot_ref, *refs):
+    terms, (hidden_ref, agg_ref, wgrad_ref, bgrad_ref) = refs[:-4], refs[-4:]
+    summed = terms[0][...].astype(F32)
+    for term in terms[1:]:
+        summed = summed + term[...].astype(F32)
+    summed = summed.astype(BF)
+    pre = jnp.dot(summed, weight_ref[...], preferred_element_type=F32) + bias_ref[...]
+    sigma = jax.nn.sigmoid(pre)
+    hidden_ref[...] = (pre * sigma).astype(BF)
+    slope = sigma * (1.0 + pre * (1.0 - sigma))
+    grad_pre = (cot_ref[...].astype(F32) * slope).astype(BF)
+    agg_ref[...] = lax.dot_general(
+        grad_pre, weight_ref[...], (((1,), (1,)), ((), ())), preferred_element_type=F32
+    ).astype(BF)
+    wgrad_ref[...] = lax.dot_general(
+        summed, grad_pre, (((0,), (0,)), ((), ())), preferred_element_type=F32
+    )
+    bgrad_ref[...] = jnp.sum(grad_pre.astype(F32), axis=0, keepdims=True)
+
+
+def layer(weight, bias, cot, terms):
+    rows, feat = cot.shape
+    return pl.pallas_call(
+        layer_kernel,
+        in_specs=[VMEM] * (3 + len(terms)),
+        out_specs=[VMEM] * 4,
+        out_shape=[
+            jax.ShapeDtypeStruct((rows, feat), BF),
+            jax.ShapeDtypeStruct((rows, feat), BF),
+            jax.ShapeDtypeStruct((feat, feat), F32),
+            jax.ShapeDtypeStruct((1, feat), F32),
+        ],
+        cost_estimate=pl.CostEstimate(
+            flops=6 * rows * feat * feat, bytes_accessed=20 * rows * feat, transcendentals=rows * feat
+        ),
+        name="layer",
+    )(weight, bias, cot, *terms)
+
+
+def dense_device(features, weight, bias, tile_rows, tile_cols, tile_vals, tile_count, cotangent):
+    own = features[0, 0]
+    rows, feat = own.shape
+    row, col = lax.axis_index("row"), lax.axis_index("col")
+    place = jnp.stack([row, col]).astype(jnp.int32)
+
+    from_chip = swap(own, "row", 2)
+    from_core = swap(own, "row", 1)
+    dense = build_dense(tile_vals[0, 0], tile_rows[0, 0], tile_cols[0, 0], tile_count[0], 4, rows)
+    sources = [own, from_core, from_chip, swap(from_chip, "row", 1)]
+    partial = product(forward_kernel, "forward", place, dense, sources)
+
+    terms = [partial[0]] + [swap(partial[k], "col", k) for k in (2, 3, 1)]
+    hidden, agg, wgrad, bgrad = layer(weight, bias[None, :], cotangent[0, 0], terms)
+
+    grads = {0: agg}
+    for k in (2, 3, 1):
+        grads[k] = swap(agg, "col", k)
+
+    packed = jnp.concatenate([wgrad, jnp.broadcast_to(bgrad, (16, feat))], axis=0)
+    packed = packed + swap(packed, "row", 1)
+    height = packed.shape[0] // 2
+    half = lax.dynamic_slice_in_dim(packed, (row % 2) * height, height, 0)
+    half = half + swap(half, "row", 2)
+
+    back = product(backward_kernel, "backward", place, dense, [grads[k] for k in range(4)])
+
+    arrived = swap(jnp.stack([back[1], back[3]]), "row", 1)
+    keep = back[0].astype(F32) + arrived[0].astype(F32)
+    send = (back[2].astype(F32) + arrived[1].astype(F32)).astype(BF)
+    other = swap(send, "row", 2)
+
+    pieces = [swap(half, "col", k) for k in (2, 3, 1)]
+    half = half + pieces[0] + pieces[1] + pieces[2]
+    twin = swap(half, "row", 1)
+    first = row % 2 == 0
+    whole = jnp.concatenate([jnp.where(first, half, twin), jnp.where(first, twin, half)], axis=0)
+    factor = float(rows * 16) ** (-0.5)
+
+    grad_features = (keep + other.astype(F32)).astype(BF)
+    return (
+        hidden[None, None],
+        grad_features[None, None],
+        whole[:feat] * factor,
+        whole[feat] * factor,
+    )
+
+
+def per_device(features, weight, bias, tile_rows, tile_cols, tile_vals, tile_count, cotangent):
+    rows = features.shape[2]
+    slots, tile, _ = tile_vals.shape[2:]
+    square = lax.axis_size("row") == 4 and lax.axis_size("col") == 4
+    dense_fits = (4 * rows // tile) ** 2 <= slots
+    chosen = dense_device if square and dense_fits else sparse_device
+    return chosen(features, weight, bias, tile_rows, tile_cols, tile_vals, tile_count, cotangent)
 
 
 def solution(mesh):

time: 244 us -> 75.6 us (0.31)
  matrix products: 96.6 us -> 0 us
  blocking collectives: 57 us -> 0 us
  local copies, waits for them, and re-layouts: 31.1 us -> 6.37 us
  starting transfers between devices: 0.12 us -> 21.7 us
  other arithmetic: 20.4 us -> 4.14 us
  waiting for transfers between devices: 22.2 us -> 34.9 us
  between operations: 13.8 us -> 1.43 us
  Pallas kernels: 0 us -> 6.93 us
    dot_general x35 -> x0, matrix products: 96.6 us -> none  [the longest x16 68.8 us: advance(): jnp.einsum('rt,tif->rif', placing, terms, precision=lax.Precision.HIGHEST)]
    ppermute x0 -> x17, waiting for transfers between devices: none -> 34.9 us  [swap(): return lax.ppermute(x, axis, [(i, i ^ bit) for i in range(size)])]
    psum x1 -> x0, blocking collectives: 29.9 us -> none  [per_device(): weight_sum, bias_sum = lax.psum((weight_term, bias_term), ('row', 'col'))]
    all_gather x2 -> x0, blocking collectives: 27.1 us -> none  [the longest x1 16.9 us: per_device(): grad_rows = lax.all_gather(grad_local, 'col', axis=0, tiled=True)]
    gather x16 -> x0, local copies, waits for them, and re-layouts: 26.5 us -> none  [advance(): picked = jnp.take(source, block_source, axis=0)]
    reduce_scatter x2 -> x0, waiting for transfers between devices: 22.1 us -> none  [the longest x1 22.1 us: per_device(): lax.psum_scatter(forward_terms.reshape(block_nodes, feat).astype(jnp.bflo...]
    ppermute x0 -> x17, starting transfers between devices: none -> 21.7 us  [swap(): return lax.ppermute(x, axis, [(i, i ^ bit) for i in range(size)])]
    and x16 -> x0, other arithmetic: 16.8 us -> none  [advance(): picked = jnp.take(source, block_source, axis=0)]
  transfers between devices with their start and end apart: 3 -> 17, of which waited for: 1 -> 10; matrix products, arithmetic and copies ran while one was open for 29% -> 5% of each run, Pallas kernels for 0% -> 4%
where the time goes in v1:
time: 75.6 us; the launch traced here: 75.4 us
  waiting for transfers between devices  34.9 us (46%)
  starting transfers between devices  21.7 us (29%)
  Pallas kernels  6.93 us (9%)
  local copies, waits for them, and re-layouts  6.37 us (8%)
  other arithmetic  4.14 us (5%)
  between operations  1.43 us (2%)
    ppermute x17, waiting for transfers between devices, swap(): return lax.ppermute(x, axis, [(i, i ^ bit) for i in range(size)])  34.9 us
    ppermute x17, starting transfers between devices, swap(): return lax.ppermute(x, axis, [(i, i ^ bit) for i in range(size)])  21.7 us
    unnamed x18, local copies, waits for them, and re-layouts  5.69 us
    pallas_call x2, Pallas kernels, product(): pl.pallas_call(kernel, in_specs=[SMEM] + [VMEM] * (1 + parts), out_specs=...  2.56 us
    pallas_call x1, Pallas kernels, layer(): pl.pallas_call(layer_kernel, in_specs=[VMEM] * (3 + len(terms)), out_spec...  2.36 us
    pallas_call x1, Pallas kernels, build_dense(): pl.pallas_call(build_kernel, grid_spec=pltpu.PrefetchScalarGridSpec(num_s...  2.01 us
  transfers between devices with their start and end apart: 17, of which 10 were waited for; matrix products, arithmetic and copies ran while one was open for 5% of the time, Pallas kernels for 4%

profile of v1, /device:TPU:0, one launch (start us, length us, event | category | flops | bytes accessed | tf_op | source)
XLA Modules:
  0.0 75.4 jit_solution(7133156651510941534)
XLA Ops:
  0.6 3.0 %collective-permute-start.1 = (bf16[256,256]{1,0:T(8,128)(2,1)}, bf16[256,256]{1,0:T(8,128)(2,1)S(1)}, u32[]{:S(2)}, u32[]{:S(2)}) collective-permute-start(bf16[256,256]{1,0:T(8,128)(2,1)} %bitcast.28), channel_id=1, source_target_pairs={{0,8},{4,12},{8,0},{12,4},{1,9},{5,13},{9,1},{13,5},{2,10},{6,14},... | collective-permute-start | bytes 393224 | tf_op jit(solution)/shard_map/ppermute | solution.py:84
  3.6 3.7 %collective-permute-done.1.refs_2_ = bf16[256,256]{1,0:T(8,128)(2,1)S(1)} collective-permute-done((bf16[256,256]{1,0:T(8,128)(2,1)}, bf16[256,256]{1,0:T(8,128)(2,1)S(1)}, u32[]{:S(2)}, u32[]{:S(2)}) %collective-permute-start.1) | collective-permute-done | bytes 131104 | tf_op jit(solution)/shard_map/ppermute | solution.py:84
  8.0 2.2 %copy-done = bf16[1,1,128,128,128]{4,3,2,1,0:T(8,128)(2,1)S(1)} copy-done((bf16[1,1,128,128,128]{4,3,2,1,0:T(8,128)(2,1)S(1)}, bf16[1,1,128,128,128]{4,3,2,1,0:T(8,128)(2,1)}, u32[]{:S(2)}) %copy-start) | copy-done | bytes 4194328
  11.5 2.0 %build_dense.1.dense_ref = bf16[4,1024,256]{2,1,0:T(8,128)(2,1)S(1)} custom-call(s32[128]{0:T(128)S(1)} %bitcast.33, s32[128]{0:T(128)S(1)} %bitcast.34, s32[1]{0:T(128)} %bitcast.26.count_ref, bf16[128,128,128]{2,1,0:T(8,128)(2,1)S(1)} %bitcast.27), custom_call_target="tpu_custom_call" | custom-call | flops 8388608 | bytes 6291456 | tf_op jit(solution)/shard_map/build_dense/pallas_call | solution.py:120
  13.6 1.3 %forward.1 = (bf16[256,256]{1,0:T(8,128)(2,1)S(1)}, bf16[256,256]{1,0:T(8,128)(2,1)S(1)}, bf16[256,256]{1,0:T(8,128)(2,1)S(1)}, bf16[256,256]{1,0:T(8,128)(2,1)S(1)}) custom-call(s32[2]{0:T(128)S(1)} %pad_add_fusion.place_ref, bf16[4,1024,256]{2,1,0:T(8,128)(2,1)S(1)} %build_dense.1.dense_ref, bf16[256,256]{1,0:T(8,128)(2,1)S(1)} %bitcast.30, ...), custom_call_target="tpu_custom_call" | custom-call | flops 536870912 | bytes 3145728 | tf_op jit(solution)/shard_map/forward/pallas_call | solution.py:170
  15.5 3.6 %collective-permute-start.3 = (bf16[256,256]{1,0:T(8,128)(2,1)S(1)}, bf16[256,256]{1,0:T(8,128)(2,1)S(1)}, u32[]{:S(2)}, u32[]{:S(2)}) collective-permute-start(bf16[256,256]{1,0:T(8,128)(2,1)S(1)} %get-tuple-element.17), channel_id=1, source_target_pairs={{0,2},{1,3},{2,0},{3,1},{4,6},{5,7},{6,4},{7,5},{8,10},{9,11},{10,... | collective-permute-start | bytes 393224 | tf_op jit(solution)/shard_map/ppermute | solution.py:84
  20.4 8.7 %collective-permute-done.3.refs_1_ = bf16[256,256]{1,0:T(8,128)(2,1)S(1)} collective-permute-done((bf16[256,256]{1,0:T(8,128)(2,1)S(1)}, bf16[256,256]{1,0:T(8,128)(2,1)S(1)}, u32[]{:S(2)}, u32[]{:S(2)}) %collective-permute-start.3) | collective-permute-done | bytes 131104 | tf_op jit(solution)/shard_map/ppermute | solution.py:84
  30.6 2.4 %layer.1 = (bf16[256,256]{1,0:T(8,128)(2,1)}, bf16[256,256]{1,0:T(8,128)(2,1)}, f32[256,256]{1,0:T(8,128)}, f32[1,256]{1,0:T(1,128)}) custom-call(bf16[256,256]{1,0:T(8,128)(2,1)} %weight_ref.1, f32[1,256]{1,0:T(1,128)} %bitcast.36, bf16[256,256]{1,0:T(8,128)(2,1)} %bitcast.35, bf16[256,256]{1,0:T(8,128)(2,1)} %copy-done.3, bf16[256,256]{1,0:T(8,128)(2,1)} %copy-done.6, ...), custom_call_target="tpu_custom_call" | custom-call | flops 100663296 | bytes 1310720 | tf_op jit(solution)/shard_map/layer/pallas_call | solution.py:207
  33.0 2.2 %collective-permute-start.6 = (bf16[256,256]{1,0:T(8,128)(2,1)}, bf16[256,256]{1,0:T(8,128)(2,1)S(1)}, u32[]{:S(2)}, u32[]{:S(2)}) collective-permute-start(bf16[256,256]{1,0:T(8,128)(2,1)} %get-tuple-element.21.refs_0_), channel_id=1, source_target_pairs={{0,1},{1,0},{2,3},{3,2},{4,5},{5,4},{6,7},{7,6},{8,9},{9,8},{10,11... | collective-permute-start | bytes 393224 | tf_op jit(solution)/shard_map/ppermute | solution.py:84
  35.1 1.9 %collective-permute-start.7 = (bf16[256,256]{1,0:T(8,128)(2,1)}, bf16[256,256]{1,0:T(8,128)(2,1)S(1)}, u32[]{:S(2)}, u32[]{:S(2)}) collective-permute-start(bf16[256,256]{1,0:T(8,128)(2,1)} %get-tuple-element.21.refs_0_), channel_id=1, source_target_pairs={{0,2},{1,3},{2,0},{3,1},{4,6},{5,7},{6,4},{7,5},{8,10},{9,11},{10,... | collective-permute-start | bytes 393224 | tf_op jit(solution)/shard_map/ppermute | solution.py:84
  37.0 1.5 %collective-permute-start.8 = (bf16[256,256]{1,0:T(8,128)(2,1)}, bf16[256,256]{1,0:T(8,128)(2,1)S(1)}, u32[]{:S(2)}, u32[]{:S(2)}) collective-permute-start(bf16[256,256]{1,0:T(8,128)(2,1)} %get-tuple-element.21.refs_0_), channel_id=1, source_target_pairs={{0,3},{1,2},{2,1},{3,0},{4,7},{5,6},{6,5},{7,4},{8,11},{9,10},{10,... | collective-permute-start | bytes 393224 | tf_op jit(solution)/shard_map/ppermute | solution.py:84
  39.2 1.0 %pad_maximum_fusion = f32[272,256]{1,0:T(8,128)S(1)} fusion(f32[16,256]{1,0:T(8,128)S(1)} %broadcast_in_dim.20, f32[256,256]{1,0:T(8,128)} %get-tuple-element.26), kind=kLoop, calls=%fused_computation.1 | loop fusion | flops 69632 | bytes 557056 | tf_op jit(solution)/shard_map/concatenate | solution.py:243
  40.2 1.3 %collective-permute-done.6.refs_1_ = bf16[256,256]{1,0:T(8,128)(2,1)S(1)} collective-permute-done((bf16[256,256]{1,0:T(8,128)(2,1)}, bf16[256,256]{1,0:T(8,128)(2,1)S(1)}, u32[]{:S(2)}, u32[]{:S(2)}) %collective-permute-start.6) | collective-permute-done | bytes 131104 | tf_op jit(solution)/shard_map/ppermute | solution.py:84
  41.5 1.5 %collective-permute-done.7.refs_2_ = bf16[256,256]{1,0:T(8,128)(2,1)S(1)} collective-permute-done((bf16[256,256]{1,0:T(8,128)(2,1)}, bf16[256,256]{1,0:T(8,128)(2,1)S(1)}, u32[]{:S(2)}, u32[]{:S(2)}) %collective-permute-start.7) | collective-permute-done | bytes 131104 | tf_op jit(solution)/shard_map/ppermute | solution.py:84
  43.0 4.9 %collective-permute-done.8.refs_3_ = bf16[256,256]{1,0:T(8,128)(2,1)S(1)} collective-permute-done((bf16[256,256]{1,0:T(8,128)(2,1)}, bf16[256,256]{1,0:T(8,128)(2,1)S(1)}, u32[]{:S(2)}, u32[]{:S(2)}) %collective-permute-start.8) | collective-permute-done | bytes 131104 | tf_op jit(solution)/shard_map/ppermute | solution.py:84
  47.9 0.9 %copy-done.2 = bf16[256,256]{1,0:T(8,128)(2,1)S(1)} copy-done((bf16[256,256]{1,0:T(8,128)(2,1)S(1)}, bf16[256,256]{1,0:T(8,128)(2,1)}, u32[]{:S(2)}) %copy-start.2) | copy-done | bytes 131096
  48.8 1.3 %backward.1 = (bf16[256,256]{1,0:T(8,128)(2,1)S(1)}, bf16[256,256]{1,0:T(8,128)(2,1)S(1)}, bf16[256,256]{1,0:T(8,128)(2,1)S(1)}, bf16[256,256]{1,0:T(8,128)(2,1)S(1)}) custom-call(s32[2]{0:T(128)S(1)} %pad_add_fusion.place_ref, bf16[4,1024,256]{2,1,0:T(8,128)(2,1)S(1)} %build_dense.1.dense_ref, bf16[256,256]{1,0:T(8,128)(2,1)S(1)} %copy-done.2, ...), custom_call_target="tpu_custom_call" | custom-call | flops 536870912 | bytes 3145728 | tf_op jit(solution)/shard_map/backward/pallas_call | solution.py:170
  50.2 0.9 %fusion.5 = f32[136,256]{1,0:T(8,128)S(1)} fusion(s32[]{:T(128)S(6)} %select_n.26, f32[256,256]{1,0:T(8,128)} %get-tuple-element.26, f32[16,256]{1,0:T(8,128)S(1)} %broadcast_in_dim.20, f32[272,256]{1,0:T(8,128)S(1)} %collective-permute-done.11), kind=kLoop, calls=%fused_computation.12 | loop fusion | flops 69632 | bytes 557060 | tf_op jit(solution)/shard_map/add | solution.py:244
  51.2 1.5 %collective-permute-start.12 = (f32[136,256]{1,0:T(8,128)S(1)}, f32[136,256]{1,0:T(8,128)S(1)}, u32[]{:S(2)}, u32[]{:S(2)}) collective-permute-start(f32[136,256]{1,0:T(8,128)S(1)} %fusion.5), channel_id=1, source_target_pairs={{0,8},{4,12},{8,0},{12,4},{1,9},{5,13},{9,1},{13,5},{2,10},{6,14},... | collective-permute-start | bytes 417800 | tf_op jit(solution)/shard_map/ppermute | solution.py:84
  52.7 4.6 %collective-permute-done.12 = f32[136,256]{1,0:T(8,128)S(1)} collective-permute-done((f32[136,256]{1,0:T(8,128)S(1)}, f32[136,256]{1,0:T(8,128)S(1)}, u32[]{:S(2)}, u32[]{:S(2)}) %collective-permute-start.12) | collective-permute-done | bytes 139296 | tf_op jit(solution)/shard_map/ppermute | solution.py:84
  57.3 4.4 %collective-permute-start.13 = (f32[136,256]{1,0:T(8,128)S(1)}, f32[136,256]{1,0:T(8,128)S(1)}, u32[]{:S(2)}, u32[]{:S(2)}) collective-permute-start(f32[136,256]{1,0:T(8,128)S(1)} %add.38), channel_id=1, source_target_pairs={{0,2},{1,3},{2,0},{3,1},{4,6},{5,7},{6,4},{7,5},{8,10},{9,11},{10,... | collective-permute-start | bytes 417800 | tf_op jit(solution)/shard_map/ppermute | solution.py:84
  62.4 1.5 %collective-permute-start.10 = (bf16[256,256]{1,0:T(8,128)(2,1)S(1)}, bf16[256,256]{1,0:T(8,128)(2,1)S(1)}, u32[]{:S(2)}, u32[]{:S(2)}) collective-permute-start(bf16[256,256]{1,0:T(8,128)(2,1)S(1)} %fusion.1), channel_id=1, source_target_pairs={{0,8},{4,12},{8,0},{12,4},{1,9},{5,13},{9,1},{13,5},{2,10},{6,14},... | collective-permute-start | bytes 393224 | tf_op jit(solution)/shard_map/ppermute | solution.py:84
  63.9 7.8 %collective-permute-done.13 = f32[136,256]{1,0:T(8,128)S(1)} collective-permute-done((f32[136,256]{1,0:T(8,128)S(1)}, f32[136,256]{1,0:T(8,128)S(1)}, u32[]{:S(2)}, u32[]{:S(2)}) %collective-permute-start.13) | collective-permute-done | bytes 139296 | tf_op jit(solution)/shard_map/ppermute | solution.py:84
  71.7 1.0 %collective-permute-done.15 = f32[136,256]{1,0:T(8,128)S(1)} collective-permute-done((f32[136,256]{1,0:T(8,128)S(1)}, f32[136,256]{1,0:T(8,128)S(1)}, u32[]{:S(2)}, u32[]{:S(2)}) %collective-permute-start.15) | collective-permute-done | bytes 139296 | tf_op jit(solution)/shard_map/ppermute | solution.py:84
  (44 shorter events, 9.1 us)
Async XLA Ops:
  0.6 6.7 %collective-permute-start.1 = (bf16[256,256]{1,0:T(8,128)(2,1)}, bf16[256,256]{1,0:T(8,128)(2,1)S(1)}, u32[]{:S(2)}, u32[]{:S(2)}) collective-permute-start(bf16[256,256]{1,0:T(8,128)(2,1)} %bitcast.28), channel_id=1, source_target_pairs={{0,8},{4,12},{8,0},{12,4},{1,9},{5,13},{9,1},{13,5},{2,10},{6,14},... | collective-permute-start | bytes 393224 | tf_op jit(solution)/shard_map/ppermute | solution.py:84
  3.6 10.0 %collective-permute-start = (bf16[256,256]{1,0:T(8,128)(2,1)}, bf16[256,256]{1,0:T(8,128)(2,1)S(1)}, u32[]{:S(2)}, u32[]{:S(2)}) collective-permute-start(bf16[256,256]{1,0:T(8,128)(2,1)} %bitcast.29), channel_id=1, source_target_pairs={{0,4},{4,0},{8,12},{12,8},{1,5},{5,1},{9,13},{13,9},{2,6},{6,2},{1... | collective-permute-start | bytes 393224 | tf_op jit(solution)/shard_map/ppermute | solution.py:84
  7.3 6.3 %collective-permute-start.2 = (bf16[256,256]{1,0:T(8,128)(2,1)S(1)}, bf16[256,256]{1,0:T(8,128)(2,1)S(1)}, u32[]{:S(2)}, u32[]{:S(2)}) collective-permute-start(bf16[256,256]{1,0:T(8,128)(2,1)S(1)} %collective-permute-done.1.refs_2_), channel_id=1, source_target_pairs={{0,4},{4,0},{8,12},{12,8},{1,5},{5,1},{9,13},{13,9},{2,6},{6,2},{1... | collective-permute-start | bytes 393224 | tf_op jit(solution)/shard_map/ppermute | solution.py:84
  8.0 2.2 %copy-start = (bf16[1,1,128,128,128]{4,3,2,1,0:T(8,128)(2,1)S(1)}, bf16[1,1,128,128,128]{4,3,2,1,0:T(8,128)(2,1)}, u32[]{:S(2)}) copy-start(bf16[1,1,128,128,128]{4,3,2,1,0:T(8,128)(2,1)} %param.13) | copy-start | bytes 12582916
  10.2 0.7 copy-start.4
  11.5 2.1 %copy-start.1 = (bf16[1,1,256,256]{3,2,1,0:T(8,128)(2,1)S(1)}, bf16[1,1,256,256]{3,2,1,0:T(8,128)(2,1)}, u32[]{:S(2)}) copy-start(bf16[1,1,256,256]{3,2,1,0:T(8,128)(2,1)} %param.8) | copy-start | bytes 393220
  14.9 0.7 copy-start.3
  15.5 13.6 %collective-permute-start.3 = (bf16[256,256]{1,0:T(8,128)(2,1)S(1)}, bf16[256,256]{1,0:T(8,128)(2,1)S(1)}, u32[]{:S(2)}, u32[]{:S(2)}) collective-permute-start(bf16[256,256]{1,0:T(8,128)(2,1)S(1)} %get-tuple-element.17), channel_id=1, source_target_pairs={{0,2},{1,3},{2,0},{3,1},{4,6},{5,7},{6,4},{7,5},{8,10},{9,11},{10,... | collective-permute-start | bytes 393224 | tf_op jit(solution)/shard_map/ppermute | solution.py:84
  19.2 10.0 %collective-permute-start.4 = (bf16[256,256]{1,0:T(8,128)(2,1)S(1)}, bf16[256,256]{1,0:T(8,128)(2,1)S(1)}, u32[]{:S(2)}, u32[]{:S(2)}) collective-permute-start(bf16[256,256]{1,0:T(8,128)(2,1)S(1)} %get-tuple-element.18), channel_id=1, source_target_pairs={{0,3},{1,2},{2,1},{3,0},{4,7},{5,6},{6,5},{7,4},{8,11},{9,10},{10,... | collective-permute-start | bytes 393224 | tf_op jit(solution)/shard_map/ppermute | solution.py:84
  20.0 10.0 %collective-permute-start.5 = (bf16[256,256]{1,0:T(8,128)(2,1)S(1)}, bf16[256,256]{1,0:T(8,128)(2,1)S(1)}, u32[]{:S(2)}, u32[]{:S(2)}) collective-permute-start(bf16[256,256]{1,0:T(8,128)(2,1)S(1)} %get-tuple-element.19), channel_id=1, source_target_pairs={{0,1},{1,0},{2,3},{3,2},{4,5},{5,4},{6,7},{7,6},{8,9},{9,8},{10,11... | collective-permute-start | bytes 393224 | tf_op jit(solution)/shard_map/ppermute | solution.py:84
  29.1 0.9 %copy-start.6 = (bf16[256,256]{1,0:T(8,128)(2,1)}, bf16[256,256]{1,0:T(8,128)(2,1)S(1)}, u32[]{:S(2)}) copy-start(bf16[256,256]{1,0:T(8,128)(2,1)S(1)} %collective-permute-done.3.refs_1_) | copy-start | bytes 393220
  29.1 0.9 %copy-start.7 = (bf16[256,256]{1,0:T(8,128)(2,1)}, bf16[256,256]{1,0:T(8,128)(2,1)S(1)}, u32[]{:S(2)}) copy-start(bf16[256,256]{1,0:T(8,128)(2,1)S(1)} %collective-permute-done.4.refs_2_) | copy-start | bytes 393220
  33.0 8.5 %collective-permute-start.6 = (bf16[256,256]{1,0:T(8,128)(2,1)}, bf16[256,256]{1,0:T(8,128)(2,1)S(1)}, u32[]{:S(2)}, u32[]{:S(2)}) collective-permute-start(bf16[256,256]{1,0:T(8,128)(2,1)} %get-tuple-element.21.refs_0_), channel_id=1, source_target_pairs={{0,1},{1,0},{2,3},{3,2},{4,5},{5,4},{6,7},{7,6},{8,9},{9,8},{10,11... | collective-permute-start | bytes 393224 | tf_op jit(solution)/shard_map/ppermute | solution.py:84
  35.1 7.8 %collective-permute-start.7 = (bf16[256,256]{1,0:T(8,128)(2,1)}, bf16[256,256]{1,0:T(8,128)(2,1)S(1)}, u32[]{:S(2)}, u32[]{:S(2)}) collective-permute-start(bf16[256,256]{1,0:T(8,128)(2,1)} %get-tuple-element.21.refs_0_), channel_id=1, source_target_pairs={{0,2},{1,3},{2,0},{3,1},{4,6},{5,7},{6,4},{7,5},{8,10},{9,11},{10,... | collective-permute-start | bytes 393224 | tf_op jit(solution)/shard_map/ppermute | solution.py:84
  37.0 10.8 %collective-permute-start.8 = (bf16[256,256]{1,0:T(8,128)(2,1)}, bf16[256,256]{1,0:T(8,128)(2,1)S(1)}, u32[]{:S(2)}, u32[]{:S(2)}) collective-permute-start(bf16[256,256]{1,0:T(8,128)(2,1)} %get-tuple-element.21.refs_0_), channel_id=1, source_target_pairs={{0,3},{1,2},{2,1},{3,0},{4,7},{5,6},{6,5},{7,4},{8,11},{9,10},{10,... | collective-permute-start | bytes 393224 | tf_op jit(solution)/shard_map/ppermute | solution.py:84
  40.1 10.1 %collective-permute-start.11 = (f32[272,256]{1,0:T(8,128)S(1)}, f32[272,256]{1,0:T(8,128)S(1)}, u32[]{:S(2)}, u32[]{:S(2)}) collective-permute-start(f32[272,256]{1,0:T(8,128)S(1)} %pad_maximum_fusion), channel_id=1, source_target_pairs={{0,4},{4,0},{8,12},{12,8},{1,5},{5,1},{9,13},{13,9},{2,6},{6,2},{1... | collective-permute-start | bytes 835592 | tf_op jit(solution)/shard_map/ppermute | solution.py:84
  47.9 0.9 %copy-start.2 = (bf16[256,256]{1,0:T(8,128)(2,1)S(1)}, bf16[256,256]{1,0:T(8,128)(2,1)}, u32[]{:S(2)}) copy-start(bf16[256,256]{1,0:T(8,128)(2,1)} %get-tuple-element.21.refs_0_) | copy-start | bytes 393220
  50.1 12.2 %collective-permute-start.9 = (bf16[2,256,256]{2,1,0:T(8,128)(2,1)S(1)}, bf16[2,256,256]{2,1,0:T(8,128)(2,1)S(1)}, u32[]{:S(2)}, u32[]{:S(2)}) collective-permute-start(bf16[2,256,256]{2,1,0:T(8,128)(2,1)S(1)} %pad_maximum_fusion.2), channel_id=1, source_target_pairs={{0,4},{4,0},{8,12},{12,8},{1,5},{5,1},{9,13},{13,9},{2,6},{6,2},{1... | collective-permute-start | bytes 786440 | tf_op jit(solution)/shard_map/ppermute | solution.py:84
  51.2 6.1 %collective-permute-start.12 = (f32[136,256]{1,0:T(8,128)S(1)}, f32[136,256]{1,0:T(8,128)S(1)}, u32[]{:S(2)}, u32[]{:S(2)}) collective-permute-start(f32[136,256]{1,0:T(8,128)S(1)} %fusion.5), channel_id=1, source_target_pairs={{0,8},{4,12},{8,0},{12,4},{1,9},{5,13},{9,1},{13,5},{2,10},{6,14},... | collective-permute-start | bytes 417800 | tf_op jit(solution)/shard_map/ppermute | solution.py:84
  57.3 14.3 %collective-permute-start.13 = (f32[136,256]{1,0:T(8,128)S(1)}, f32[136,256]{1,0:T(8,128)S(1)}, u32[]{:S(2)}, u32[]{:S(2)}) collective-permute-start(f32[136,256]{1,0:T(8,128)S(1)} %add.38), channel_id=1, source_target_pairs={{0,2},{1,3},{2,0},{3,1},{4,6},{5,7},{6,4},{7,5},{8,10},{9,11},{10,... | collective-permute-start | bytes 417800 | tf_op jit(solution)/shard_map/ppermute | solution.py:84
  61.7 10.0 %collective-permute-start.14 = (f32[136,256]{1,0:T(8,128)S(1)}, f32[136,256]{1,0:T(8,128)S(1)}, u32[]{:S(2)}, u32[]{:S(2)}) collective-permute-start(f32[136,256]{1,0:T(8,128)S(1)} %add.38), channel_id=1, source_target_pairs={{0,3},{1,2},{2,1},{3,0},{4,7},{5,6},{6,5},{7,4},{8,11},{9,10},{10,... | collective-permute-start | bytes 417800 | tf_op jit(solution)/shard_map/ppermute | solution.py:84
  62.3 10.3 %collective-permute-start.15 = (f32[136,256]{1,0:T(8,128)S(1)}, f32[136,256]{1,0:T(8,128)S(1)}, u32[]{:S(2)}, u32[]{:S(2)}) collective-permute-start(f32[136,256]{1,0:T(8,128)S(1)} %add.38), channel_id=1, source_target_pairs={{0,1},{1,0},{2,3},{3,2},{4,5},{5,4},{6,7},{7,6},{8,9},{9,8},{10,11... | collective-permute-start | bytes 417800 | tf_op jit(solution)/shard_map/ppermute | solution.py:84
  62.4 10.4 %collective-permute-start.10 = (bf16[256,256]{1,0:T(8,128)(2,1)S(1)}, bf16[256,256]{1,0:T(8,128)(2,1)S(1)}, u32[]{:S(2)}, u32[]{:S(2)}) collective-permute-start(bf16[256,256]{1,0:T(8,128)(2,1)S(1)} %fusion.1), channel_id=1, source_target_pairs={{0,8},{4,12},{8,0},{12,4},{1,9},{5,13},{9,1},{13,5},{2,10},{6,14},... | collective-permute-start | bytes 393224 | tf_op jit(solution)/shard_map/ppermute | solution.py:84
  72.7 1.4 %collective-permute-start.16 = (f32[136,256]{1,0:T(8,128)S(1)}, f32[136,256]{1,0:T(8,128)S(1)}, u32[]{:S(2)}, u32[]{:S(2)}) collective-permute-start(f32[136,256]{1,0:T(8,128)S(1)} %add_add_fusion), channel_id=1, source_target_pairs={{0,4},{4,0},{8,12},{12,8},{1,5},{5,1},{9,13},{13,9},{2,6},{6,2},{1... | collective-permute-start | bytes 417800 | tf_op jit(solution)/shard_map/ppermute | solution.py:84
  (2 other events, 1.3 us)

commit v2 on v1

v2 whole, which is shorter than its diff:
```python
import functools

import jax
import jax.numpy as jnp
from jax import lax
from jax.experimental import pallas as pl
from jax.experimental.pallas import tpu as pltpu
from jax.sharding import PartitionSpec as P

BF = jnp.bfloat16
F32 = jnp.float32
VMEM = pl.BlockSpec(memory_space=pltpu.VMEM)
HBM = pl.BlockSpec(memory_space=pltpu.HBM)
PIECES = 1


def tile_terms(values, picked, forward):
    if forward:
        return jnp.einsum("tij,tjf->tif", values, picked, preferred_element_type=jnp.float32)
    return jnp.einsum("tji,tjf->tif", values, picked, preferred_element_type=jnp.float32)


def every_slot(values, source_idx, target_idx, live_count, source, forward):
    width = min(16, values.shape[0])
    targets = source.shape[0]

    def advance(index, carry):
        start = index * width
        block_values = lax.dynamic_slice_in_dim(values, start, width, 0)
        block_source = lax.dynamic_slice_in_dim(source_idx, start, width, 0)
        block_target = lax.dynamic_slice_in_dim(target_idx, start, width, 0)
        picked = jnp.take(source, block_source, axis=0)
        terms = tile_terms(block_values, picked, forward)
        alive_mask = (start + jnp.arange(width) < live_count).astype(jnp.float32)
        placing = (jnp.arange(targets)[:, None] == block_target[None, :]).astype(jnp.float32)
        placing = placing * alive_mask[None, :]
        added = jnp.einsum("rt,tif->rif", placing, terms, precision=lax.Precision.HIGHEST)
        return carry + added

    initial = jnp.zeros(source.shape, jnp.float32)
    return lax.fori_loop(0, values.shape[0] // width, advance, initial)


def sparse_device(features, weight, bias, tile_rows, tile_cols, tile_vals, tile_count, cotangent):
    own_rows = features[0, 0]
    rows_dev, feat = own_rows.shape
    tile = tile_vals.shape[-1]
    values = tile_vals[0, 0]
    row_idx = tile_rows[0, 0]
    col_idx = tile_cols[0, 0]
    live_count = tile_count[0, 0]
    gathered = lax.all_gather(own_rows, "row", axis=0, tiled=True)
    block_nodes = gathered.shape[0]
    source = gathered.reshape(block_nodes // tile, tile, feat)
    forward_terms = every_slot(values, col_idx, row_idx, live_count, source, True)
    summed = lax.psum_scatter(
        forward_terms.reshape(block_nodes, feat).astype(BF), "col", scatter_dimension=0, tiled=True
    )
    pre = jnp.dot(summed, weight, preferred_element_type=F32) + bias
    hidden = jax.nn.silu(pre).astype(BF)
    sigma = jax.nn.sigmoid(pre)
    slope = sigma * (1.0 + pre * (1.0 - sigma))
    grad_pre = (cotangent[0, 0].astype(F32) * slope).astype(BF)
    weight_term = lax.dot_general(
        summed, grad_pre, (((0,), (0,)), ((), ())), preferred_element_type=F32
    )
    bias_term = jnp.sum(grad_pre.astype(F32), axis=0)
    weight_sum, bias_sum = lax.psum((weight_term, bias_term), ("row", "col"))
    node_total = rows_dev * lax.axis_size("row") * lax.axis_size("col")
    factor = float(node_total) ** (-0.5)
    grad_local = jnp.dot(grad_pre, weight.T, preferred_element_type=F32).astype(BF)
    grad_rows = lax.all_gather(grad_local, "col", axis=0, tiled=True)
    grad_source = grad_rows.reshape(block_nodes // tile, tile, feat)
    backward_terms = every_slot(values, row_idx, col_idx, live_count, grad_source, False)
    back_summed = lax.psum_scatter(
        backward_terms.reshape(block_nodes, feat).astype(BF), "row", scatter_dimension=0, tiled=True
    )
    hidden_out = hidden.reshape(1, 1, rows_dev, feat)
    grad_features = back_summed.reshape(1, 1, rows_dev, feat)
    return (hidden_out, grad_features, weight_sum * factor, bias_sum * factor)


def swap(x, axis, bit):
    size = lax.axis_size(axis)
    return lax.ppermute(x, axis, [(i, i ^ bit) for i in range(size)])


def tree(own, near, far, cross):
    own, near, far, cross = (x.astype(F32) for x in (own, near, far, cross))
    return (own + near) + (far + cross)


def build_kernel(slots_hbm, vals_hbm, dense_ref, slots_ref, vals_ref, total, sem):
    slots, tile, _ = vals_ref.shape
    chunks = sem.shape[0] - 1
    width = slots // chunks
    per = dense_ref.shape[2] // tile
    wide = total.shape[0]
    small = pltpu.make_async_copy(slots_hbm, slots_ref, sem.at[chunks])
    big = [
        pltpu.make_async_copy(
            vals_hbm.at[pl.ds(i * width, width)], vals_ref.at[pl.ds(i * width, width)], sem.at[i]
        )
        for i in range(chunks)
    ]
    small.start()
    for copy in big:
        copy.start()
    total[...] = jnp.zeros_like(total)
    small.wait()
    live = slots_ref[slots]

    def place(slot, carry):
        spot = slots_ref[slot]
        where = pl.ds(pl.multiple_of(lax.div(spot, wide) * tile, tile), tile)
        total[lax.rem(spot, wide), where, :] += vals_ref[slot].astype(F32)
        return carry

    for i in range(chunks):
        big[i].wait()
        lax.fori_loop(i * width, jnp.clip(live, i * width, (i + 1) * width), place, 0)

    for col in range(wide):
        dense_ref[col // per, :, (col % per) * tile : (col % per + 1) * tile] = total[col].astype(BF)


def build_dense(values, row_idx, col_idx, count, parts, rows_dev):
    slots, tile, _ = values.shape
    nodes = parts * rows_dev
    wide = nodes // tile
    chunks = 8
    listed = jnp.concatenate([row_idx * wide + col_idx, jnp.broadcast_to(count, (slots,))])
    return pl.pallas_call(
        build_kernel,
        in_specs=[HBM] * 2,
        out_specs=VMEM,
        out_shape=jax.ShapeDtypeStruct((parts, nodes, rows_dev), BF),
        scratch_shapes=[
            pltpu.SMEM(listed.shape, jnp.int32),
            pltpu.VMEM(values.shape, BF),
            pltpu.VMEM((wide, nodes, tile), F32),
            pltpu.SemaphoreType.DMA((chunks + 1,)),
        ],
        compiler_params=pltpu.CompilerParams(vmem_limit_bytes=50 << 20),
        cost_estimate=pl.CostEstimate(flops=8 * nodes * nodes, bytes_accessed=6 * nodes * nodes, transcendentals=0),
        name="build_dense",
    )(listed, values)


def forward_kernel(dense_ref, *refs):
    parts = dense_ref.shape[0]
    sources, outs = refs[:parts], refs[parts:]
    rows = sources[0].shape[0]
    row, col = lax.axis_index("row"), lax.axis_index("col")
    for k in range(parts):
        where = pl.ds(pl.multiple_of((col ^ k) * rows, rows), rows)
        total = None
        for j in range(parts):
            term = jnp.dot(dense_ref[row ^ j, where, :], sources[j][...], preferred_element_type=F32)
            total = term if total is None else total + term
        total = total.astype(BF)
        for h in range(PIECES):
            height = rows // PIECES
            outs[h * parts + k][...] = total[h * height : (h + 1) * height]


def forward(dense, sources):
    parts = len(sources)
    rows, feat = sources[0].shape
    return pl.pallas_call(
        forward_kernel,
        in_specs=[VMEM] * (1 + parts),
        out_specs=[VMEM] * (parts * PIECES),
        out_shape=[jax.ShapeDtypeStruct((rows // PIECES, feat), BF)] * (parts * PIECES),
        compiler_params=pltpu.CompilerParams(vmem_limit_bytes=8 << 20),
        cost_estimate=product_cost(parts, rows, feat),
        name="forward",
    )(dense, *sources)


def product_cost(parts, rows, feat):
    return pl.CostEstimate(
        flops=2 * parts * parts * rows * rows * feat,
        bytes_accessed=2 * parts * rows * (parts * rows + 2 * feat),
        transcendentals=0,
    )


def backward_kernel(dense_ref, *refs):
    parts = dense_ref.shape[0]
    sources, refs = refs[: parts * PIECES], refs[parts * PIECES :]
    keep_refs, pair_ref = refs[:2], refs[2]
    rows = sources[0].shape[0] * PIECES
    row, col = lax.axis_index("row"), lax.axis_index("col")
    for k in (1, 3, 0, 2):
        total = None
        for j in range(parts):
            where = pl.ds(pl.multiple_of((col ^ j) * rows, rows), rows)
            source = jnp.concatenate([sources[h * parts + j][...] for h in range(PIECES)], axis=0)
            term = lax.dot_general(
                dense_ref[row ^ k, where, :], source, (((0,), (0,)), ((), ())),
                preferred_element_type=F32,
            )
            total = term if total is None else total + term
        if k % 2:
            pair_ref[k // 2] = total.astype(BF)
        else:
            keep_refs[k // 2][...] = total


def backward(dense, sources):
    parts = len(sources) // PIECES
    rows, feat = sources[0].shape[0] * PIECES, sources[0].shape[1]
    return pl.pallas_call(
        backward_kernel,
        in_specs=[VMEM] * (1 + parts * PIECES),
        out_specs=[VMEM] * 3,
        out_shape=[
            jax.ShapeDtypeStruct((rows, feat), F32),
            jax.ShapeDtypeStruct((rows, feat), F32),
            jax.ShapeDtypeStruct((2, rows, feat), BF),
        ],
        compiler_params=pltpu.CompilerParams(vmem_limit_bytes=8 << 20),
        cost_estimate=product_cost(parts, rows, feat),
        name="backward",
    )(dense, *sources)


def pair_kernel(keep_ref, send_ref, arrived_ref, kept_ref, sent_ref):
    kept_ref[...] = keep_ref[...] + arrived_ref[0].astype(F32)
    sent_ref[...] = (send_ref[...] + arrived_ref[1].astype(F32)).astype(BF)


def pair_sum(keep, send, arrived):
    return pl.pallas_call(
        pair_kernel,
        in_specs=[VMEM] * 3,
        out_specs=[VMEM] * 2,
        out_shape=[
            jax.ShapeDtypeStruct(keep.shape, F32),
            jax.ShapeDtypeStruct(send.shape, BF),
        ],
        compiler_params=pltpu.CompilerParams(vmem_limit_bytes=8 << 20),
        cost_estimate=pl.CostEstimate(flops=3 * keep.size, bytes_accessed=20 * keep.size, transcendentals=0),
        name="pair_sum",
    )(keep, send, arrived)


def gradient_kernel(weight_ref, bias_ref, cot_ref, *refs):
    refs, (agg_ref, summed_ref, pre_ref, grad_ref) = refs[:-4], refs[-4:]
    terms = refs[:4]
    summed = terms[0][...].astype(F32)
    for term in terms[1:]:
        summed = summed + term[...].astype(F32)
    summed = summed.astype(BF)
    summed_ref[...] = summed
    pre = jnp.dot(summed, weight_ref[...], preferred_element_type=F32) + bias_ref[...]
    pre_ref[...] = pre
    sigma = jax.nn.sigmoid(pre)
    slope = sigma * (1.0 + pre * (1.0 - sigma))
    grad_pre = (cot_ref[...].astype(F32) * slope).astype(BF)
    grad_ref[...] = grad_pre
    agg_ref[...] = lax.dot_general(
        grad_pre, weight_ref[...], (((1,), (1,)), ((), ())), preferred_element_type=F32
    ).astype(BF)


def gradient(weight, bias, cot, terms, after, piece):
    rows, feat = terms[0].shape
    block = jax.ShapeDtypeStruct((rows, feat), BF)
    return pl.pallas_call(
        gradient_kernel,
        grid=(1,),
        in_specs=[VMEM, VMEM, pl.BlockSpec((rows, feat), lambda _: (piece, 0))]
        + [VMEM] * (len(terms) + len(after)),
        out_specs=[VMEM] * 4,
        out_shape=[block, block, jax.ShapeDtypeStruct((rows, feat), F32), block],
        compiler_params=pltpu.CompilerParams(vmem_limit_bytes=8 << 20),
        cost_estimate=pl.CostEstimate(
            flops=4 * rows * feat * feat, bytes_accessed=20 * rows * feat, transcendentals=rows * feat
        ),
        name="gradient",
    )(weight, bias, cot, *terms, *after)


def totals_kernel(after_ref, *refs):
    del after_ref
    summed_refs, pre_refs, grad_refs = (refs[i * PIECES : (i + 1) * PIECES] for i in range(3))
    hidden_ref, mine_ref, other_ref = refs[3 * PIECES :]
    height, feat = summed_refs[0].shape
    core = lax.axis_index("row") & 1
    for h in range(PIECES):
        pre = pre_refs[h][...]
        hidden_ref[h * height : (h + 1) * height, :] = (pre * jax.nn.sigmoid(pre)).astype(BF)
    grad_pre = jnp.concatenate([ref[...] for ref in grad_refs], axis=0)
    bias_row = jnp.sum(grad_pre.astype(F32), axis=0, keepdims=True)
    middle = feat // 2
    for target, index in ((mine_ref, core), (other_ref, 1 - core)):
        window = pl.ds(pl.multiple_of(index * middle, middle), middle)
        columns = jnp.concatenate([ref[:, window] for ref in summed_refs], axis=0)
        product = lax.dot_general(columns, grad_pre, (((0,), (0,)), ((), ())), preferred_element_type=F32)
        spread = jnp.broadcast_to(bias_row, (mine_ref.shape[0] - middle, feat))
        target[:middle, :] = product.astype(BF)
        target[middle:, :] = spread.astype(BF)


def totals(after, summed, pre, grad_pre):
    rows, feat = pre[0].shape[0] * PIECES, pre[0].shape[1]
    half = (feat // 2 + 16, feat)
    return pl.pallas_call(
        totals_kernel,
        in_specs=[VMEM] * (1 + 3 * PIECES),
        out_specs=[VMEM] * 3,
        out_shape=[
            jax.ShapeDtypeStruct((rows, feat), BF),
            jax.ShapeDtypeStruct(half, BF),
            jax.ShapeDtypeStruct(half, BF),
        ],
        compiler_params=pltpu.CompilerParams(vmem_limit_bytes=8 << 20),
        cost_estimate=pl.CostEstimate(
            flops=2 * rows * feat * feat, bytes_accessed=20 * rows * feat, transcendentals=rows * feat
        ),
        name="totals",
    )(after, *summed, *pre, *grad_pre)


def dense_device(features, weight, bias, tile_rows, tile_cols, tile_vals, tile_count, cotangent):
    own = features[0, 0]
    rows, feat = own.shape
    row = lax.axis_index("row")

    from_chip = swap(own, "row", 2)
    from_core = swap(own, "row", 1)
    dense = build_dense(tile_vals[0, 0], tile_rows[0, 0], tile_cols[0, 0], tile_count[0], 4, rows)
    dense, from_chip = lax.optimization_barrier((dense, from_chip))
    sources = [own, from_core, from_chip, swap(from_chip, "row", 1)]
    partial = forward(dense, sources)

    kept, gathered, after = [], [], []
    for h in range(PIECES):
        mine = partial[h * 4 : (h + 1) * 4]
        terms = [mine[0]] + [swap(mine[k], "col", k) for k in (2, 3, 1)]
        agg, *rest = gradient(weight, bias[None, :], cotangent[0, 0], terms, after, h)
        kept.append(rest)
        after = [agg]
        early = swap(agg, "col", 1)
        grads = {0: agg, 1: early}
        grads[2] = swap(agg, "col", 2)
        grads[3] = swap(grads[2], "col", 1)
        gathered += [grads[k] for k in range(4)]

    hidden, mine, others = totals(agg, *zip(*kept))
    half = tree(mine, swap(others, "row", 1), swap(mine, "row", 2), swap(others, "row", 3)).astype(BF)

    keep, send, pair = backward(dense, gathered)
    keep, send = pair_sum(keep, send, swap(pair, "row", 1))
    grad_features = (keep + swap(send, "row", 2).astype(F32)).astype(BF)

    half = tree(half, *(swap(half, "col", k) for k in (1, 2, 3)))
    twin = swap(half, "row", 1)
    first = row % 2 == 0
    middle = feat // 2
    factor = float(rows * 16) ** (-0.5)
    low, high = jnp.where(first, half, twin), jnp.where(first, twin, half)
    grad_weight = jnp.concatenate([low[:middle], high[:middle]], axis=0) * factor
    return (hidden[None, None], grad_features[None, None], grad_weight, half[middle] * factor)


def per_device(features, weight, bias, tile_rows, tile_cols, tile_vals, tile_count, cotangent):
    rows = features.shape[2]
    slots, tile, _ = tile_vals.shape[2:]
    square = lax.axis_size("row") == 4 and lax.axis_size("col") == 4
    dense_fits = (4 * rows // tile) ** 2 <= slots
    chosen = dense_device if square and dense_fits else sparse_device
    return chosen(features, weight, bias, tile_rows, tile_cols, tile_vals, tile_count, cotangent)


def solution(mesh):
    placed = (
        P(("groups", "col"), "row", None, None),
        P(),
        P(),
        P(("groups", "row"), "col", None),
        P(("groups", "row"), "col", None),
        P(("groups", "row"), "col", None, None, None),
        P(("groups", "row"), "col"),
        P(("groups", "row"), "col", None, None),
    )
    return jax.shard_map(
        per_device,
        mesh=mesh,
        in_specs=placed,
        out_specs=(
            P(("groups", "row"), "col", None, None),
            P(("groups", "col"), "row", None, None),
            P("groups", None),
            P("groups"),
        ),
        check_vma=False,
    )
```

time: 75.6 us -> 52.8 us (0.70)
  waiting for transfers between devices: 34.9 us -> 24 us
  local copies, waits for them, and re-layouts: 6.37 us -> 0.02 us
  starting transfers between devices: 21.7 us -> 19.5 us
  Pallas kernels: 6.93 us -> 5.24 us
  other arithmetic: 4.14 us -> 2.75 us
    ppermute x17 -> x18, waiting for transfers between devices: 34.9 us -> 24 us  [swap(): return lax.ppermute(x, axis, [(i, i ^ bit) for i in range(size)])]
    unnamed x18 -> x8, local copies, waits for them, and re-layouts: 5.69 us -> 0.02 us
    ppermute x17 -> x18, starting transfers between devices: 21.7 us -> 19.5 us  [swap(): return lax.ppermute(x, axis, [(i, i ^ bit) for i in range(size)])]
    pallas_call x4 -> x6, Pallas kernels: 6.93 us -> 5.24 us  [the longest x1 2.54 us: build_dense(): pl.pallas_call(build_kernel, in_specs=[HBM] * 2, out_specs=VMEM, out_shap...]
    concatenate x1 -> x0, other arithmetic: 0.97 us -> none  [dense_device(): jnp.concatenate([wgrad, jnp.broadcast_to(bgrad, (16, feat))], axis=0)]
  transfers between devices with their start and end apart: 17 -> 18, of which waited for: 10 -> 11; matrix products, arithmetic and copies ran while one was open for 5% -> 4% of each run, Pallas kernels for 4% -> 8%
where the time goes in v2:
time: 52.8 us; the launch traced here: 53 us
  waiting for transfers between devices  24 us (45%)
  starting transfers between devices  19.5 us (37%)
  Pallas kernels  5.24 us (10%)
  other arithmetic  2.75 us (5%)
  between operations  1.4 us (3%)
    ppermute x18, waiting for transfers between devices, swap(): return lax.ppermute(x, axis, [(i, i ^ bit) for i in range(size)])  24 us
    ppermute x18, starting transfers between devices, swap(): return lax.ppermute(x, axis, [(i, i ^ bit) for i in range(size)])  19.5 us
    pallas_call x1, Pallas kernels, build_dense(): pl.pallas_call(build_kernel, in_specs=[HBM] * 2, out_specs=VMEM, out_shap...  2.54 us
  transfers between devices with their start and end apart: 18, of which 11 were waited for; matrix products, arithmetic and copies ran while one was open for 4% of the time, Pallas kernels for 8%

profile of v2, /device:TPU:0, one launch (start us, length us, event | category | flops | bytes accessed | tf_op | source)
XLA Modules:
  0.0 53.0 jit_solution(13598098477753923947)
XLA Ops:
  0.6 3.0 %collective-permute-start = (bf16[256,256]{1,0:T(8,128)(2,1)}, bf16[256,256]{1,0:T(8,128)(2,1)S(1)}, u32[]{:S(2)}, u32[]{:S(2)}) collective-permute-start(bf16[256,256]{1,0:T(8,128)(2,1)} %bitcast.12), channel_id=1, source_target_pairs={{0,8},{4,12},{8,0},{12,4},{1,9},{5,13},{9,1},{13,5},{2,10},{6,14},... | collective-permute-start | bytes 393224 | tf_op jit(solution)/shard_map/ppermute | solution.py:85
  4.3 0.7 %add_bitcast_fusion = s32[128]{0:T(128)S(1)} fusion(s32[1,1,128]{2,1,0:T(1,128)} %param.12, s32[1,1,128]{2,1,0:T(1,128)} %param.11), kind=kLoop, calls=%fused_computation.8 | loop fusion | flops 256 | bytes 1536 | tf_op jit(solution)/shard_map/add | solution.py:132
  5.0 2.5 %build_dense.1.dense_ref = bf16[4,1024,256]{2,1,0:T(8,128)(2,1)S(1)} custom-call(s32[256]{0:T(256)S(1)} %concatenate.6.slots_hbm, bf16[128,128,128]{2,1,0:T(8,128)(2,1)} %bitcast.17), custom_call_target="tpu_custom_call" | custom-call | flops 8388608 | bytes 6291456 | tf_op jit(solution)/shard_map/build_dense/pallas_call | solution.py:133
  7.6 1.0 %collective-permute-start.2 = (bf16[256,256]{1,0:T(8,128)(2,1)S(1)}, bf16[256,256]{1,0:T(8,128)(2,1)S(1)}, u32[]{:S(2)}, u32[]{:S(2)}) collective-permute-start(bf16[256,256]{1,0:T(8,128)(2,1)S(1)} %collective-permute-done.refs_2_), channel_id=1, source_target_pairs={{0,4},{4,0},{8,12},{12,8},{1,5},{5,1},{9,13},{13,9},{2,6},{6,2},{1... | collective-permute-start | bytes 393224 | tf_op jit(solution)/shard_map/ppermute | solution.py:85
  8.6 1.0 %collective-permute-done.2.refs_3_ = bf16[256,256]{1,0:T(8,128)(2,1)S(1)} collective-permute-done((bf16[256,256]{1,0:T(8,128)(2,1)S(1)}, bf16[256,256]{1,0:T(8,128)(2,1)S(1)}, u32[]{:S(2)}, u32[]{:S(2)}) %collective-permute-start.2) | collective-permute-done | bytes 131104 | tf_op jit(solution)/shard_map/ppermute | solution.py:85
  9.6 0.7 %forward.1 = (bf16[256,256]{1,0:T(8,128)(2,1)S(1)}, bf16[256,256]{1,0:T(8,128)(2,1)S(1)}, bf16[256,256]{1,0:T(8,128)(2,1)S(1)}, bf16[256,256]{1,0:T(8,128)(2,1)S(1)}) custom-call(bf16[4,1024,256]{2,1,0:T(8,128)(2,1)S(1)} %build_dense.1.dense_ref, bf16[256,256]{1,0:T(8,128)(2,1)S(1)} %bitcast.14, bf16[256,256]{1,0:T(8,128)(2,1)S(1)} %collective-permute-done.1.refs_1_, ...), custom_call_target="tpu_custom_call" | custom-call | flops 536870912 | bytes 3145728 | tf_op jit(solution)/shard_map/forward/pallas_call | solution.py:170
  10.3 2.8 %collective-permute-start.3 = (bf16[256,256]{1,0:T(8,128)(2,1)S(1)}, bf16[256,256]{1,0:T(8,128)(2,1)S(1)}, u32[]{:S(2)}, u32[]{:S(2)}) collective-permute-start(bf16[256,256]{1,0:T(8,128)(2,1)S(1)} %get-tuple-element.25), channel_id=1, source_target_pairs={{0,2},{1,3},{2,0},{3,1},{4,6},{5,7},{6,4},{7,5},{8,10},{9,11},{10,... | collective-permute-start | bytes 393224 | tf_op jit(solution)/shard_map/ppermute | solution.py:85
  13.1 1.0 %collective-permute-start.4 = (bf16[256,256]{1,0:T(8,128)(2,1)S(1)}, bf16[256,256]{1,0:T(8,128)(2,1)S(1)}, u32[]{:S(2)}, u32[]{:S(2)}) collective-permute-start(bf16[256,256]{1,0:T(8,128)(2,1)S(1)} %get-tuple-element.26), channel_id=1, source_target_pairs={{0,3},{1,2},{2,1},{3,0},{4,7},{5,6},{6,5},{7,4},{8,11},{9,10},{10,... | collective-permute-start | bytes 393224 | tf_op jit(solution)/shard_map/ppermute | solution.py:85
  14.6 8.6 %collective-permute-done.3.refs_1_ = bf16[256,256]{1,0:T(8,128)(2,1)S(1)} collective-permute-done((bf16[256,256]{1,0:T(8,128)(2,1)S(1)}, bf16[256,256]{1,0:T(8,128)(2,1)S(1)}, u32[]{:S(2)}, u32[]{:S(2)}) %collective-permute-start.3) | collective-permute-done | bytes 131104 | tf_op jit(solution)/shard_map/ppermute | solution.py:85
  23.2 0.9 %collective-permute-done.5.refs_3_ = bf16[256,256]{1,0:T(8,128)(2,1)S(1)} collective-permute-done((bf16[256,256]{1,0:T(8,128)(2,1)S(1)}, bf16[256,256]{1,0:T(8,128)(2,1)S(1)}, u32[]{:S(2)}, u32[]{:S(2)}) %collective-permute-start.5) | collective-permute-done | bytes 131104 | tf_op jit(solution)/shard_map/ppermute | solution.py:85
  24.6 4.1 %collective-permute-start.7 = (bf16[256,256]{1,0:T(8,128)(2,1)S(1)}, bf16[256,256]{1,0:T(8,128)(2,1)S(1)}, u32[]{:S(2)}, u32[]{:S(2)}) collective-permute-start(bf16[256,256]{1,0:T(8,128)(2,1)S(1)} %get-tuple-element.28.after_ref.refs_0_), channel_id=1, source_target_pairs={{0,2},{1,3},{2,0},{3,1},{4,6},{5,7},{6,4},{7,5},{8,10},{9,11},{10,... | collective-permute-start | bytes 393224 | tf_op jit(solution)/shard_map/ppermute | solution.py:85
  28.7 0.8 %totals.1 = (bf16[256,256]{1,0:T(8,128)(2,1)}, bf16[144,256]{1,0:T(8,128)(2,1)S(1)}, bf16[144,256]{1,0:T(8,128)(2,1)S(1)}) custom-call(bf16[256,256]{1,0:T(8,128)(2,1)S(1)} %get-tuple-element.28.after_ref.refs_0_, bf16[256,256]{1,0:T(8,128)(2,1)S(1)} %get-tuple-element.29.refs_0_, f32[256,256]{1,0:T(8,128)S(1)} %get-tuple-element.30.refs_1_, ...), custom_call_target="tpu_custom_call" | custom-call | flops 33554432 | bytes 1310720 | tf_op jit(solution)/shard_map/totals/pallas_call | solution.py:310
  29.5 1.4 %collective-permute-start.12 = (bf16[144,256]{1,0:T(8,128)(2,1)S(1)}, bf16[144,256]{1,0:T(8,128)(2,1)S(1)}, u32[]{:S(2)}, u32[]{:S(2)}) collective-permute-start(bf16[144,256]{1,0:T(8,128)(2,1)S(1)} %get-tuple-element.38), channel_id=1, source_target_pairs={{0,8},{4,12},{8,0},{12,4},{1,9},{5,13},{9,1},{13,5},{2,10},{6,14},... | collective-permute-start | bytes 221192 | tf_op jit(solution)/shard_map/ppermute | solution.py:85
  31.4 3.9 %collective-permute-done.7.refs_2_ = bf16[256,256]{1,0:T(8,128)(2,1)S(1)} collective-permute-done((bf16[256,256]{1,0:T(8,128)(2,1)S(1)}, bf16[256,256]{1,0:T(8,128)(2,1)S(1)}, u32[]{:S(2)}, u32[]{:S(2)}) %collective-permute-start.7) | collective-permute-done | bytes 131104 | tf_op jit(solution)/shard_map/ppermute | solution.py:85
  35.6 1.4 %collective-permute-start.16 = (bf16[144,256]{1,0:T(8,128)(2,1)S(1)}, bf16[144,256]{1,0:T(8,128)(2,1)S(1)}, u32[]{:S(2)}, u32[]{:S(2)}) collective-permute-start(bf16[144,256]{1,0:T(8,128)(2,1)S(1)} %add_convert_fusion.1), channel_id=1, source_target_pairs={{0,3},{1,2},{2,1},{3,0},{4,7},{5,6},{6,5},{7,4},{8,11},{9,10},{10,... | collective-permute-start | bytes 221192 | tf_op jit(solution)/shard_map/ppermute | solution.py:85
  37.0 1.9 %collective-permute-start.15 = (bf16[144,256]{1,0:T(8,128)(2,1)S(1)}, bf16[144,256]{1,0:T(8,128)(2,1)S(1)}, u32[]{:S(2)}, u32[]{:S(2)}) collective-permute-start(bf16[144,256]{1,0:T(8,128)(2,1)S(1)} %add_convert_fusion.1), channel_id=1, source_target_pairs={{0,2},{1,3},{2,0},{3,1},{4,6},{5,7},{6,4},{7,5},{8,10},{9,11},{10,... | collective-permute-start | bytes 221192 | tf_op jit(solution)/shard_map/ppermute | solution.py:85
  38.9 1.1 %collective-permute-start.14 = (bf16[144,256]{1,0:T(8,128)(2,1)S(1)}, bf16[144,256]{1,0:T(8,128)(2,1)S(1)}, u32[]{:S(2)}, u32[]{:S(2)}) collective-permute-start(bf16[144,256]{1,0:T(8,128)(2,1)S(1)} %add_convert_fusion.1), channel_id=1, source_target_pairs={{0,1},{1,0},{2,3},{3,2},{4,5},{5,4},{6,7},{7,6},{8,9},{9,8},{10,11... | collective-permute-start | bytes 221192 | tf_op jit(solution)/shard_map/ppermute | solution.py:85
  40.1 3.9 %collective-permute-done.8.refs_3_ = bf16[256,256]{1,0:T(8,128)(2,1)S(1)} collective-permute-done((bf16[256,256]{1,0:T(8,128)(2,1)S(1)}, bf16[256,256]{1,0:T(8,128)(2,1)S(1)}, u32[]{:S(2)}, u32[]{:S(2)}) %collective-permute-start.8) | collective-permute-done | bytes 131104 | tf_op jit(solution)/shard_map/ppermute | solution.py:85
  44.0 0.8 %backward.1 = (f32[256,256]{1,0:T(8,128)S(1)}, f32[256,256]{1,0:T(8,128)S(1)}, bf16[2,256,256]{2,1,0:T(8,128)(2,1)S(1)}) custom-call(bf16[4,1024,256]{2,1,0:T(8,128)(2,1)S(1)} %build_dense.1.dense_ref, bf16[256,256]{1,0:T(8,128)(2,1)S(1)} %get-tuple-element.28.after_ref.refs_0_, bf16[256,256]{1,0:T(8,128)(2,1)S(1)} %collective-permute-done.6.refs_1_, ...), custom_call_target="tpu_custom_call" | custom-call | flops 536870912 | bytes 3145728 | tf_op jit(solution)/shard_map/backward/pallas_call | solution.py:214
  44.9 0.6 %collective-permute-done.15 = bf16[144,256]{1,0:T(8,128)(2,1)S(1)} collective-permute-done((bf16[144,256]{1,0:T(8,128)(2,1)S(1)}, bf16[144,256]{1,0:T(8,128)(2,1)S(1)}, u32[]{:S(2)}, u32[]{:S(2)}) %collective-permute-start.15) | collective-permute-done | bytes 73760 | tf_op jit(solution)/shard_map/ppermute | solution.py:85
  46.4 0.6 %collective-permute-start.10 = (bf16[256,256]{1,0:T(8,128)(2,1)S(1)}, bf16[256,256]{1,0:T(8,128)(2,1)S(1)}, u32[]{:S(2)}, u32[]{:S(2)}) collective-permute-start(bf16[256,256]{1,0:T(8,128)(2,1)S(1)} %get-tuple-element.37), channel_id=1, source_target_pairs={{0,8},{4,12},{8,0},{12,4},{1,9},{5,13},{9,1},{13,5},{2,10},{6,14},... | collective-permute-start | bytes 393224 | tf_op jit(solution)/shard_map/ppermute | solution.py:85
  47.1 0.7 %maximum_multiply_fusion = f32[256,256]{1,0:T(8,128)} fusion(f32[128,256]{1,0:T(8,128)S(1)} %get-tuple-element.41, f32[128,256]{1,0:T(8,128)S(1)} %get-tuple-element.40), kind=kLoop, calls=%fused_computation | loop fusion | flops 131072 | bytes 524288 | tf_op jit(solution)/shard_map/mul | solution.py:365
  47.8 4.5 %collective-permute-done.10 = bf16[256,256]{1,0:T(8,128)(2,1)S(1)} collective-permute-done((bf16[256,256]{1,0:T(8,128)(2,1)S(1)}, bf16[256,256]{1,0:T(8,128)(2,1)S(1)}, u32[]{:S(2)}, u32[]{:S(2)}) %collective-permute-start.10) | collective-permute-done | bytes 131104 | tf_op jit(solution)/shard_map/ppermute | solution.py:85
  52.3 0.7 %fusion = bf16[1,1,256,256]{3,2,1,0:T(8,128)(2,1)} fusion(f32[256,256]{1,0:T(8,128)S(1)} %get-tuple-element.36, bf16[256,256]{1,0:T(8,128)(2,1)S(1)} %collective-permute-done.10), kind=kLoop, calls=%fused_computation.4 | loop fusion | flops 196608 | bytes 524288 | tf_op jit(solution)/shard_map/broadcast_in_dim | solution.py:366
  (34 shorter events, 2.7 us)
Async XLA Ops:
  0.6 8.9 %copy-start = (bf16[1,1,256,256]{3,2,1,0:T(8,128)(2,1)S(1)}, bf16[1,1,256,256]{3,2,1,0:T(8,128)(2,1)}, u32[]{:S(2)}) copy-start(bf16[1,1,256,256]{3,2,1,0:T(8,128)(2,1)} %param.8) | copy-start | bytes 393220
  0.6 6.9 %collective-permute-start = (bf16[256,256]{1,0:T(8,128)(2,1)}, bf16[256,256]{1,0:T(8,128)(2,1)S(1)}, u32[]{:S(2)}, u32[]{:S(2)}) collective-permute-start(bf16[256,256]{1,0:T(8,128)(2,1)} %bitcast.12), channel_id=1, source_target_pairs={{0,8},{4,12},{8,0},{12,4},{1,9},{5,13},{9,1},{13,5},{2,10},{6,14},... | collective-permute-start | bytes 393224 | tf_op jit(solution)/shard_map/ppermute | solution.py:85
  3.6 4.9 %collective-permute-start.1 = (bf16[256,256]{1,0:T(8,128)(2,1)}, bf16[256,256]{1,0:T(8,128)(2,1)S(1)}, u32[]{:S(2)}, u32[]{:S(2)}) collective-permute-start(bf16[256,256]{1,0:T(8,128)(2,1)} %bitcast.13), channel_id=1, source_target_pairs={{0,4},{4,0},{8,12},{12,8},{1,5},{5,1},{9,13},{13,9},{2,6},{6,2},{1... | collective-permute-start | bytes 393224 | tf_op jit(solution)/shard_map/ppermute | solution.py:85
  5.0 19.2 %copy-start.1 = (bf16[256,256]{1,0:T(8,128)(2,1)S(1)}, bf16[256,256]{1,0:T(8,128)(2,1)}, u32[]{:S(2)}) copy-start(bf16[256,256]{1,0:T(8,128)(2,1)} %weight_ref.1) | copy-start | bytes 393220
  5.0 19.2 %copy-start.2 = (bf16[1,1,256,256]{3,2,1,0:T(8,128)(2,1)S(1)}, bf16[1,1,256,256]{3,2,1,0:T(8,128)(2,1)}, u32[]{:S(2)}) copy-start(bf16[1,1,256,256]{3,2,1,0:T(8,128)(2,1)} %param.15) | copy-start | bytes 393220
  5.0 19.2 %copy-start.3 = (f32[256]{0:T(256)S(1)}, f32[256]{0:T(256)}, u32[]{:S(2)}) copy-start(f32[256]{0:T(256)} %param.10) | copy-start | bytes 3076
  7.6 2.0 %collective-permute-start.2 = (bf16[256,256]{1,0:T(8,128)(2,1)S(1)}, bf16[256,256]{1,0:T(8,128)(2,1)S(1)}, u32[]{:S(2)}, u32[]{:S(2)}) collective-permute-start(bf16[256,256]{1,0:T(8,128)(2,1)S(1)} %collective-permute-done.refs_2_), channel_id=1, source_target_pairs={{0,4},{4,0},{8,12},{12,8},{1,5},{5,1},{9,13},{13,9},{2,6},{6,2},{1... | collective-permute-start | bytes 393224 | tf_op jit(solution)/shard_map/ppermute | solution.py:85
  10.3 12.9 %collective-permute-start.3 = (bf16[256,256]{1,0:T(8,128)(2,1)S(1)}, bf16[256,256]{1,0:T(8,128)(2,1)S(1)}, u32[]{:S(2)}, u32[]{:S(2)}) collective-permute-start(bf16[256,256]{1,0:T(8,128)(2,1)S(1)} %get-tuple-element.25), channel_id=1, source_target_pairs={{0,2},{1,3},{2,0},{3,1},{4,6},{5,7},{6,4},{7,5},{8,10},{9,11},{10,... | collective-permute-start | bytes 393224 | tf_op jit(solution)/shard_map/ppermute | solution.py:85
  13.1 10.1 %collective-permute-start.4 = (bf16[256,256]{1,0:T(8,128)(2,1)S(1)}, bf16[256,256]{1,0:T(8,128)(2,1)S(1)}, u32[]{:S(2)}, u32[]{:S(2)}) collective-permute-start(bf16[256,256]{1,0:T(8,128)(2,1)S(1)} %get-tuple-element.26), channel_id=1, source_target_pairs={{0,3},{1,2},{2,1},{3,0},{4,7},{5,6},{6,5},{7,4},{8,11},{9,10},{10,... | collective-permute-start | bytes 393224 | tf_op jit(solution)/shard_map/ppermute | solution.py:85
  14.1 10.1 %collective-permute-start.5 = (bf16[256,256]{1,0:T(8,128)(2,1)S(1)}, bf16[256,256]{1,0:T(8,128)(2,1)S(1)}, u32[]{:S(2)}, u32[]{:S(2)}) collective-permute-start(bf16[256,256]{1,0:T(8,128)(2,1)S(1)} %get-tuple-element.27), channel_id=1, source_target_pairs={{0,1},{1,0},{2,3},{3,2},{4,5},{5,4},{6,7},{7,6},{8,9},{9,8},{10,11... | collective-permute-start | bytes 393224 | tf_op jit(solution)/shard_map/ppermute | solution.py:85
  24.6 10.8 %collective-permute-start.7 = (bf16[256,256]{1,0:T(8,128)(2,1)S(1)}, bf16[256,256]{1,0:T(8,128)(2,1)S(1)}, u32[]{:S(2)}, u32[]{:S(2)}) collective-permute-start(bf16[256,256]{1,0:T(8,128)(2,1)S(1)} %get-tuple-element.28.after_ref.refs_0_), channel_id=1, source_target_pairs={{0,2},{1,3},{2,0},{3,1},{4,6},{5,7},{6,4},{7,5},{8,10},{9,11},{10,... | collective-permute-start | bytes 393224 | tf_op jit(solution)/shard_map/ppermute | solution.py:85
  29.5 5.8 %collective-permute-start.13 = (bf16[144,256]{1,0:T(8,128)(2,1)S(1)}, bf16[144,256]{1,0:T(8,128)(2,1)S(1)}, u32[]{:S(2)}, u32[]{:S(2)}) collective-permute-start(bf16[144,256]{1,0:T(8,128)(2,1)S(1)} %get-tuple-element.39), channel_id=1, source_target_pairs={{0,12},{4,8},{8,4},{12,0},{1,13},{5,9},{9,5},{13,1},{2,14},{6,10},... | collective-permute-start | bytes 221192 | tf_op jit(solution)/shard_map/ppermute | solution.py:85
  29.5 6.1 %collective-permute-start.12 = (bf16[144,256]{1,0:T(8,128)(2,1)S(1)}, bf16[144,256]{1,0:T(8,128)(2,1)S(1)}, u32[]{:S(2)}, u32[]{:S(2)}) collective-permute-start(bf16[144,256]{1,0:T(8,128)(2,1)S(1)} %get-tuple-element.38), channel_id=1, source_target_pairs={{0,8},{4,12},{8,0},{12,4},{1,9},{5,13},{9,1},{13,5},{2,10},{6,14},... | collective-permute-start | bytes 221192 | tf_op jit(solution)/shard_map/ppermute | solution.py:85
  30.9 4.7 %collective-permute-start.11 = (bf16[144,256]{1,0:T(8,128)(2,1)S(1)}, bf16[144,256]{1,0:T(8,128)(2,1)S(1)}, u32[]{:S(2)}, u32[]{:S(2)}) collective-permute-start(bf16[144,256]{1,0:T(8,128)(2,1)S(1)} %get-tuple-element.39), channel_id=1, source_target_pairs={{0,4},{4,0},{8,12},{12,8},{1,5},{5,1},{9,13},{13,9},{2,6},{6,2},{1... | collective-permute-start | bytes 221192 | tf_op jit(solution)/shard_map/ppermute | solution.py:85
  31.4 8.7 %collective-permute-start.6 = (bf16[256,256]{1,0:T(8,128)(2,1)S(1)}, bf16[256,256]{1,0:T(8,128)(2,1)S(1)}, u32[]{:S(2)}, u32[]{:S(2)}) collective-permute-start(bf16[256,256]{1,0:T(8,128)(2,1)S(1)} %get-tuple-element.28.after_ref.refs_0_), channel_id=1, source_target_pairs={{0,1},{1,0},{2,3},{3,2},{4,5},{5,4},{6,7},{7,6},{8,9},{9,8},{10,11... | collective-permute-start | bytes 393224 | tf_op jit(solution)/shard_map/ppermute | solution.py:85
  35.3 8.7 %collective-permute-start.8 = (bf16[256,256]{1,0:T(8,128)(2,1)S(1)}, bf16[256,256]{1,0:T(8,128)(2,1)S(1)}, u32[]{:S(2)}, u32[]{:S(2)}) collective-permute-start(bf16[256,256]{1,0:T(8,128)(2,1)S(1)} %collective-permute-done.7.refs_2_), channel_id=1, source_target_pairs={{0,1},{1,0},{2,3},{3,2},{4,5},{5,4},{6,7},{7,6},{8,9},{9,8},{10,11... | collective-permute-start | bytes 393224 | tf_op jit(solution)/shard_map/ppermute | solution.py:85
  35.6 9.2 %collective-permute-start.16 = (bf16[144,256]{1,0:T(8,128)(2,1)S(1)}, bf16[144,256]{1,0:T(8,128)(2,1)S(1)}, u32[]{:S(2)}, u32[]{:S(2)}) collective-permute-start(bf16[144,256]{1,0:T(8,128)(2,1)S(1)} %add_convert_fusion.1), channel_id=1, source_target_pairs={{0,3},{1,2},{2,1},{3,0},{4,7},{5,6},{6,5},{7,4},{8,11},{9,10},{10,... | collective-permute-start | bytes 221192 | tf_op jit(solution)/shard_map/ppermute | solution.py:85
  37.0 8.4 %collective-permute-start.15 = (bf16[144,256]{1,0:T(8,128)(2,1)S(1)}, bf16[144,256]{1,0:T(8,128)(2,1)S(1)}, u32[]{:S(2)}, u32[]{:S(2)}) collective-permute-start(bf16[144,256]{1,0:T(8,128)(2,1)S(1)} %add_convert_fusion.1), channel_id=1, source_target_pairs={{0,2},{1,3},{2,0},{3,1},{4,6},{5,7},{6,4},{7,5},{8,10},{9,11},{10,... | collective-permute-start | bytes 221192 | tf_op jit(solution)/shard_map/ppermute | solution.py:85
  38.9 6.6 %collective-permute-start.14 = (bf16[144,256]{1,0:T(8,128)(2,1)S(1)}, bf16[144,256]{1,0:T(8,128)(2,1)S(1)}, u32[]{:S(2)}, u32[]{:S(2)}) collective-permute-start(bf16[144,256]{1,0:T(8,128)(2,1)S(1)} %add_convert_fusion.1), channel_id=1, source_target_pairs={{0,1},{1,0},{2,3},{3,2},{4,5},{5,4},{6,7},{7,6},{8,9},{9,8},{10,11... | collective-permute-start | bytes 221192 | tf_op jit(solution)/shard_map/ppermute | solution.py:85
  44.8 1.6 %collective-permute-start.9 = (bf16[2,256,256]{2,1,0:T(8,128)(2,1)S(1)}, bf16[2,256,256]{2,1,0:T(8,128)(2,1)S(1)}, u32[]{:S(2)}, u32[]{:S(2)}) collective-permute-start(bf16[2,256,256]{2,1,0:T(8,128)(2,1)S(1)} %get-tuple-element.35), channel_id=1, source_target_pairs={{0,4},{4,0},{8,12},{12,8},{1,5},{5,1},{9,13},{13,9},{2,6},{6,2},{1... | collective-permute-start | bytes 786440 | tf_op jit(solution)/shard_map/ppermute | solution.py:85
  45.6 1.4 %collective-permute-start.17 = (f32[144,256]{1,0:T(8,128)S(1)}, f32[144,256]{1,0:T(8,128)S(1)}, u32[]{:S(2)}, u32[]{:S(2)}) collective-permute-start(f32[144,256]{1,0:T(8,128)S(1)} %add_add_fusion), channel_id=1, source_target_pairs={{0,4},{4,0},{8,12},{12,8},{1,5},{5,1},{9,13},{13,9},{2,6},{6,2},{1... | collective-permute-start | bytes 442376 | tf_op jit(solution)/shard_map/ppermute | solution.py:85
  46.4 5.9 %collective-permute-start.10 = (bf16[256,256]{1,0:T(8,128)(2,1)S(1)}, bf16[256,256]{1,0:T(8,128)(2,1)S(1)}, u32[]{:S(2)}, u32[]{:S(2)}) collective-permute-start(bf16[256,256]{1,0:T(8,128)(2,1)S(1)} %get-tuple-element.37), channel_id=1, source_target_pairs={{0,8},{4,12},{8,0},{12,4},{1,9},{5,13},{9,1},{13,5},{2,10},{6,14},... | collective-permute-start | bytes 393224 | tf_op jit(solution)/shard_map/ppermute | solution.py:85

commit v3 on v2

--- a/solution.py
+++ b/solution.py
@@ -324,6 +324,33 @@
     )(after, *summed, *pre, *grad_pre)
 
 
+def finish_kernel(scale, keep_ref, other_ref, half_ref, twin_ref, grad_ref, weight_ref, bias_ref):
+    grad_ref[...] = (keep_ref[...] + other_ref[...].astype(F32)).astype(BF)
+    part = weight_ref.shape[0] // 2
+    core = lax.axis_index("row") & 1
+    for k, share in enumerate((half_ref, twin_ref)):
+        window = pl.ds(pl.multiple_of((core ^ k) * part, part), part)
+        weight_ref[window, :] = share[:part, :] * scale
+    bias_ref[...] = half_ref[part : part + 1, :] * scale
+
+
+def finish(scale, keep, other, half, twin):
+    feat = keep.shape[1]
+    return pl.pallas_call(
+        functools.partial(finish_kernel, scale),
+        in_specs=[VMEM] * 4,
+        out_specs=[VMEM] * 3,
+        out_shape=[
+            jax.ShapeDtypeStruct(keep.shape, BF),
+            jax.ShapeDtypeStruct((feat, feat), F32),
+            jax.ShapeDtypeStruct((1, feat), F32),
+        ],
+        compiler_params=pltpu.CompilerParams(vmem_limit_bytes=8 << 20),
+        cost_estimate=pl.CostEstimate(flops=feat * feat, bytes_accessed=6 * feat * feat, transcendentals=0),
+        name="finish",
+    )(keep, other, half, twin)
+
+
 def dense_device(features, weight, bias, tile_rows, tile_cols, tile_vals, tile_count, cotangent):
     own = features[0, 0]
     rows, feat = own.shape
@@ -339,13 +366,14 @@
     kept, gathered, after = [], [], []
     for h in range(PIECES):
         mine = partial[h * 4 : (h + 1) * 4]
-        terms = [mine[0]] + [swap(mine[k], "col", k) for k in (2, 3, 1)]
+        terms = [mine[0]] + [swap(mine[k], "col", k) for k in (3, 1, 2)]
         agg, *rest = gradient(weight, bias[None, :], cotangent[0, 0], terms, after, h)
         kept.append(rest)
         after = [agg]
         early = swap(agg, "col", 1)
         grads = {0: agg, 1: early}
         grads[2] = swap(agg, "col", 2)
+        grads[1], grads[2] = lax.optimization_barrier((grads[1], grads[2]))
         grads[3] = swap(grads[2], "col", 1)
         gathered += [grads[k] for k in range(4)]
 
@@ -354,16 +382,13 @@
 
     keep, send, pair = backward(dense, gathered)
     keep, send = pair_sum(keep, send, swap(pair, "row", 1))
-    grad_features = (keep + swap(send, "row", 2).astype(F32)).astype(BF)
 
     half = tree(half, *(swap(half, "col", k) for k in (1, 2, 3)))
     twin = swap(half, "row", 1)
-    first = row % 2 == 0
-    middle = feat // 2
-    factor = float(rows * 16) ** (-0.5)
-    low, high = jnp.where(first, half, twin), jnp.where(first, twin, half)
-    grad_weight = jnp.concatenate([low[:middle], high[:middle]], axis=0) * factor
-    return (hidden[None, None], grad_features[None, None], grad_weight, half[middle] * factor)
+    grad_features, grad_weight, grad_bias = finish(
+        float(rows * 16) ** (-0.5), keep, swap(send, "row", 2), half, twin
+    )
+    return (hidden[None, None], grad_features[None, None], grad_weight, grad_bias[0])
 
 
 def per_device(features, weight, bias, tile_rows, tile_cols, tile_vals, tile_count, cotangent):

time: 52.8 us -> 52 us (0.985)
  other arithmetic: 2.75 us -> 0.75 us
  Pallas kernels: 5.24 us -> 6.03 us
    mul x2 -> x0, other arithmetic: 1.29 us -> none  [the longest x1 0.72 us: dense_device(): jnp.concatenate([low[:middle], high[:middle]], axis=0) * factor]
    pallas_call x0 -> x1, Pallas kernels: none -> 0.79 us  [finish(): pl.pallas_call(functools.partial(finish_kernel, scale), in_specs=[VMEM] *...]
    broadcast_in_dim x1 -> x0, other arithmetic: 0.69 us -> none  [dense_device(): grad_features[None, None]]
  transfers between devices with their start and end apart: 18 -> 18, of which waited for: 11 -> 11; matrix products, arithmetic and copies ran while one was open for 4% -> 1% of each run, Pallas kernels for 8% -> 8%
where the time goes in v3:
time: 52 us; the launch traced here: 51.8 us
  waiting for transfers between devices  24.1 us (46%)
  starting transfers between devices  19.6 us (38%)
  Pallas kernels  6.03 us (12%)
  between operations  1.38 us (3%)
  other arithmetic  0.75 us (1%)
    ppermute x18, waiting for transfers between devices, swap(): return lax.ppermute(x, axis, [(i, i ^ bit) for i in range(size)])  24.1 us
    ppermute x18, starting transfers between devices, swap(): return lax.ppermute(x, axis, [(i, i ^ bit) for i in range(size)])  19.6 us
    pallas_call x1, Pallas kernels, build_dense(): pl.pallas_call(build_kernel, in_specs=[HBM] * 2, out_specs=VMEM, out_shap...  2.54 us
  transfers between devices with their start and end apart: 18, of which 11 were waited for; matrix products, arithmetic and copies ran while one was open for 1% of the time, Pallas kernels for 8%

profile of v3, /device:TPU:0, one launch (start us, length us, event | category | flops | bytes accessed | tf_op | source)
XLA Modules:
  0.0 51.8 jit_solution(4627504914370677642)
XLA Ops:
  1.2 2.6 %collective-permute-start = (bf16[256,256]{1,0:T(8,128)(2,1)}, bf16[256,256]{1,0:T(8,128)(2,1)S(1)}, u32[]{:S(2)}, u32[]{:S(2)}) collective-permute-start(bf16[256,256]{1,0:T(8,128)(2,1)} %bitcast.12), channel_id=1, source_target_pairs={{0,8},{4,12},{8,0},{12,4},{1,9},{5,13},{9,1},{13,5},{2,10},{6,14},... | collective-permute-start | bytes 393224 | tf_op jit(solution)/shard_map/ppermute | solution.py:85
  4.4 0.7 %add_bitcast_fusion = s32[128]{0:T(128)S(1)} fusion(s32[1,1,128]{2,1,0:T(1,128)} %param.12, s32[1,1,128]{2,1,0:T(1,128)} %param.11), kind=kLoop, calls=%fused_computation.2 | loop fusion | flops 256 | bytes 1536 | tf_op jit(solution)/shard_map/add | solution.py:132
  5.1 2.5 %build_dense.1.dense_ref = bf16[4,1024,256]{2,1,0:T(8,128)(2,1)S(1)} custom-call(s32[256]{0:T(256)S(1)} %concatenate.3.slots_hbm, bf16[128,128,128]{2,1,0:T(8,128)(2,1)} %bitcast.16), custom_call_target="tpu_custom_call" | custom-call | flops 8388608 | bytes 6291456 | tf_op jit(solution)/shard_map/build_dense/pallas_call | solution.py:133
  8.5 1.0 %collective-permute-done.2.refs_3_ = bf16[256,256]{1,0:T(8,128)(2,1)S(1)} collective-permute-done((bf16[256,256]{1,0:T(8,128)(2,1)S(1)}, bf16[256,256]{1,0:T(8,128)(2,1)S(1)}, u32[]{:S(2)}, u32[]{:S(2)}) %collective-permute-start.2) | collective-permute-done | bytes 131104 | tf_op jit(solution)/shard_map/ppermute | solution.py:85
  9.5 0.7 %forward.1 = (bf16[256,256]{1,0:T(8,128)(2,1)S(1)}, bf16[256,256]{1,0:T(8,128)(2,1)S(1)}, bf16[256,256]{1,0:T(8,128)(2,1)S(1)}, bf16[256,256]{1,0:T(8,128)(2,1)S(1)}) custom-call(bf16[4,1024,256]{2,1,0:T(8,128)(2,1)S(1)} %build_dense.1.dense_ref, bf16[256,256]{1,0:T(8,128)(2,1)S(1)} %bitcast.13, bf16[256,256]{1,0:T(8,128)(2,1)S(1)} %collective-permute-done.1.refs_1_, ...), custom_call_target="tpu_custom_call" | custom-call | flops 536870912 | bytes 3145728 | tf_op jit(solution)/shard_map/forward/pallas_call | solution.py:170
  10.2 3.8 %collective-permute-start.3 = (bf16[256,256]{1,0:T(8,128)(2,1)S(1)}, bf16[256,256]{1,0:T(8,128)(2,1)S(1)}, u32[]{:S(2)}, u32[]{:S(2)}) collective-permute-start(bf16[256,256]{1,0:T(8,128)(2,1)S(1)} %get-tuple-element.30), channel_id=1, source_target_pairs={{0,3},{1,2},{2,1},{3,0},{4,7},{5,6},{6,5},{7,4},{8,11},{9,10},{10,... | collective-permute-start | bytes 393224 | tf_op jit(solution)/shard_map/ppermute | solution.py:85
  14.7 3.7 %collective-permute-done.3.refs_1_ = bf16[256,256]{1,0:T(8,128)(2,1)S(1)} collective-permute-done((bf16[256,256]{1,0:T(8,128)(2,1)S(1)}, bf16[256,256]{1,0:T(8,128)(2,1)S(1)}, u32[]{:S(2)}, u32[]{:S(2)}) %collective-permute-start.3) | collective-permute-done | bytes 131104 | tf_op jit(solution)/shard_map/ppermute | solution.py:85
  18.4 3.3 %collective-permute-done.4.refs_2_ = bf16[256,256]{1,0:T(8,128)(2,1)S(1)} collective-permute-done((bf16[256,256]{1,0:T(8,128)(2,1)S(1)}, bf16[256,256]{1,0:T(8,128)(2,1)S(1)}, u32[]{:S(2)}, u32[]{:S(2)}) %collective-permute-start.4) | collective-permute-done | bytes 131104 | tf_op jit(solution)/shard_map/ppermute | solution.py:85
  21.7 3.7 %collective-permute-done.5.refs_3_ = bf16[256,256]{1,0:T(8,128)(2,1)S(1)} collective-permute-done((bf16[256,256]{1,0:T(8,128)(2,1)S(1)}, bf16[256,256]{1,0:T(8,128)(2,1)S(1)}, u32[]{:S(2)}, u32[]{:S(2)}) %collective-permute-start.5) | collective-permute-done | bytes 131104 | tf_op jit(solution)/shard_map/ppermute | solution.py:85
  25.8 0.9 %collective-permute-start.7 = (bf16[256,256]{1,0:T(8,128)(2,1)S(1)}, bf16[256,256]{1,0:T(8,128)(2,1)S(1)}, u32[]{:S(2)}, u32[]{:S(2)}) collective-permute-start(bf16[256,256]{1,0:T(8,128)(2,1)S(1)} %get-tuple-element.33.after_ref.refs_0_), channel_id=1, source_target_pairs={{0,2},{1,3},{2,0},{3,1},{4,6},{5,7},{6,4},{7,5},{8,10},{9,11},{10,... | collective-permute-start | bytes 393224 | tf_op jit(solution)/shard_map/ppermute | solution.py:85
  26.7 2.2 %collective-permute-start.6 = (bf16[256,256]{1,0:T(8,128)(2,1)S(1)}, bf16[256,256]{1,0:T(8,128)(2,1)S(1)}, u32[]{:S(2)}, u32[]{:S(2)}) collective-permute-start(bf16[256,256]{1,0:T(8,128)(2,1)S(1)} %get-tuple-element.33.after_ref.refs_0_), channel_id=1, source_target_pairs={{0,1},{1,0},{2,3},{3,2},{4,5},{5,4},{6,7},{7,6},{8,9},{9,8},{10,11... | collective-permute-start | bytes 393224 | tf_op jit(solution)/shard_map/ppermute | solution.py:85
  28.9 0.8 %totals.1 = (bf16[256,256]{1,0:T(8,128)(2,1)}, bf16[144,256]{1,0:T(8,128)(2,1)S(1)}, bf16[144,256]{1,0:T(8,128)(2,1)S(1)}) custom-call(bf16[256,256]{1,0:T(8,128)(2,1)S(1)} %get-tuple-element.33.after_ref.refs_0_, bf16[256,256]{1,0:T(8,128)(2,1)S(1)} %get-tuple-element.34.refs_0_, f32[256,256]{1,0:T(8,128)S(1)} %get-tuple-element.35.refs_1_, ...), custom_call_target="tpu_custom_call" | custom-call | flops 33554432 | bytes 1310720 | tf_op jit(solution)/shard_map/totals/pallas_call | solution.py:310
  29.7 1.5 %collective-permute-start.12 = (bf16[144,256]{1,0:T(8,128)(2,1)S(1)}, bf16[144,256]{1,0:T(8,128)(2,1)S(1)}, u32[]{:S(2)}, u32[]{:S(2)}) collective-permute-start(bf16[144,256]{1,0:T(8,128)(2,1)S(1)} %get-tuple-element.45), channel_id=1, source_target_pairs={{0,8},{4,12},{8,0},{12,4},{1,9},{5,13},{9,1},{13,5},{2,10},{6,14},... | collective-permute-start | bytes 221192 | tf_op jit(solution)/shard_map/ppermute | solution.py:85
  31.9 1.1 %collective-permute-done.7.refs_2_ = bf16[256,256]{1,0:T(8,128)(2,1)S(1)} collective-permute-done((bf16[256,256]{1,0:T(8,128)(2,1)S(1)}, bf16[256,256]{1,0:T(8,128)(2,1)S(1)}, u32[]{:S(2)}, u32[]{:S(2)}) %collective-permute-start.7) | collective-permute-done | bytes 131104 | tf_op jit(solution)/shard_map/ppermute | solution.py:85
  33.0 0.9 %collective-permute-done.6.refs_1_ = bf16[256,256]{1,0:T(8,128)(2,1)S(1)} collective-permute-done((bf16[256,256]{1,0:T(8,128)(2,1)S(1)}, bf16[256,256]{1,0:T(8,128)(2,1)S(1)}, u32[]{:S(2)}, u32[]{:S(2)}) %collective-permute-start.6) | collective-permute-done | bytes 131104 | tf_op jit(solution)/shard_map/ppermute | solution.py:85
  34.2 1.4 %collective-permute-done.13 = bf16[144,256]{1,0:T(8,128)(2,1)S(1)} collective-permute-done((bf16[144,256]{1,0:T(8,128)(2,1)S(1)}, bf16[144,256]{1,0:T(8,128)(2,1)S(1)}, u32[]{:S(2)}, u32[]{:S(2)}) %collective-permute-start.13) | collective-permute-done | bytes 73760 | tf_op jit(solution)/shard_map/ppermute | solution.py:85
  35.7 1.4 %collective-permute-start.16 = (bf16[144,256]{1,0:T(8,128)(2,1)S(1)}, bf16[144,256]{1,0:T(8,128)(2,1)S(1)}, u32[]{:S(2)}, u32[]{:S(2)}) collective-permute-start(bf16[144,256]{1,0:T(8,128)(2,1)S(1)} %add_convert_fusion), channel_id=1, source_target_pairs={{0,3},{1,2},{2,1},{3,0},{4,7},{5,6},{6,5},{7,4},{8,11},{9,10},{10,... | collective-permute-start | bytes 221192 | tf_op jit(solution)/shard_map/ppermute | solution.py:85
  37.5 2.7 %collective-permute-start.14 = (bf16[144,256]{1,0:T(8,128)(2,1)S(1)}, bf16[144,256]{1,0:T(8,128)(2,1)S(1)}, u32[]{:S(2)}, u32[]{:S(2)}) collective-permute-start(bf16[144,256]{1,0:T(8,128)(2,1)S(1)} %add_convert_fusion), channel_id=1, source_target_pairs={{0,1},{1,0},{2,3},{3,2},{4,5},{5,4},{6,7},{7,6},{8,9},{9,8},{10,11... | collective-permute-start | bytes 221192 | tf_op jit(solution)/shard_map/ppermute | solution.py:85
  40.2 0.8 %backward.1 = (f32[256,256]{1,0:T(8,128)S(1)}, f32[256,256]{1,0:T(8,128)S(1)}, bf16[2,256,256]{2,1,0:T(8,128)(2,1)S(1)}) custom-call(bf16[4,1024,256]{2,1,0:T(8,128)(2,1)S(1)} %build_dense.1.dense_ref, bf16[256,256]{1,0:T(8,128)(2,1)S(1)} %get-tuple-element.33.after_ref.refs_0_, bf16[256,256]{1,0:T(8,128)(2,1)S(1)} %collective-permute-done.6.refs_1_, ...), custom_call_target="tpu_custom_call" | custom-call | flops 536870912 | bytes 3145728 | tf_op jit(solution)/shard_map/backward/pallas_call | solution.py:214
  41.0 1.8 %collective-permute-done.16 = bf16[144,256]{1,0:T(8,128)(2,1)S(1)} collective-permute-done((bf16[144,256]{1,0:T(8,128)(2,1)S(1)}, bf16[144,256]{1,0:T(8,128)(2,1)S(1)}, u32[]{:S(2)}, u32[]{:S(2)}) %collective-permute-start.16) | collective-permute-done | bytes 73760 | tf_op jit(solution)/shard_map/ppermute | solution.py:85
  42.8 2.1 %collective-permute-done.15 = bf16[144,256]{1,0:T(8,128)(2,1)S(1)} collective-permute-done((bf16[144,256]{1,0:T(8,128)(2,1)S(1)}, bf16[144,256]{1,0:T(8,128)(2,1)S(1)}, u32[]{:S(2)}, u32[]{:S(2)}) %collective-permute-start.15) | collective-permute-done | bytes 73760 | tf_op jit(solution)/shard_map/ppermute | solution.py:85
  45.1 1.4 %collective-permute-start.10 = (bf16[256,256]{1,0:T(8,128)(2,1)S(1)}, bf16[256,256]{1,0:T(8,128)(2,1)S(1)}, u32[]{:S(2)}, u32[]{:S(2)}) collective-permute-start(bf16[256,256]{1,0:T(8,128)(2,1)S(1)} %get-tuple-element.44), channel_id=1, source_target_pairs={{0,8},{4,12},{8,0},{12,4},{1,9},{5,13},{9,1},{13,5},{2,10},{6,14},... | collective-permute-start | bytes 393224 | tf_op jit(solution)/shard_map/ppermute | solution.py:85
  46.5 4.6 %collective-permute-done.10.other_ref = bf16[256,256]{1,0:T(8,128)(2,1)S(1)} collective-permute-done((bf16[256,256]{1,0:T(8,128)(2,1)S(1)}, bf16[256,256]{1,0:T(8,128)(2,1)S(1)}, u32[]{:S(2)}, u32[]{:S(2)}) %collective-permute-start.10) | collective-permute-done | bytes 131104 | tf_op jit(solution)/shard_map/ppermute | solution.py:85
  51.0 0.8 %finish.1 = (bf16[256,256]{1,0:T(8,128)(2,1)}, f32[256,256]{1,0:T(8,128)}, f32[1,256]{1,0:T(1,128)}) custom-call(f32[256,256]{1,0:T(8,128)S(1)} %get-tuple-element.43.keep_ref, bf16[256,256]{1,0:T(8,128)(2,1)S(1)} %collective-permute-done.10.other_ref, f32[144,256]{1,0:T(8,128)S(1)} %add_add_fusion.half_ref, f32[144,256]{1,0:T(8,128)S(1)} %collective-permute-done.17.twin_ref), custom_call_target="tpu_custom_call" | custom-call | flops 65536 | bytes 393216 | tf_op jit(solution)/shard_map/finish/pallas_call | solution.py:339
  (31 shorter events, 4.1 us)
Async XLA Ops:
  0.6 8.8 %copy-start = (bf16[1,1,256,256]{3,2,1,0:T(8,128)(2,1)S(1)}, bf16[1,1,256,256]{3,2,1,0:T(8,128)(2,1)}, u32[]{:S(2)}) copy-start(bf16[1,1,256,256]{3,2,1,0:T(8,128)(2,1)} %param.8) | copy-start | bytes 393220
  0.6 7.8 %collective-permute-start.1 = (bf16[256,256]{1,0:T(8,128)(2,1)}, bf16[256,256]{1,0:T(8,128)(2,1)S(1)}, u32[]{:S(2)}, u32[]{:S(2)}) collective-permute-start(bf16[256,256]{1,0:T(8,128)(2,1)} %bitcast.11), channel_id=1, source_target_pairs={{0,4},{4,0},{8,12},{12,8},{1,5},{5,1},{9,13},{13,9},{2,6},{6,2},{1... | collective-permute-start | bytes 393224 | tf_op jit(solution)/shard_map/ppermute | solution.py:85
  1.2 6.9 %collective-permute-start = (bf16[256,256]{1,0:T(8,128)(2,1)}, bf16[256,256]{1,0:T(8,128)(2,1)S(1)}, u32[]{:S(2)}, u32[]{:S(2)}) collective-permute-start(bf16[256,256]{1,0:T(8,128)(2,1)} %bitcast.12), channel_id=1, source_target_pairs={{0,8},{4,12},{8,0},{12,4},{1,9},{5,13},{9,1},{13,5},{2,10},{6,14},... | collective-permute-start | bytes 393224 | tf_op jit(solution)/shard_map/ppermute | solution.py:85
  5.1 20.4 %copy-start.1 = (bf16[256,256]{1,0:T(8,128)(2,1)S(1)}, bf16[256,256]{1,0:T(8,128)(2,1)}, u32[]{:S(2)}) copy-start(bf16[256,256]{1,0:T(8,128)(2,1)} %weight_ref.1) | copy-start | bytes 393220
  5.1 20.4 %copy-start.2 = (bf16[1,1,256,256]{3,2,1,0:T(8,128)(2,1)S(1)}, bf16[1,1,256,256]{3,2,1,0:T(8,128)(2,1)}, u32[]{:S(2)}) copy-start(bf16[1,1,256,256]{3,2,1,0:T(8,128)(2,1)} %param.15) | copy-start | bytes 393220
  5.1 20.4 %copy-start.3 = (f32[256]{0:T(256)S(1)}, f32[256]{0:T(256)}, u32[]{:S(2)}) copy-start(f32[256]{0:T(256)} %param.10) | copy-start | bytes 3076
  8.0 1.4 %collective-permute-start.2 = (bf16[256,256]{1,0:T(8,128)(2,1)S(1)}, bf16[256,256]{1,0:T(8,128)(2,1)S(1)}, u32[]{:S(2)}, u32[]{:S(2)}) collective-permute-start(bf16[256,256]{1,0:T(8,128)(2,1)S(1)} %collective-permute-done.refs_2_), channel_id=1, source_target_pairs={{0,4},{4,0},{8,12},{12,8},{1,5},{5,1},{9,13},{13,9},{2,6},{6,2},{1... | collective-permute-start | bytes 393224 | tf_op jit(solution)/shard_map/ppermute | solution.py:85
  10.2 8.2 %collective-permute-start.3 = (bf16[256,256]{1,0:T(8,128)(2,1)S(1)}, bf16[256,256]{1,0:T(8,128)(2,1)S(1)}, u32[]{:S(2)}, u32[]{:S(2)}) collective-permute-start(bf16[256,256]{1,0:T(8,128)(2,1)S(1)} %get-tuple-element.30), channel_id=1, source_target_pairs={{0,3},{1,2},{2,1},{3,0},{4,7},{5,6},{6,5},{7,4},{8,11},{9,10},{10,... | collective-permute-start | bytes 393224 | tf_op jit(solution)/shard_map/ppermute | solution.py:85
  14.0 7.7 %collective-permute-start.4 = (bf16[256,256]{1,0:T(8,128)(2,1)S(1)}, bf16[256,256]{1,0:T(8,128)(2,1)S(1)}, u32[]{:S(2)}, u32[]{:S(2)}) collective-permute-start(bf16[256,256]{1,0:T(8,128)(2,1)S(1)} %get-tuple-element.31), channel_id=1, source_target_pairs={{0,1},{1,0},{2,3},{3,2},{4,5},{5,4},{6,7},{7,6},{8,9},{9,8},{10,11... | collective-permute-start | bytes 393224 | tf_op jit(solution)/shard_map/ppermute | solution.py:85
  14.0 11.4 %collective-permute-start.5 = (bf16[256,256]{1,0:T(8,128)(2,1)S(1)}, bf16[256,256]{1,0:T(8,128)(2,1)S(1)}, u32[]{:S(2)}, u32[]{:S(2)}) collective-permute-start(bf16[256,256]{1,0:T(8,128)(2,1)S(1)} %get-tuple-element.32), channel_id=1, source_target_pairs={{0,2},{1,3},{2,0},{3,1},{4,6},{5,7},{6,4},{7,5},{8,10},{9,11},{10,... | collective-permute-start | bytes 393224 | tf_op jit(solution)/shard_map/ppermute | solution.py:85
  25.8 7.2 %collective-permute-start.7 = (bf16[256,256]{1,0:T(8,128)(2,1)S(1)}, bf16[256,256]{1,0:T(8,128)(2,1)S(1)}, u32[]{:S(2)}, u32[]{:S(2)}) collective-permute-start(bf16[256,256]{1,0:T(8,128)(2,1)S(1)} %get-tuple-element.33.after_ref.refs_0_), channel_id=1, source_target_pairs={{0,2},{1,3},{2,0},{3,1},{4,6},{5,7},{6,4},{7,5},{8,10},{9,11},{10,... | collective-permute-start | bytes 393224 | tf_op jit(solution)/shard_map/ppermute | solution.py:85
  26.7 7.2 %collective-permute-start.6 = (bf16[256,256]{1,0:T(8,128)(2,1)S(1)}, bf16[256,256]{1,0:T(8,128)(2,1)S(1)}, u32[]{:S(2)}, u32[]{:S(2)}) collective-permute-start(bf16[256,256]{1,0:T(8,128)(2,1)S(1)} %get-tuple-element.33.after_ref.refs_0_), channel_id=1, source_target_pairs={{0,1},{1,0},{2,3},{3,2},{4,5},{5,4},{6,7},{7,6},{8,9},{9,8},{10,11... | collective-permute-start | bytes 393224 | tf_op jit(solution)/shard_map/ppermute | solution.py:85
  29.7 4.5 %collective-permute-start.12 = (bf16[144,256]{1,0:T(8,128)(2,1)S(1)}, bf16[144,256]{1,0:T(8,128)(2,1)S(1)}, u32[]{:S(2)}, u32[]{:S(2)}) collective-permute-start(bf16[144,256]{1,0:T(8,128)(2,1)S(1)} %get-tuple-element.45), channel_id=1, source_target_pairs={{0,8},{4,12},{8,0},{12,4},{1,9},{5,13},{9,1},{13,5},{2,10},{6,14},... | collective-permute-start | bytes 221192 | tf_op jit(solution)/shard_map/ppermute | solution.py:85
  31.2 4.4 %collective-permute-start.13 = (bf16[144,256]{1,0:T(8,128)(2,1)S(1)}, bf16[144,256]{1,0:T(8,128)(2,1)S(1)}, u32[]{:S(2)}, u32[]{:S(2)}) collective-permute-start(bf16[144,256]{1,0:T(8,128)(2,1)S(1)} %get-tuple-element.46), channel_id=1, source_target_pairs={{0,12},{4,8},{8,4},{12,0},{1,13},{5,9},{9,5},{13,1},{2,14},{6,10},... | collective-permute-start | bytes 221192 | tf_op jit(solution)/shard_map/ppermute | solution.py:85
  31.2 4.4 %collective-permute-start.11 = (bf16[144,256]{1,0:T(8,128)(2,1)S(1)}, bf16[144,256]{1,0:T(8,128)(2,1)S(1)}, u32[]{:S(2)}, u32[]{:S(2)}) collective-permute-start(bf16[144,256]{1,0:T(8,128)(2,1)S(1)} %get-tuple-element.46), channel_id=1, source_target_pairs={{0,4},{4,0},{8,12},{12,8},{1,5},{5,1},{9,13},{13,9},{2,6},{6,2},{1... | collective-permute-start | bytes 221192 | tf_op jit(solution)/shard_map/ppermute | solution.py:85
  33.9 6.3 %collective-permute-start.8 = (bf16[256,256]{1,0:T(8,128)(2,1)S(1)}, bf16[256,256]{1,0:T(8,128)(2,1)S(1)}, u32[]{:S(2)}, u32[]{:S(2)}) collective-permute-start(bf16[256,256]{1,0:T(8,128)(2,1)S(1)} %collective-permute-done.7.refs_2_), channel_id=1, source_target_pairs={{0,1},{1,0},{2,3},{3,2},{4,5},{5,4},{6,7},{7,6},{8,9},{9,8},{10,11... | collective-permute-start | bytes 393224 | tf_op jit(solution)/shard_map/ppermute | solution.py:85
  35.7 7.1 %collective-permute-start.16 = (bf16[144,256]{1,0:T(8,128)(2,1)S(1)}, bf16[144,256]{1,0:T(8,128)(2,1)S(1)}, u32[]{:S(2)}, u32[]{:S(2)}) collective-permute-start(bf16[144,256]{1,0:T(8,128)(2,1)S(1)} %add_convert_fusion), channel_id=1, source_target_pairs={{0,3},{1,2},{2,1},{3,0},{4,7},{5,6},{6,5},{7,4},{8,11},{9,10},{10,... | collective-permute-start | bytes 221192 | tf_op jit(solution)/shard_map/ppermute | solution.py:85
  37.1 7.8 %collective-permute-start.15 = (bf16[144,256]{1,0:T(8,128)(2,1)S(1)}, bf16[144,256]{1,0:T(8,128)(2,1)S(1)}, u32[]{:S(2)}, u32[]{:S(2)}) collective-permute-start(bf16[144,256]{1,0:T(8,128)(2,1)S(1)} %add_convert_fusion), channel_id=1, source_target_pairs={{0,2},{1,3},{2,0},{3,1},{4,6},{5,7},{6,4},{7,5},{8,10},{9,11},{10,... | collective-permute-start | bytes 221192 | tf_op jit(solution)/shard_map/ppermute | solution.py:85
  37.5 7.4 %collective-permute-start.14 = (bf16[144,256]{1,0:T(8,128)(2,1)S(1)}, bf16[144,256]{1,0:T(8,128)(2,1)S(1)}, u32[]{:S(2)}, u32[]{:S(2)}) collective-permute-start(bf16[144,256]{1,0:T(8,128)(2,1)S(1)} %add_convert_fusion), channel_id=1, source_target_pairs={{0,1},{1,0},{2,3},{3,2},{4,5},{5,4},{6,7},{7,6},{8,9},{9,8},{10,11... | collective-permute-start | bytes 221192 | tf_op jit(solution)/shard_map/ppermute | solution.py:85
  40.9 4.1 %collective-permute-start.9 = (bf16[2,256,256]{2,1,0:T(8,128)(2,1)S(1)}, bf16[2,256,256]{2,1,0:T(8,128)(2,1)S(1)}, u32[]{:S(2)}, u32[]{:S(2)}) collective-permute-start(bf16[2,256,256]{2,1,0:T(8,128)(2,1)S(1)} %get-tuple-element.42), channel_id=1, source_target_pairs={{0,4},{4,0},{8,12},{12,8},{1,5},{5,1},{9,13},{13,9},{2,6},{6,2},{1... | collective-permute-start | bytes 786440 | tf_op jit(solution)/shard_map/ppermute | solution.py:85
  44.9 1.5 %collective-permute-start.17 = (f32[144,256]{1,0:T(8,128)S(1)}, f32[144,256]{1,0:T(8,128)S(1)}, u32[]{:S(2)}, u32[]{:S(2)}) collective-permute-start(f32[144,256]{1,0:T(8,128)S(1)} %add_add_fusion.half_ref), channel_id=1, source_target_pairs={{0,4},{4,0},{8,12},{12,8},{1,5},{5,1},{9,13},{13,9},{2,6},{6,2},{1... | collective-permute-start | bytes 442376 | tf_op jit(solution)/shard_map/ppermute | solution.py:85
  45.1 6.0 %collective-permute-start.10 = (bf16[256,256]{1,0:T(8,128)(2,1)S(1)}, bf16[256,256]{1,0:T(8,128)(2,1)S(1)}, u32[]{:S(2)}, u32[]{:S(2)}) collective-permute-start(bf16[256,256]{1,0:T(8,128)(2,1)S(1)} %get-tuple-element.44), channel_id=1, source_target_pairs={{0,8},{4,12},{8,0},{12,4},{1,9},{5,13},{9,1},{13,5},{2,10},{6,14},... | collective-permute-start | bytes 393224 | tf_op jit(solution)/shard_map/ppermute | solution.py:85

commit v4 on v3

--- a/solution.py
+++ b/solution.py
@@ -285,13 +285,10 @@
 
 def totals_kernel(after_ref, *refs):
     del after_ref
-    summed_refs, pre_refs, grad_refs = (refs[i * PIECES : (i + 1) * PIECES] for i in range(3))
-    hidden_ref, mine_ref, other_ref = refs[3 * PIECES :]
-    height, feat = summed_refs[0].shape
+    summed_refs, grad_refs = refs[:PIECES], refs[PIECES : 2 * PIECES]
+    mine_ref, other_ref = refs[2 * PIECES :]
+    feat = summed_refs[0].shape[1]
     core = lax.axis_index("row") & 1
-    for h in range(PIECES):
-        pre = pre_refs[h][...]
-        hidden_ref[h * height : (h + 1) * height, :] = (pre * jax.nn.sigmoid(pre)).astype(BF)
     grad_pre = jnp.concatenate([ref[...] for ref in grad_refs], axis=0)
     bias_row = jnp.sum(grad_pre.astype(F32), axis=0, keepdims=True)
     middle = feat // 2
@@ -304,15 +301,14 @@
         target[middle:, :] = spread.astype(BF)
 
 
-def totals(after, summed, pre, grad_pre):
-    rows, feat = pre[0].shape[0] * PIECES, pre[0].shape[1]
+def totals(after, summed, grad_pre):
+    rows, feat = summed[0].shape[0] * PIECES, summed[0].shape[1]
     half = (feat // 2 + 16, feat)
     return pl.pallas_call(
         totals_kernel,
-        in_specs=[VMEM] * (1 + 3 * PIECES),
-        out_specs=[VMEM] * 3,
+        in_specs=[VMEM] * (1 + 2 * PIECES),
+        out_specs=[VMEM] * 2,
         out_shape=[
-            jax.ShapeDtypeStruct((rows, feat), BF),
             jax.ShapeDtypeStruct(half, BF),
             jax.ShapeDtypeStruct(half, BF),
         ],
@@ -321,7 +317,7 @@
             flops=2 * rows * feat * feat, bytes_accessed=20 * rows * feat, transcendentals=rows * feat
         ),
         name="totals",
-    )(after, *summed, *pre, *grad_pre)
+    )(after, *summed, *grad_pre)
 
 
 def finish_kernel(scale, keep_ref, other_ref, half_ref, twin_ref, grad_ref, weight_ref, bias_ref):
@@ -377,13 +373,16 @@
         grads[3] = swap(grads[2], "col", 1)
         gathered += [grads[k] for k in range(4)]
 
-    hidden, mine, others = totals(agg, *zip(*kept))
+    summed, pre, grad_pre = zip(*kept)
+    mine, others = totals(agg, summed, grad_pre)
+    hidden = jax.nn.silu(jnp.concatenate(pre, axis=0)).astype(BF)
     half = tree(mine, swap(others, "row", 1), swap(mine, "row", 2), swap(others, "row", 3)).astype(BF)
 
     keep, send, pair = backward(dense, gathered)
     keep, send = pair_sum(keep, send, swap(pair, "row", 1))
 
     half = tree(half, *(swap(half, "col", k) for k in (1, 2, 3)))
+    half, keep = lax.optimization_barrier((half, keep))
     twin = swap(half, "row", 1)
     grad_features, grad_weight, grad_bias = finish(
         float(rows * 16) ** (-0.5), keep, swap(send, "row", 2), half, twin

time: 52 us -> 50.9 us (0.979)
  waiting for transfers between devices: 24.1 us -> 23.2 us
  other arithmetic: 0.75 us -> 1.49 us
  Pallas kernels: 6.03 us -> 5.46 us
    ppermute x18, waiting for transfers between devices: 24.1 us -> 23.2 us  [swap(): return lax.ppermute(x, axis, [(i, i ^ bit) for i in range(size)])]
    broadcast_in_dim x0 -> x1, other arithmetic: none -> 0.73 us  [dense_device(): hidden[None, None]]
    pallas_call x1, Pallas kernels: 0.82 us -> 0.24 us  [totals(): pl.pallas_call(totals_kernel, in_specs=[VMEM] * (1 + 2 * PIECES), out_spe...]
  transfers between devices with their start and end apart: 18 -> 18, of which waited for: 11 -> 10; matrix products, arithmetic and copies ran while one was open for 1% -> 3% of each run, Pallas kernels for 8% -> 7%
where the time goes in v4:
time: 50.9 us; the launch traced here: 50.7 us
  waiting for transfers between devices  23.2 us (46%)
  starting transfers between devices  19.1 us (38%)
  Pallas kernels  5.46 us (11%)
  other arithmetic  1.49 us (3%)
  between operations  1.42 us (3%)
    ppermute x18, waiting for transfers between devices, swap(): return lax.ppermute(x, axis, [(i, i ^ bit) for i in range(size)])  23.2 us
    ppermute x18, starting transfers between devices, swap(): return lax.ppermute(x, axis, [(i, i ^ bit) for i in range(size)])  19.1 us
    pallas_call x1, Pallas kernels, build_dense(): pl.pallas_call(build_kernel, in_specs=[HBM] * 2, out_specs=VMEM, out_shap...  2.54 us
  transfers between devices with their start and end apart: 18, of which 10 were waited for; matrix products, arithmetic and copies ran while one was open for 3% of the time, Pallas kernels for 7%

profile of v4, /device:TPU:0, one launch (start us, length us, event | category | flops | bytes accessed | tf_op | source)
XLA Modules:
  0.0 50.7 jit_solution(13442142063666233525)
XLA Ops:
  0.6 3.0 %collective-permute-start = (bf16[256,256]{1,0:T(8,128)(2,1)}, bf16[256,256]{1,0:T(8,128)(2,1)S(1)}, u32[]{:S(2)}, u32[]{:S(2)}) collective-permute-start(bf16[256,256]{1,0:T(8,128)(2,1)} %bitcast.12), channel_id=1, source_target_pairs={{0,8},{4,12},{8,0},{12,4},{1,9},{5,13},{9,1},{13,5},{2,10},{6,14},... | collective-permute-start | bytes 393224 | tf_op jit(solution)/shard_map/ppermute | solution.py:85
  4.3 0.7 %add_bitcast_fusion = s32[128]{0:T(128)S(1)} fusion(s32[1,1,128]{2,1,0:T(1,128)} %param.12, s32[1,1,128]{2,1,0:T(1,128)} %param.11), kind=kLoop, calls=%fused_computation.4 | loop fusion | flops 256 | bytes 1536 | tf_op jit(solution)/shard_map/add | solution.py:132
  5.0 2.5 %build_dense.1.dense_ref = bf16[4,1024,256]{2,1,0:T(8,128)(2,1)S(1)} custom-call(s32[256]{0:T(256)S(1)} %concatenate.3.slots_hbm, bf16[128,128,128]{2,1,0:T(8,128)(2,1)} %bitcast.17), custom_call_target="tpu_custom_call" | custom-call | flops 8388608 | bytes 6291456 | tf_op jit(solution)/shard_map/build_dense/pallas_call | solution.py:133
  8.1 1.0 %collective-permute-done.2.refs_3_ = bf16[256,256]{1,0:T(8,128)(2,1)S(1)} collective-permute-done((bf16[256,256]{1,0:T(8,128)(2,1)S(1)}, bf16[256,256]{1,0:T(8,128)(2,1)S(1)}, u32[]{:S(2)}, u32[]{:S(2)}) %collective-permute-start.2) | collective-permute-done | bytes 131104 | tf_op jit(solution)/shard_map/ppermute | solution.py:85
  9.1 0.7 %forward.1 = (bf16[256,256]{1,0:T(8,128)(2,1)S(1)}, bf16[256,256]{1,0:T(8,128)(2,1)S(1)}, bf16[256,256]{1,0:T(8,128)(2,1)S(1)}, bf16[256,256]{1,0:T(8,128)(2,1)S(1)}) custom-call(bf16[4,1024,256]{2,1,0:T(8,128)(2,1)S(1)} %build_dense.1.dense_ref, bf16[256,256]{1,0:T(8,128)(2,1)S(1)} %bitcast.14, bf16[256,256]{1,0:T(8,128)(2,1)S(1)} %collective-permute-done.1.refs_1_, ...), custom_call_target="tpu_custom_call" | custom-call | flops 536870912 | bytes 3145728 | tf_op jit(solution)/shard_map/forward/pallas_call | solution.py:170
  9.8 4.1 %collective-permute-start.3 = (bf16[256,256]{1,0:T(8,128)(2,1)S(1)}, bf16[256,256]{1,0:T(8,128)(2,1)S(1)}, u32[]{:S(2)}, u32[]{:S(2)}) collective-permute-start(bf16[256,256]{1,0:T(8,128)(2,1)S(1)} %get-tuple-element.31), channel_id=1, source_target_pairs={{0,3},{1,2},{2,1},{3,0},{4,7},{5,6},{6,5},{7,4},{8,11},{9,10},{10,... | collective-permute-start | bytes 393224 | tf_op jit(solution)/shard_map/ppermute | solution.py:85
  14.6 3.7 %collective-permute-done.3.refs_1_ = bf16[256,256]{1,0:T(8,128)(2,1)S(1)} collective-permute-done((bf16[256,256]{1,0:T(8,128)(2,1)S(1)}, bf16[256,256]{1,0:T(8,128)(2,1)S(1)}, u32[]{:S(2)}, u32[]{:S(2)}) %collective-permute-start.3) | collective-permute-done | bytes 131104 | tf_op jit(solution)/shard_map/ppermute | solution.py:85
  18.3 3.5 %collective-permute-done.4.refs_2_ = bf16[256,256]{1,0:T(8,128)(2,1)S(1)} collective-permute-done((bf16[256,256]{1,0:T(8,128)(2,1)S(1)}, bf16[256,256]{1,0:T(8,128)(2,1)S(1)}, u32[]{:S(2)}, u32[]{:S(2)}) %collective-permute-start.4) | collective-permute-done | bytes 131104 | tf_op jit(solution)/shard_map/ppermute | solution.py:85
  21.8 3.4 %collective-permute-done.5.refs_3_ = bf16[256,256]{1,0:T(8,128)(2,1)S(1)} collective-permute-done((bf16[256,256]{1,0:T(8,128)(2,1)S(1)}, bf16[256,256]{1,0:T(8,128)(2,1)S(1)}, u32[]{:S(2)}, u32[]{:S(2)}) %collective-permute-start.5) | collective-permute-done | bytes 131104 | tf_op jit(solution)/shard_map/ppermute | solution.py:85
  25.6 3.0 %collective-permute-start.13 = (bf16[256,256]{1,0:T(8,128)(2,1)S(1)}, bf16[256,256]{1,0:T(8,128)(2,1)S(1)}, u32[]{:S(2)}, u32[]{:S(2)}) collective-permute-start(bf16[256,256]{1,0:T(8,128)(2,1)S(1)} %get-tuple-element.35.after_ref.refs_0_), channel_id=1, source_target_pairs={{0,2},{1,3},{2,0},{3,1},{4,6},{5,7},{6,4},{7,5},{8,10},{9,11},{10,... | collective-permute-start | bytes 393224 | tf_op jit(solution)/shard_map/ppermute | solution.py:85
  28.9 1.2 %collective-permute-start.7 = (bf16[144,256]{1,0:T(8,128)(2,1)S(1)}, bf16[144,256]{1,0:T(8,128)(2,1)S(1)}, u32[]{:S(2)}, u32[]{:S(2)}) collective-permute-start(bf16[144,256]{1,0:T(8,128)(2,1)S(1)} %get-tuple-element.38), channel_id=1, source_target_pairs={{0,8},{4,12},{8,0},{12,4},{1,9},{5,13},{9,1},{13,5},{2,10},{6,14},... | collective-permute-start | bytes 221192 | tf_op jit(solution)/shard_map/ppermute | solution.py:85
  30.8 2.4 %collective-permute-done.12.refs_1_ = bf16[256,256]{1,0:T(8,128)(2,1)S(1)} collective-permute-done((bf16[256,256]{1,0:T(8,128)(2,1)S(1)}, bf16[256,256]{1,0:T(8,128)(2,1)S(1)}, u32[]{:S(2)}, u32[]{:S(2)}) %collective-permute-start.12) | collective-permute-done | bytes 131104 | tf_op jit(solution)/shard_map/ppermute | solution.py:85
  33.2 1.3 %collective-permute-done.13.refs_2_ = bf16[256,256]{1,0:T(8,128)(2,1)S(1)} collective-permute-done((bf16[256,256]{1,0:T(8,128)(2,1)S(1)}, bf16[256,256]{1,0:T(8,128)(2,1)S(1)}, u32[]{:S(2)}, u32[]{:S(2)}) %collective-permute-start.13) | collective-permute-done | bytes 131104 | tf_op jit(solution)/shard_map/ppermute | solution.py:85
  34.8 2.2 %collective-permute-start.11 = (bf16[144,256]{1,0:T(8,128)(2,1)S(1)}, bf16[144,256]{1,0:T(8,128)(2,1)S(1)}, u32[]{:S(2)}, u32[]{:S(2)}) collective-permute-start(bf16[144,256]{1,0:T(8,128)(2,1)S(1)} %add_convert_fusion), channel_id=1, source_target_pairs={{0,3},{1,2},{2,1},{3,0},{4,7},{5,6},{6,5},{7,4},{8,11},{9,10},{10,... | collective-permute-start | bytes 221192 | tf_op jit(solution)/shard_map/ppermute | solution.py:85
  37.0 1.0 %collective-permute-start.10 = (bf16[144,256]{1,0:T(8,128)(2,1)S(1)}, bf16[144,256]{1,0:T(8,128)(2,1)S(1)}, u32[]{:S(2)}, u32[]{:S(2)}) collective-permute-start(bf16[144,256]{1,0:T(8,128)(2,1)S(1)} %add_convert_fusion), channel_id=1, source_target_pairs={{0,2},{1,3},{2,0},{3,1},{4,6},{5,7},{6,4},{7,5},{8,10},{9,11},{10,... | collective-permute-start | bytes 221192 | tf_op jit(solution)/shard_map/ppermute | solution.py:85
  38.0 1.2 %collective-permute-start.9 = (bf16[144,256]{1,0:T(8,128)(2,1)S(1)}, bf16[144,256]{1,0:T(8,128)(2,1)S(1)}, u32[]{:S(2)}, u32[]{:S(2)}) collective-permute-start(bf16[144,256]{1,0:T(8,128)(2,1)S(1)} %add_convert_fusion), channel_id=1, source_target_pairs={{0,1},{1,0},{2,3},{3,2},{4,5},{5,4},{6,7},{7,6},{8,9},{9,8},{10,11... | collective-permute-start | bytes 221192 | tf_op jit(solution)/shard_map/ppermute | solution.py:85
  39.3 1.4 %collective-permute-done.14.refs_3_ = bf16[256,256]{1,0:T(8,128)(2,1)S(1)} collective-permute-done((bf16[256,256]{1,0:T(8,128)(2,1)S(1)}, bf16[256,256]{1,0:T(8,128)(2,1)S(1)}, u32[]{:S(2)}, u32[]{:S(2)}) %collective-permute-start.14) | collective-permute-done | bytes 131104 | tf_op jit(solution)/shard_map/ppermute | solution.py:85
  40.7 0.8 %backward.1 = (f32[256,256]{1,0:T(8,128)S(1)}, f32[256,256]{1,0:T(8,128)S(1)}, bf16[2,256,256]{2,1,0:T(8,128)(2,1)S(1)}) custom-call(bf16[4,1024,256]{2,1,0:T(8,128)(2,1)S(1)} %build_dense.1.dense_ref, bf16[256,256]{1,0:T(8,128)(2,1)S(1)} %get-tuple-element.35.after_ref.refs_0_, bf16[256,256]{1,0:T(8,128)(2,1)S(1)} %collective-permute-done.12.refs_1_, ...), custom_call_target="tpu_custom_call" | custom-call | flops 536870912 | bytes 3145728 | tf_op jit(solution)/shard_map/backward/pallas_call | solution.py:214
  41.6 0.7 %collective-permute-done.11 = bf16[144,256]{1,0:T(8,128)(2,1)S(1)} collective-permute-done((bf16[144,256]{1,0:T(8,128)(2,1)S(1)}, bf16[144,256]{1,0:T(8,128)(2,1)S(1)}, u32[]{:S(2)}, u32[]{:S(2)}) %collective-permute-start.11) | collective-permute-done | bytes 73760 | tf_op jit(solution)/shard_map/ppermute | solution.py:85
  42.3 2.5 %collective-permute-done.10 = bf16[144,256]{1,0:T(8,128)(2,1)S(1)} collective-permute-done((bf16[144,256]{1,0:T(8,128)(2,1)S(1)}, bf16[144,256]{1,0:T(8,128)(2,1)S(1)}, u32[]{:S(2)}, u32[]{:S(2)}) %collective-permute-start.10) | collective-permute-done | bytes 73760 | tf_op jit(solution)/shard_map/ppermute | solution.py:85
  44.9 1.0 %collective-permute-start.16 = (bf16[256,256]{1,0:T(8,128)(2,1)S(1)}, bf16[256,256]{1,0:T(8,128)(2,1)S(1)}, u32[]{:S(2)}, u32[]{:S(2)}) collective-permute-start(bf16[256,256]{1,0:T(8,128)(2,1)S(1)} %get-tuple-element.47), channel_id=1, source_target_pairs={{0,8},{4,12},{8,0},{12,4},{1,9},{5,13},{9,1},{13,5},{2,10},{6,14},... | collective-permute-start | bytes 393224 | tf_op jit(solution)/shard_map/ppermute | solution.py:85
  45.9 0.7 %fusion = bf16[1,1,256,256]{3,2,1,0:T(8,128)(2,1)} fusion(f32[256,256]{1,0:T(8,128)S(1)} %get-tuple-element.34), kind=kLoop, calls=%fused_computation.3 | loop fusion | flops 327680 | bytes 393216 | tf_op jit(solution)/shard_map/broadcast_in_dim | solution.py:390
  46.6 3.3 %collective-permute-done.16.other_ref = bf16[256,256]{1,0:T(8,128)(2,1)S(1)} collective-permute-done((bf16[256,256]{1,0:T(8,128)(2,1)S(1)}, bf16[256,256]{1,0:T(8,128)(2,1)S(1)}, u32[]{:S(2)}, u32[]{:S(2)}) %collective-permute-start.16) | collective-permute-done | bytes 131104 | tf_op jit(solution)/shard_map/ppermute | solution.py:85
  49.9 0.8 %finish.1 = (bf16[256,256]{1,0:T(8,128)(2,1)}, f32[256,256]{1,0:T(8,128)}, f32[1,256]{1,0:T(1,128)}) custom-call(f32[256,256]{1,0:T(8,128)S(1)} %get-tuple-element.46.keep_ref, bf16[256,256]{1,0:T(8,128)(2,1)S(1)} %collective-permute-done.16.other_ref, f32[144,256]{1,0:T(8,128)S(1)} %add_add_fusion.half_ref, f32[144,256]{1,0:T(8,128)S(1)} %collective-permute-done.17.twin_ref), custom_call_target="tpu_custom_call" | custom-call | flops 65536 | bytes 393216 | tf_op jit(solution)/shard_map/finish/pallas_call | solution.py:335
  (32 shorter events, 3.2 us)
Async XLA Ops:
  0.6 8.5 %copy-start = (bf16[1,1,256,256]{3,2,1,0:T(8,128)(2,1)S(1)}, bf16[1,1,256,256]{3,2,1,0:T(8,128)(2,1)}, u32[]{:S(2)}) copy-start(bf16[1,1,256,256]{3,2,1,0:T(8,128)(2,1)} %param.8) | copy-start | bytes 393220
  0.6 6.9 %collective-permute-start = (bf16[256,256]{1,0:T(8,128)(2,1)}, bf16[256,256]{1,0:T(8,128)(2,1)S(1)}, u32[]{:S(2)}, u32[]{:S(2)}) collective-permute-start(bf16[256,256]{1,0:T(8,128)(2,1)} %bitcast.12), channel_id=1, source_target_pairs={{0,8},{4,12},{8,0},{12,4},{1,9},{5,13},{9,1},{13,5},{2,10},{6,14},... | collective-permute-start | bytes 393224 | tf_op jit(solution)/shard_map/ppermute | solution.py:85
  3.6 4.5 %collective-permute-start.1 = (bf16[256,256]{1,0:T(8,128)(2,1)}, bf16[256,256]{1,0:T(8,128)(2,1)S(1)}, u32[]{:S(2)}, u32[]{:S(2)}) collective-permute-start(bf16[256,256]{1,0:T(8,128)(2,1)} %bitcast.13), channel_id=1, source_target_pairs={{0,4},{4,0},{8,12},{12,8},{1,5},{5,1},{9,13},{13,9},{2,6},{6,2},{1... | collective-permute-start | bytes 393224 | tf_op jit(solution)/shard_map/ppermute | solution.py:85
  5.0 20.2 %copy-start.1 = (bf16[256,256]{1,0:T(8,128)(2,1)S(1)}, bf16[256,256]{1,0:T(8,128)(2,1)}, u32[]{:S(2)}) copy-start(bf16[256,256]{1,0:T(8,128)(2,1)} %weight_ref.1) | copy-start | bytes 393220
  5.0 20.2 %copy-start.2 = (bf16[1,1,256,256]{3,2,1,0:T(8,128)(2,1)S(1)}, bf16[1,1,256,256]{3,2,1,0:T(8,128)(2,1)}, u32[]{:S(2)}) copy-start(bf16[1,1,256,256]{3,2,1,0:T(8,128)(2,1)} %param.15) | copy-start | bytes 393220
  5.0 20.2 %copy-start.3 = (f32[256]{0:T(256)S(1)}, f32[256]{0:T(256)}, u32[]{:S(2)}) copy-start(f32[256]{0:T(256)} %param.10) | copy-start | bytes 3076
  7.6 1.6 %collective-permute-start.2 = (bf16[256,256]{1,0:T(8,128)(2,1)S(1)}, bf16[256,256]{1,0:T(8,128)(2,1)S(1)}, u32[]{:S(2)}, u32[]{:S(2)}) collective-permute-start(bf16[256,256]{1,0:T(8,128)(2,1)S(1)} %collective-permute-done.refs_2_), channel_id=1, source_target_pairs={{0,4},{4,0},{8,12},{12,8},{1,5},{5,1},{9,13},{13,9},{2,6},{6,2},{1... | collective-permute-start | bytes 393224 | tf_op jit(solution)/shard_map/ppermute | solution.py:85
  9.8 8.4 %collective-permute-start.3 = (bf16[256,256]{1,0:T(8,128)(2,1)S(1)}, bf16[256,256]{1,0:T(8,128)(2,1)S(1)}, u32[]{:S(2)}, u32[]{:S(2)}) collective-permute-start(bf16[256,256]{1,0:T(8,128)(2,1)S(1)} %get-tuple-element.31), channel_id=1, source_target_pairs={{0,3},{1,2},{2,1},{3,0},{4,7},{5,6},{6,5},{7,4},{8,11},{9,10},{10,... | collective-permute-start | bytes 393224 | tf_op jit(solution)/shard_map/ppermute | solution.py:85
  13.9 7.9 %collective-permute-start.4 = (bf16[256,256]{1,0:T(8,128)(2,1)S(1)}, bf16[256,256]{1,0:T(8,128)(2,1)S(1)}, u32[]{:S(2)}, u32[]{:S(2)}) collective-permute-start(bf16[256,256]{1,0:T(8,128)(2,1)S(1)} %get-tuple-element.32), channel_id=1, source_target_pairs={{0,1},{1,0},{2,3},{3,2},{4,5},{5,4},{6,7},{7,6},{8,9},{9,8},{10,11... | collective-permute-start | bytes 393224 | tf_op jit(solution)/shard_map/ppermute | solution.py:85
  13.9 11.2 %collective-permute-start.5 = (bf16[256,256]{1,0:T(8,128)(2,1)S(1)}, bf16[256,256]{1,0:T(8,128)(2,1)S(1)}, u32[]{:S(2)}, u32[]{:S(2)}) collective-permute-start(bf16[256,256]{1,0:T(8,128)(2,1)S(1)} %get-tuple-element.33), channel_id=1, source_target_pairs={{0,2},{1,3},{2,0},{3,1},{4,6},{5,7},{6,4},{7,5},{8,10},{9,11},{10,... | collective-permute-start | bytes 393224 | tf_op jit(solution)/shard_map/ppermute | solution.py:85
  25.6 7.6 %collective-permute-start.12 = (bf16[256,256]{1,0:T(8,128)(2,1)S(1)}, bf16[256,256]{1,0:T(8,128)(2,1)S(1)}, u32[]{:S(2)}, u32[]{:S(2)}) collective-permute-start(bf16[256,256]{1,0:T(8,128)(2,1)S(1)} %get-tuple-element.35.after_ref.refs_0_), channel_id=1, source_target_pairs={{0,1},{1,0},{2,3},{3,2},{4,5},{5,4},{6,7},{7,6},{8,9},{9,8},{10,11... | collective-permute-start | bytes 393224 | tf_op jit(solution)/shard_map/ppermute | solution.py:85
  25.6 8.8 %collective-permute-start.13 = (bf16[256,256]{1,0:T(8,128)(2,1)S(1)}, bf16[256,256]{1,0:T(8,128)(2,1)S(1)}, u32[]{:S(2)}, u32[]{:S(2)}) collective-permute-start(bf16[256,256]{1,0:T(8,128)(2,1)S(1)} %get-tuple-element.35.after_ref.refs_0_), channel_id=1, source_target_pairs={{0,2},{1,3},{2,0},{3,1},{4,6},{5,7},{6,4},{7,5},{8,10},{9,11},{10,... | collective-permute-start | bytes 393224 | tf_op jit(solution)/shard_map/ppermute | solution.py:85
  28.8 5.9 %collective-permute-start.8 = (bf16[144,256]{1,0:T(8,128)(2,1)S(1)}, bf16[144,256]{1,0:T(8,128)(2,1)S(1)}, u32[]{:S(2)}, u32[]{:S(2)}) collective-permute-start(bf16[144,256]{1,0:T(8,128)(2,1)S(1)} %get-tuple-element.39), channel_id=1, source_target_pairs={{0,12},{4,8},{8,4},{12,0},{1,13},{5,9},{9,5},{13,1},{2,14},{6,10},... | collective-permute-start | bytes 221192 | tf_op jit(solution)/shard_map/ppermute | solution.py:85
  28.9 5.9 %collective-permute-start.7 = (bf16[144,256]{1,0:T(8,128)(2,1)S(1)}, bf16[144,256]{1,0:T(8,128)(2,1)S(1)}, u32[]{:S(2)}, u32[]{:S(2)}) collective-permute-start(bf16[144,256]{1,0:T(8,128)(2,1)S(1)} %get-tuple-element.38), channel_id=1, source_target_pairs={{0,8},{4,12},{8,0},{12,4},{1,9},{5,13},{9,1},{13,5},{2,10},{6,14},... | collective-permute-start | bytes 221192 | tf_op jit(solution)/shard_map/ppermute | solution.py:85
  30.1 4.7 %collective-permute-start.6 = (bf16[144,256]{1,0:T(8,128)(2,1)S(1)}, bf16[144,256]{1,0:T(8,128)(2,1)S(1)}, u32[]{:S(2)}, u32[]{:S(2)}) collective-permute-start(bf16[144,256]{1,0:T(8,128)(2,1)S(1)} %get-tuple-element.39), channel_id=1, source_target_pairs={{0,4},{4,0},{8,12},{12,8},{1,5},{5,1},{9,13},{13,9},{2,6},{6,2},{1... | collective-permute-start | bytes 221192 | tf_op jit(solution)/shard_map/ppermute | solution.py:85
  34.4 6.3 %collective-permute-start.14 = (bf16[256,256]{1,0:T(8,128)(2,1)S(1)}, bf16[256,256]{1,0:T(8,128)(2,1)S(1)}, u32[]{:S(2)}, u32[]{:S(2)}) collective-permute-start(bf16[256,256]{1,0:T(8,128)(2,1)S(1)} %collective-permute-done.13.refs_2_), channel_id=1, source_target_pairs={{0,1},{1,0},{2,3},{3,2},{4,5},{5,4},{6,7},{7,6},{8,9},{9,8},{10,11... | collective-permute-start | bytes 393224 | tf_op jit(solution)/shard_map/ppermute | solution.py:85
  34.8 7.5 %collective-permute-start.11 = (bf16[144,256]{1,0:T(8,128)(2,1)S(1)}, bf16[144,256]{1,0:T(8,128)(2,1)S(1)}, u32[]{:S(2)}, u32[]{:S(2)}) collective-permute-start(bf16[144,256]{1,0:T(8,128)(2,1)S(1)} %add_convert_fusion), channel_id=1, source_target_pairs={{0,3},{1,2},{2,1},{3,0},{4,7},{5,6},{6,5},{7,4},{8,11},{9,10},{10,... | collective-permute-start | bytes 221192 | tf_op jit(solution)/shard_map/ppermute | solution.py:85
  37.0 7.8 %collective-permute-start.10 = (bf16[144,256]{1,0:T(8,128)(2,1)S(1)}, bf16[144,256]{1,0:T(8,128)(2,1)S(1)}, u32[]{:S(2)}, u32[]{:S(2)}) collective-permute-start(bf16[144,256]{1,0:T(8,128)(2,1)S(1)} %add_convert_fusion), channel_id=1, source_target_pairs={{0,2},{1,3},{2,0},{3,1},{4,6},{5,7},{6,4},{7,5},{8,10},{9,11},{10,... | collective-permute-start | bytes 221192 | tf_op jit(solution)/shard_map/ppermute | solution.py:85
  38.0 6.7 %collective-permute-start.9 = (bf16[144,256]{1,0:T(8,128)(2,1)S(1)}, bf16[144,256]{1,0:T(8,128)(2,1)S(1)}, u32[]{:S(2)}, u32[]{:S(2)}) collective-permute-start(bf16[144,256]{1,0:T(8,128)(2,1)S(1)} %add_convert_fusion), channel_id=1, source_target_pairs={{0,1},{1,0},{2,3},{3,2},{4,5},{5,4},{6,7},{7,6},{8,9},{9,8},{10,11... | collective-permute-start | bytes 221192 | tf_op jit(solution)/shard_map/ppermute | solution.py:85
  41.5 3.3 %collective-permute-start.15 = (bf16[2,256,256]{2,1,0:T(8,128)(2,1)S(1)}, bf16[2,256,256]{2,1,0:T(8,128)(2,1)S(1)}, u32[]{:S(2)}, u32[]{:S(2)}) collective-permute-start(bf16[2,256,256]{2,1,0:T(8,128)(2,1)S(1)} %get-tuple-element.44), channel_id=1, source_target_pairs={{0,4},{4,0},{8,12},{12,8},{1,5},{5,1},{9,13},{13,9},{2,6},{6,2},{1... | collective-permute-start | bytes 786440 | tf_op jit(solution)/shard_map/ppermute | solution.py:85
  44.9 5.0 %collective-permute-start.16 = (bf16[256,256]{1,0:T(8,128)(2,1)S(1)}, bf16[256,256]{1,0:T(8,128)(2,1)S(1)}, u32[]{:S(2)}, u32[]{:S(2)}) collective-permute-start(bf16[256,256]{1,0:T(8,128)(2,1)S(1)} %get-tuple-element.47), channel_id=1, source_target_pairs={{0,8},{4,12},{8,0},{12,4},{1,9},{5,13},{9,1},{13,5},{2,10},{6,14},... | collective-permute-start | bytes 393224 | tf_op jit(solution)/shard_map/ppermute | solution.py:85
  45.9 4.0 %collective-permute-start.17 = (f32[144,256]{1,0:T(8,128)S(1)}, f32[144,256]{1,0:T(8,128)S(1)}, u32[]{:S(2)}, u32[]{:S(2)}) collective-permute-start(f32[144,256]{1,0:T(8,128)S(1)} %add_add_fusion.half_ref), channel_id=1, source_target_pairs={{0,4},{4,0},{8,12},{12,8},{1,5},{5,1},{9,13},{13,9},{2,6},{6,2},{1... | collective-permute-start | bytes 442376 | tf_op jit(solution)/shard_map/ppermute | solution.py:85

commit v5 on v4

--- a/solution.py
+++ b/solution.py
@@ -362,7 +362,7 @@
     kept, gathered, after = [], [], []
     for h in range(PIECES):
         mine = partial[h * 4 : (h + 1) * 4]
-        terms = [mine[0]] + [swap(mine[k], "col", k) for k in (3, 1, 2)]
+        terms = [mine[0]] + [swap(mine[k], "col", k) for k in (3, 2, 1)]
         agg, *rest = gradient(weight, bias[None, :], cotangent[0, 0], terms, after, h)
         kept.append(rest)
         after = [agg]

time: 50.9 us -> 51.1 us (level)
  starting transfers between devices: 19.1 us -> 18.4 us
    ppermute x18, starting transfers between devices: 19.1 us -> 18.4 us  [swap(): return lax.ppermute(x, axis, [(i, i ^ bit) for i in range(size)])]
  transfers between devices with their start and end apart: 18 -> 18, of which waited for: 10 -> 9; matrix products, arithmetic and copies ran while one was open for 3% -> 3% of each run, Pallas kernels for 7% -> 8%
where the time goes in v5:
time: 51.1 us; the launch traced here: 50.8 us
  waiting for transfers between devices  23.6 us (46%)
  starting transfers between devices  18.4 us (36%)
  Pallas kernels  5.83 us (11%)
  other arithmetic  1.49 us (3%)
  between operations  1.42 us (3%)
    ppermute x18, waiting for transfers between devices, swap(): return lax.ppermute(x, axis, [(i, i ^ bit) for i in range(size)])  23.6 us
    ppermute x18, starting transfers between devices, swap(): return lax.ppermute(x, axis, [(i, i ^ bit) for i in range(size)])  18.4 us
    pallas_call x1, Pallas kernels, build_dense(): pl.pallas_call(build_kernel, in_specs=[HBM] * 2, out_specs=VMEM, out_shap...  2.91 us
  transfers between devices with their start and end apart: 18, of which 9 were waited for; matrix products, arithmetic and copies ran while one was open for 3% of the time, Pallas kernels for 8%

profile of v5, /device:TPU:0, one launch (start us, length us, event | category | flops | bytes accessed | tf_op | source)
XLA Modules:
  0.0 50.8 jit_solution(13996694412281585383)
XLA Ops:
  0.6 3.0 %collective-permute-start = (bf16[256,256]{1,0:T(8,128)(2,1)}, bf16[256,256]{1,0:T(8,128)(2,1)S(1)}, u32[]{:S(2)}, u32[]{:S(2)}) collective-permute-start(bf16[256,256]{1,0:T(8,128)(2,1)} %bitcast.12), channel_id=1, source_target_pairs={{0,8},{4,12},{8,0},{12,4},{1,9},{5,13},{9,1},{13,5},{2,10},{6,14},... | collective-permute-start | bytes 393224 | tf_op jit(solution)/shard_map/ppermute | solution.py:85
  4.3 0.7 %add_bitcast_fusion = s32[128]{0:T(128)S(1)} fusion(s32[1,1,128]{2,1,0:T(1,128)} %param.12, s32[1,1,128]{2,1,0:T(1,128)} %param.11), kind=kLoop, calls=%fused_computation.4 | loop fusion | flops 256 | bytes 1536 | tf_op jit(solution)/shard_map/add | solution.py:132
  5.0 2.9 %build_dense.1.dense_ref = bf16[4,1024,256]{2,1,0:T(8,128)(2,1)S(1)} custom-call(s32[256]{0:T(256)S(1)} %concatenate.3.slots_hbm, bf16[128,128,128]{2,1,0:T(8,128)(2,1)} %bitcast.17), custom_call_target="tpu_custom_call" | custom-call | flops 8388608 | bytes 6291456 | tf_op jit(solution)/shard_map/build_dense/pallas_call | solution.py:133
  8.1 1.2 %collective-permute-done.2.refs_3_ = bf16[256,256]{1,0:T(8,128)(2,1)S(1)} collective-permute-done((bf16[256,256]{1,0:T(8,128)(2,1)S(1)}, bf16[256,256]{1,0:T(8,128)(2,1)S(1)}, u32[]{:S(2)}, u32[]{:S(2)}) %collective-permute-start.2) | collective-permute-done | bytes 131104 | tf_op jit(solution)/shard_map/ppermute | solution.py:85
  9.4 0.7 %forward.1 = (bf16[256,256]{1,0:T(8,128)(2,1)S(1)}, bf16[256,256]{1,0:T(8,128)(2,1)S(1)}, bf16[256,256]{1,0:T(8,128)(2,1)S(1)}, bf16[256,256]{1,0:T(8,128)(2,1)S(1)}) custom-call(bf16[4,1024,256]{2,1,0:T(8,128)(2,1)S(1)} %build_dense.1.dense_ref, bf16[256,256]{1,0:T(8,128)(2,1)S(1)} %bitcast.14, bf16[256,256]{1,0:T(8,128)(2,1)S(1)} %collective-permute-done.1.refs_1_, ...), custom_call_target="tpu_custom_call" | custom-call | flops 536870912 | bytes 3145728 | tf_op jit(solution)/shard_map/forward/pallas_call | solution.py:170
  10.1 3.8 %collective-permute-start.3 = (bf16[256,256]{1,0:T(8,128)(2,1)S(1)}, bf16[256,256]{1,0:T(8,128)(2,1)S(1)}, u32[]{:S(2)}, u32[]{:S(2)}) collective-permute-start(bf16[256,256]{1,0:T(8,128)(2,1)S(1)} %get-tuple-element.31), channel_id=1, source_target_pairs={{0,3},{1,2},{2,1},{3,0},{4,7},{5,6},{6,5},{7,4},{8,11},{9,10},{10,... | collective-permute-start | bytes 393224 | tf_op jit(solution)/shard_map/ppermute | solution.py:85
  14.5 3.8 %collective-permute-done.3.refs_1_ = bf16[256,256]{1,0:T(8,128)(2,1)S(1)} collective-permute-done((bf16[256,256]{1,0:T(8,128)(2,1)S(1)}, bf16[256,256]{1,0:T(8,128)(2,1)S(1)}, u32[]{:S(2)}, u32[]{:S(2)}) %collective-permute-start.3) | collective-permute-done | bytes 131104 | tf_op jit(solution)/shard_map/ppermute | solution.py:85
  18.3 6.9 %collective-permute-done.4.refs_2_ = bf16[256,256]{1,0:T(8,128)(2,1)S(1)} collective-permute-done((bf16[256,256]{1,0:T(8,128)(2,1)S(1)}, bf16[256,256]{1,0:T(8,128)(2,1)S(1)}, u32[]{:S(2)}, u32[]{:S(2)}) %collective-permute-start.4) | collective-permute-done | bytes 131104 | tf_op jit(solution)/shard_map/ppermute | solution.py:85
  25.8 2.9 %collective-permute-start.13 = (bf16[256,256]{1,0:T(8,128)(2,1)S(1)}, bf16[256,256]{1,0:T(8,128)(2,1)S(1)}, u32[]{:S(2)}, u32[]{:S(2)}) collective-permute-start(bf16[256,256]{1,0:T(8,128)(2,1)S(1)} %get-tuple-element.35.after_ref.refs_0_), channel_id=1, source_target_pairs={{0,2},{1,3},{2,0},{3,1},{4,6},{5,7},{6,4},{7,5},{8,10},{9,11},{10,... | collective-permute-start | bytes 393224 | tf_op jit(solution)/shard_map/ppermute | solution.py:85
  29.0 1.2 %collective-permute-start.7 = (bf16[144,256]{1,0:T(8,128)(2,1)S(1)}, bf16[144,256]{1,0:T(8,128)(2,1)S(1)}, u32[]{:S(2)}, u32[]{:S(2)}) collective-permute-start(bf16[144,256]{1,0:T(8,128)(2,1)S(1)} %get-tuple-element.38), channel_id=1, source_target_pairs={{0,8},{4,12},{8,0},{12,4},{1,9},{5,13},{9,1},{13,5},{2,10},{6,14},... | collective-permute-start | bytes 221192 | tf_op jit(solution)/shard_map/ppermute | solution.py:85
  30.1 0.7 %collective-permute-start.6 = (bf16[144,256]{1,0:T(8,128)(2,1)S(1)}, bf16[144,256]{1,0:T(8,128)(2,1)S(1)}, u32[]{:S(2)}, u32[]{:S(2)}) collective-permute-start(bf16[144,256]{1,0:T(8,128)(2,1)S(1)} %get-tuple-element.39), channel_id=1, source_target_pairs={{0,4},{4,0},{8,12},{12,8},{1,5},{5,1},{9,13},{13,9},{2,6},{6,2},{1... | collective-permute-start | bytes 221192 | tf_op jit(solution)/shard_map/ppermute | solution.py:85
  30.8 2.4 %collective-permute-done.12.refs_1_ = bf16[256,256]{1,0:T(8,128)(2,1)S(1)} collective-permute-done((bf16[256,256]{1,0:T(8,128)(2,1)S(1)}, bf16[256,256]{1,0:T(8,128)(2,1)S(1)}, u32[]{:S(2)}, u32[]{:S(2)}) %collective-permute-start.12) | collective-permute-done | bytes 131104 | tf_op jit(solution)/shard_map/ppermute | solution.py:85
  33.2 1.3 %collective-permute-done.13.refs_2_ = bf16[256,256]{1,0:T(8,128)(2,1)S(1)} collective-permute-done((bf16[256,256]{1,0:T(8,128)(2,1)S(1)}, bf16[256,256]{1,0:T(8,128)(2,1)S(1)}, u32[]{:S(2)}, u32[]{:S(2)}) %collective-permute-start.13) | collective-permute-done | bytes 131104 | tf_op jit(solution)/shard_map/ppermute | solution.py:85
  34.8 2.2 %collective-permute-start.11 = (bf16[144,256]{1,0:T(8,128)(2,1)S(1)}, bf16[144,256]{1,0:T(8,128)(2,1)S(1)}, u32[]{:S(2)}, u32[]{:S(2)}) collective-permute-start(bf16[144,256]{1,0:T(8,128)(2,1)S(1)} %add_convert_fusion), channel_id=1, source_target_pairs={{0,3},{1,2},{2,1},{3,0},{4,7},{5,6},{6,5},{7,4},{8,11},{9,10},{10,... | collective-permute-start | bytes 221192 | tf_op jit(solution)/shard_map/ppermute | solution.py:85
  37.1 1.0 %collective-permute-start.10 = (bf16[144,256]{1,0:T(8,128)(2,1)S(1)}, bf16[144,256]{1,0:T(8,128)(2,1)S(1)}, u32[]{:S(2)}, u32[]{:S(2)}) collective-permute-start(bf16[144,256]{1,0:T(8,128)(2,1)S(1)} %add_convert_fusion), channel_id=1, source_target_pairs={{0,2},{1,3},{2,0},{3,1},{4,6},{5,7},{6,4},{7,5},{8,10},{9,11},{10,... | collective-permute-start | bytes 221192 | tf_op jit(solution)/shard_map/ppermute | solution.py:85
  38.1 1.2 %collective-permute-start.9 = (bf16[144,256]{1,0:T(8,128)(2,1)S(1)}, bf16[144,256]{1,0:T(8,128)(2,1)S(1)}, u32[]{:S(2)}, u32[]{:S(2)}) collective-permute-start(bf16[144,256]{1,0:T(8,128)(2,1)S(1)} %add_convert_fusion), channel_id=1, source_target_pairs={{0,1},{1,0},{2,3},{3,2},{4,5},{5,4},{6,7},{7,6},{8,9},{9,8},{10,11... | collective-permute-start | bytes 221192 | tf_op jit(solution)/shard_map/ppermute | solution.py:85
  39.3 1.5 %collective-permute-done.14.refs_3_ = bf16[256,256]{1,0:T(8,128)(2,1)S(1)} collective-permute-done((bf16[256,256]{1,0:T(8,128)(2,1)S(1)}, bf16[256,256]{1,0:T(8,128)(2,1)S(1)}, u32[]{:S(2)}, u32[]{:S(2)}) %collective-permute-start.14) | collective-permute-done | bytes 131104 | tf_op jit(solution)/shard_map/ppermute | solution.py:85
  40.8 0.8 %backward.1 = (f32[256,256]{1,0:T(8,128)S(1)}, f32[256,256]{1,0:T(8,128)S(1)}, bf16[2,256,256]{2,1,0:T(8,128)(2,1)S(1)}) custom-call(bf16[4,1024,256]{2,1,0:T(8,128)(2,1)S(1)} %build_dense.1.dense_ref, bf16[256,256]{1,0:T(8,128)(2,1)S(1)} %get-tuple-element.35.after_ref.refs_0_, bf16[256,256]{1,0:T(8,128)(2,1)S(1)} %collective-permute-done.12.refs_1_, ...), custom_call_target="tpu_custom_call" | custom-call | flops 536870912 | bytes 3145728 | tf_op jit(solution)/shard_map/backward/pallas_call | solution.py:214
  41.7 0.7 %collective-permute-done.11 = bf16[144,256]{1,0:T(8,128)(2,1)S(1)} collective-permute-done((bf16[144,256]{1,0:T(8,128)(2,1)S(1)}, bf16[144,256]{1,0:T(8,128)(2,1)S(1)}, u32[]{:S(2)}, u32[]{:S(2)}) %collective-permute-start.11) | collective-permute-done | bytes 73760 | tf_op jit(solution)/shard_map/ppermute | solution.py:85
  42.4 2.5 %collective-permute-done.10 = bf16[144,256]{1,0:T(8,128)(2,1)S(1)} collective-permute-done((bf16[144,256]{1,0:T(8,128)(2,1)S(1)}, bf16[144,256]{1,0:T(8,128)(2,1)S(1)}, u32[]{:S(2)}, u32[]{:S(2)}) %collective-permute-start.10) | collective-permute-done | bytes 73760 | tf_op jit(solution)/shard_map/ppermute | solution.py:85
  44.9 1.0 %collective-permute-start.16 = (bf16[256,256]{1,0:T(8,128)(2,1)S(1)}, bf16[256,256]{1,0:T(8,128)(2,1)S(1)}, u32[]{:S(2)}, u32[]{:S(2)}) collective-permute-start(bf16[256,256]{1,0:T(8,128)(2,1)S(1)} %get-tuple-element.47), channel_id=1, source_target_pairs={{0,8},{4,12},{8,0},{12,4},{1,9},{5,13},{9,1},{13,5},{2,10},{6,14},... | collective-permute-start | bytes 393224 | tf_op jit(solution)/shard_map/ppermute | solution.py:85
  45.9 0.7 %fusion = bf16[1,1,256,256]{3,2,1,0:T(8,128)(2,1)} fusion(f32[256,256]{1,0:T(8,128)S(1)} %get-tuple-element.34), kind=kLoop, calls=%fused_computation.3 | loop fusion | flops 327680 | bytes 393216 | tf_op jit(solution)/shard_map/broadcast_in_dim | solution.py:390
  46.7 3.3 %collective-permute-done.16.other_ref = bf16[256,256]{1,0:T(8,128)(2,1)S(1)} collective-permute-done((bf16[256,256]{1,0:T(8,128)(2,1)S(1)}, bf16[256,256]{1,0:T(8,128)(2,1)S(1)}, u32[]{:S(2)}, u32[]{:S(2)}) %collective-permute-start.16) | collective-permute-done | bytes 131104 | tf_op jit(solution)/shard_map/ppermute | solution.py:85
  50.0 0.8 %finish.1 = (bf16[256,256]{1,0:T(8,128)(2,1)}, f32[256,256]{1,0:T(8,128)}, f32[1,256]{1,0:T(1,128)}) custom-call(f32[256,256]{1,0:T(8,128)S(1)} %get-tuple-element.46.keep_ref, bf16[256,256]{1,0:T(8,128)(2,1)S(1)} %collective-permute-done.16.other_ref, f32[144,256]{1,0:T(8,128)S(1)} %add_add_fusion.half_ref, f32[144,256]{1,0:T(8,128)S(1)} %collective-permute-done.17.twin_ref), custom_call_target="tpu_custom_call" | custom-call | flops 65536 | bytes 393216 | tf_op jit(solution)/shard_map/finish/pallas_call | solution.py:335
  (32 shorter events, 2.2 us)
Async XLA Ops:
  0.6 8.7 %copy-start = (bf16[1,1,256,256]{3,2,1,0:T(8,128)(2,1)S(1)}, bf16[1,1,256,256]{3,2,1,0:T(8,128)(2,1)}, u32[]{:S(2)}) copy-start(bf16[1,1,256,256]{3,2,1,0:T(8,128)(2,1)} %param.8) | copy-start | bytes 393220
  0.6 7.3 %collective-permute-start = (bf16[256,256]{1,0:T(8,128)(2,1)}, bf16[256,256]{1,0:T(8,128)(2,1)S(1)}, u32[]{:S(2)}, u32[]{:S(2)}) collective-permute-start(bf16[256,256]{1,0:T(8,128)(2,1)} %bitcast.12), channel_id=1, source_target_pairs={{0,8},{4,12},{8,0},{12,4},{1,9},{5,13},{9,1},{13,5},{2,10},{6,14},... | collective-permute-start | bytes 393224 | tf_op jit(solution)/shard_map/ppermute | solution.py:85
  3.6 4.5 %collective-permute-start.1 = (bf16[256,256]{1,0:T(8,128)(2,1)}, bf16[256,256]{1,0:T(8,128)(2,1)S(1)}, u32[]{:S(2)}, u32[]{:S(2)}) collective-permute-start(bf16[256,256]{1,0:T(8,128)(2,1)} %bitcast.13), channel_id=1, source_target_pairs={{0,4},{4,0},{8,12},{12,8},{1,5},{5,1},{9,13},{13,9},{2,6},{6,2},{1... | collective-permute-start | bytes 393224 | tf_op jit(solution)/shard_map/ppermute | solution.py:85
  5.0 20.3 %copy-start.1 = (bf16[256,256]{1,0:T(8,128)(2,1)S(1)}, bf16[256,256]{1,0:T(8,128)(2,1)}, u32[]{:S(2)}) copy-start(bf16[256,256]{1,0:T(8,128)(2,1)} %weight_ref.1) | copy-start | bytes 393220
  5.0 20.3 %copy-start.2 = (bf16[1,1,256,256]{3,2,1,0:T(8,128)(2,1)S(1)}, bf16[1,1,256,256]{3,2,1,0:T(8,128)(2,1)}, u32[]{:S(2)}) copy-start(bf16[1,1,256,256]{3,2,1,0:T(8,128)(2,1)} %param.15) | copy-start | bytes 393220
  5.0 20.3 %copy-start.3 = (f32[256]{0:T(256)S(1)}, f32[256]{0:T(256)}, u32[]{:S(2)}) copy-start(f32[256]{0:T(256)} %param.10) | copy-start | bytes 3076
  7.9 1.4 %collective-permute-start.2 = (bf16[256,256]{1,0:T(8,128)(2,1)S(1)}, bf16[256,256]{1,0:T(8,128)(2,1)S(1)}, u32[]{:S(2)}, u32[]{:S(2)}) collective-permute-start(bf16[256,256]{1,0:T(8,128)(2,1)S(1)} %collective-permute-done.refs_2_), channel_id=1, source_target_pairs={{0,4},{4,0},{8,12},{12,8},{1,5},{5,1},{9,13},{13,9},{2,6},{6,2},{1... | collective-permute-start | bytes 393224 | tf_op jit(solution)/shard_map/ppermute | solution.py:85
  10.1 8.3 %collective-permute-start.3 = (bf16[256,256]{1,0:T(8,128)(2,1)S(1)}, bf16[256,256]{1,0:T(8,128)(2,1)S(1)}, u32[]{:S(2)}, u32[]{:S(2)}) collective-permute-start(bf16[256,256]{1,0:T(8,128)(2,1)S(1)} %get-tuple-element.31), channel_id=1, source_target_pairs={{0,3},{1,2},{2,1},{3,0},{4,7},{5,6},{6,5},{7,4},{8,11},{9,10},{10,... | collective-permute-start | bytes 393224 | tf_op jit(solution)/shard_map/ppermute | solution.py:85
  13.9 11.4 %collective-permute-start.4 = (bf16[256,256]{1,0:T(8,128)(2,1)S(1)}, bf16[256,256]{1,0:T(8,128)(2,1)S(1)}, u32[]{:S(2)}, u32[]{:S(2)}) collective-permute-start(bf16[256,256]{1,0:T(8,128)(2,1)S(1)} %get-tuple-element.32), channel_id=1, source_target_pairs={{0,2},{1,3},{2,0},{3,1},{4,6},{5,7},{6,4},{7,5},{8,10},{9,11},{10,... | collective-permute-start | bytes 393224 | tf_op jit(solution)/shard_map/ppermute | solution.py:85
  13.9 11.4 %collective-permute-start.5 = (bf16[256,256]{1,0:T(8,128)(2,1)S(1)}, bf16[256,256]{1,0:T(8,128)(2,1)S(1)}, u32[]{:S(2)}, u32[]{:S(2)}) collective-permute-start(bf16[256,256]{1,0:T(8,128)(2,1)S(1)} %get-tuple-element.33), channel_id=1, source_target_pairs={{0,1},{1,0},{2,3},{3,2},{4,5},{5,4},{6,7},{7,6},{8,9},{9,8},{10,11... | collective-permute-start | bytes 393224 | tf_op jit(solution)/shard_map/ppermute | solution.py:85
  25.6 7.5 %collective-permute-start.12 = (bf16[256,256]{1,0:T(8,128)(2,1)S(1)}, bf16[256,256]{1,0:T(8,128)(2,1)S(1)}, u32[]{:S(2)}, u32[]{:S(2)}) collective-permute-start(bf16[256,256]{1,0:T(8,128)(2,1)S(1)} %get-tuple-element.35.after_ref.refs_0_), channel_id=1, source_target_pairs={{0,1},{1,0},{2,3},{3,2},{4,5},{5,4},{6,7},{7,6},{8,9},{9,8},{10,11... | collective-permute-start | bytes 393224 | tf_op jit(solution)/shard_map/ppermute | solution.py:85
  25.8 8.7 %collective-permute-start.13 = (bf16[256,256]{1,0:T(8,128)(2,1)S(1)}, bf16[256,256]{1,0:T(8,128)(2,1)S(1)}, u32[]{:S(2)}, u32[]{:S(2)}) collective-permute-start(bf16[256,256]{1,0:T(8,128)(2,1)S(1)} %get-tuple-element.35.after_ref.refs_0_), channel_id=1, source_target_pairs={{0,2},{1,3},{2,0},{3,1},{4,6},{5,7},{6,4},{7,5},{8,10},{9,11},{10,... | collective-permute-start | bytes 393224 | tf_op jit(solution)/shard_map/ppermute | solution.py:85
  28.9 5.9 %collective-permute-start.8 = (bf16[144,256]{1,0:T(8,128)(2,1)S(1)}, bf16[144,256]{1,0:T(8,128)(2,1)S(1)}, u32[]{:S(2)}, u32[]{:S(2)}) collective-permute-start(bf16[144,256]{1,0:T(8,128)(2,1)S(1)} %get-tuple-element.39), channel_id=1, source_target_pairs={{0,12},{4,8},{8,4},{12,0},{1,13},{5,9},{9,5},{13,1},{2,14},{6,10},... | collective-permute-start | bytes 221192 | tf_op jit(solution)/shard_map/ppermute | solution.py:85
  29.0 5.8 %collective-permute-start.7 = (bf16[144,256]{1,0:T(8,128)(2,1)S(1)}, bf16[144,256]{1,0:T(8,128)(2,1)S(1)}, u32[]{:S(2)}, u32[]{:S(2)}) collective-permute-start(bf16[144,256]{1,0:T(8,128)(2,1)S(1)} %get-tuple-element.38), channel_id=1, source_target_pairs={{0,8},{4,12},{8,0},{12,4},{1,9},{5,13},{9,1},{13,5},{2,10},{6,14},... | collective-permute-start | bytes 221192 | tf_op jit(solution)/shard_map/ppermute | solution.py:85
  30.1 4.6 %collective-permute-start.6 = (bf16[144,256]{1,0:T(8,128)(2,1)S(1)}, bf16[144,256]{1,0:T(8,128)(2,1)S(1)}, u32[]{:S(2)}, u32[]{:S(2)}) collective-permute-start(bf16[144,256]{1,0:T(8,128)(2,1)S(1)} %get-tuple-element.39), channel_id=1, source_target_pairs={{0,4},{4,0},{8,12},{12,8},{1,5},{5,1},{9,13},{13,9},{2,6},{6,2},{1... | collective-permute-start | bytes 221192 | tf_op jit(solution)/shard_map/ppermute | solution.py:85
  34.5 6.3 %collective-permute-start.14 = (bf16[256,256]{1,0:T(8,128)(2,1)S(1)}, bf16[256,256]{1,0:T(8,128)(2,1)S(1)}, u32[]{:S(2)}, u32[]{:S(2)}) collective-permute-start(bf16[256,256]{1,0:T(8,128)(2,1)S(1)} %collective-permute-done.13.refs_2_), channel_id=1, source_target_pairs={{0,1},{1,0},{2,3},{3,2},{4,5},{5,4},{6,7},{7,6},{8,9},{9,8},{10,11... | collective-permute-start | bytes 393224 | tf_op jit(solution)/shard_map/ppermute | solution.py:85
  34.8 7.5 %collective-permute-start.11 = (bf16[144,256]{1,0:T(8,128)(2,1)S(1)}, bf16[144,256]{1,0:T(8,128)(2,1)S(1)}, u32[]{:S(2)}, u32[]{:S(2)}) collective-permute-start(bf16[144,256]{1,0:T(8,128)(2,1)S(1)} %add_convert_fusion), channel_id=1, source_target_pairs={{0,3},{1,2},{2,1},{3,0},{4,7},{5,6},{6,5},{7,4},{8,11},{9,10},{10,... | collective-permute-start | bytes 221192 | tf_op jit(solution)/shard_map/ppermute | solution.py:85
  37.1 7.7 %collective-permute-start.10 = (bf16[144,256]{1,0:T(8,128)(2,1)S(1)}, bf16[144,256]{1,0:T(8,128)(2,1)S(1)}, u32[]{:S(2)}, u32[]{:S(2)}) collective-permute-start(bf16[144,256]{1,0:T(8,128)(2,1)S(1)} %add_convert_fusion), channel_id=1, source_target_pairs={{0,2},{1,3},{2,0},{3,1},{4,6},{5,7},{6,4},{7,5},{8,10},{9,11},{10,... | collective-permute-start | bytes 221192 | tf_op jit(solution)/shard_map/ppermute | solution.py:85
  38.1 6.7 %collective-permute-start.9 = (bf16[144,256]{1,0:T(8,128)(2,1)S(1)}, bf16[144,256]{1,0:T(8,128)(2,1)S(1)}, u32[]{:S(2)}, u32[]{:S(2)}) collective-permute-start(bf16[144,256]{1,0:T(8,128)(2,1)S(1)} %add_convert_fusion), channel_id=1, source_target_pairs={{0,1},{1,0},{2,3},{3,2},{4,5},{5,4},{6,7},{7,6},{8,9},{9,8},{10,11... | collective-permute-start | bytes 221192 | tf_op jit(solution)/shard_map/ppermute | solution.py:85
  41.6 3.3 %collective-permute-start.15 = (bf16[2,256,256]{2,1,0:T(8,128)(2,1)S(1)}, bf16[2,256,256]{2,1,0:T(8,128)(2,1)S(1)}, u32[]{:S(2)}, u32[]{:S(2)}) collective-permute-start(bf16[2,256,256]{2,1,0:T(8,128)(2,1)S(1)} %get-tuple-element.44), channel_id=1, source_target_pairs={{0,4},{4,0},{8,12},{12,8},{1,5},{5,1},{9,13},{13,9},{2,6},{6,2},{1... | collective-permute-start | bytes 786440 | tf_op jit(solution)/shard_map/ppermute | solution.py:85
  44.9 5.0 %collective-permute-start.16 = (bf16[256,256]{1,0:T(8,128)(2,1)S(1)}, bf16[256,256]{1,0:T(8,128)(2,1)S(1)}, u32[]{:S(2)}, u32[]{:S(2)}) collective-permute-start(bf16[256,256]{1,0:T(8,128)(2,1)S(1)} %get-tuple-element.47), channel_id=1, source_target_pairs={{0,8},{4,12},{8,0},{12,4},{1,9},{5,13},{9,1},{13,5},{2,10},{6,14},... | collective-permute-start | bytes 393224 | tf_op jit(solution)/shard_map/ppermute | solution.py:85
  45.9 4.0 %collective-permute-start.17 = (f32[144,256]{1,0:T(8,128)S(1)}, f32[144,256]{1,0:T(8,128)S(1)}, u32[]{:S(2)}, u32[]{:S(2)}) collective-permute-start(f32[144,256]{1,0:T(8,128)S(1)} %add_add_fusion.half_ref), channel_id=1, source_target_pairs={{0,4},{4,0},{8,12},{12,8},{1,5},{5,1},{9,13},{13,9},{2,6},{6,2},{1... | collective-permute-start | bytes 442376 | tf_op jit(solution)/shard_map/ppermute | solution.py:85
